TPU v7x, 512 devices: a whole 4x4x16 slice. The times are simulated.
512 devices in a mesh: ctx: 64 (over z, y), head: 8 (over x, core).
Axes of the slice: x: 4, y: 4, z: 16, core: 2. Of those that a mesh axis runs over, the one named last changes fastest.
Arguments:
- normalized_layer_input: bfloat16 [8192, 5120], P('ctx', 'head'), may hold values from -6 to 6
- queries: bfloat16 [8192, 8192], P('ctx', 'head'), may hold values from -40 to 40
- projected_keys: bfloat16 [8192, 1024], P('ctx', 'head'), may hold values from -9 to 9
- projected_values: bfloat16 [8192, 1024], P('ctx', 'head'), may hold values from -6 to 6
- frozen_path_gradient: bfloat16 [8192, 8192], P('ctx', 'head'), may hold values from -6 to 6
- output_gradient: bfloat16 [8192, 5120], P('ctx', 'head'), may hold values from -6 to 6
- document_length_list: int32 [128], replicated, may hold values from 1 to 1921, as said below
- query_down_adapter: bfloat16 [5120, 16], P('head'), may hold values from -0.078125 to 0.078125
- query_up_adapter: bfloat16 [16, 8192], P(None, 'head'), may hold values from -1.5 to 1.5
- key_down_adapter: bfloat16 [5120, 16], P('head'), may hold values from -0.078125 to 0.078125
- key_up_adapter: bfloat16 [16, 1024], P(None, 'head'), may hold values from -1.5 to 1.5
- value_down_adapter: bfloat16 [5120, 16], P('head'), may hold values from -0.078125 to 0.078125
- value_up_adapter: bfloat16 [16, 1024], P(None, 'head'), may hold values from -1.5 to 1.5
- output_down_adapter: bfloat16 [8192, 16], P('head'), may hold values from -0.0625 to 0.0625
- output_up_adapter: bfloat16 [16, 5120], P(None, 'head'), may hold values from -1.5 to 1.5
Outputs:
- query_gradient: bfloat16 [8192, 8192], P('ctx', 'head')
- key_gradient: bfloat16 [8192, 1024], P('ctx', 'head')
- value_gradient: bfloat16 [8192, 1024], P('ctx', 'head')
- query_down_gradient: float32 [5120, 16], P('head')
- query_up_gradient: float32 [16, 8192], P(None, 'head')
- key_down_gradient: float32 [5120, 16], P('head')
- key_up_gradient: float32 [16, 1024], P(None, 'head')
- value_down_gradient: float32 [5120, 16], P('head')
- value_up_gradient: float32 [16, 1024], P(None, 'head')
- output_down_gradient: float32 [8192, 16], P('head')
- output_up_gradient: float32 [16, 5120], P(None, 'head')
Inputs may be any that keep to these rules, and one draw needn't show every extreme that they name: `document_length_list`: they sum to 8192; exactly two of them, at places in the list that vary from draw to draw, have 1921 tokens.
All inputs are finite; a program needn't handle non-finite values.
Results may differ from a plain program's by a relative error of at most 0.015.
Values may be sent and summed in bfloat16 or wider, within the bound.
No kernel may reach another device: no remote copies, remote signals or barrier semaphores. Data moves between devices by JAX's collectives and lax.ppermute only.
A program may use at most 64 MiB of HBM per device.

v0:
```python
import jax
import jax.numpy as jnp
from jax import lax
from jax.sharding import PartitionSpec as P

HEAD_SIZE = 128


ADAPTER_SCALE = 2.0
NEG = -1e30


def passed_along(value, axis, steps):
    count = lax.axis_size(axis)
    initial, last = (max(0, -steps), min(count, count - steps))
    return lax.ppermute(value, axis, [(source, source + steps) for source in range(initial, last)])


def doc_index(positions, doc_ends):
    found = jnp.sum((positions[:, None] >= doc_ends[None, :]).astype(jnp.int32), axis=1)
    return jnp.where(positions >= 0, found, -1)


def contract_trailing(left, right):
    return lax.dot_general(
        left, right, (((1,), (1,)), ((), ())), preferred_element_type=jnp.float32
    )


def contract_leading(left, right):
    return lax.dot_general(
        left, right, (((0,), (0,)), ((), ())), preferred_element_type=jnp.float32
    )


def shards(
    normalized_layer_input,
    queries,
    projected_keys,
    projected_values,
    frozen_path_gradient,
    output_gradient,
    document_length_list,
    query_down_adapter,
    query_up_adapter,
    key_down_adapter,
    key_up_adapter,
    value_down_adapter,
    value_up_adapter,
    output_down_adapter,
    output_up_adapter,
):
    row_count = queries.shape[0]
    width_kv = projected_keys.shape[1]
    kv_local = width_kv // HEAD_SIZE
    group_size = queries.shape[1] // width_kv
    chain_span = min(16, lax.axis_size("ctx") // 2)
    score_scale = HEAD_SIZE ** (-0.5)
    device = lax.axis_index("ctx")
    doc_ends = jnp.cumsum(document_length_list, dtype=jnp.int32)
    offsets = jnp.arange(row_count, dtype=jnp.int32)
    q_pos = device * row_count + offsets
    q_doc = doc_index(q_pos, doc_ends)
    query_down_product = jnp.dot(
        normalized_layer_input, query_down_adapter, preferred_element_type=jnp.float32
    )
    key_down_product = jnp.dot(
        normalized_layer_input, key_down_adapter, preferred_element_type=jnp.float32
    )
    value_down_product = jnp.dot(
        normalized_layer_input, value_down_adapter, preferred_element_type=jnp.float32
    )
    down_product_portion = contract_trailing(output_gradient, output_up_adapter)
    summed_in = lax.psum(
        (query_down_product, key_down_product, value_down_product, down_product_portion), "head"
    )
    query_down_product, key_down_product, value_down_product, output_down_product = [
        summed_term.astype(jnp.bfloat16) for summed_term in summed_in
    ]
    flattened_gradient = (
        frozen_path_gradient.astype(jnp.float32)
        + ADAPTER_SCALE * contract_trailing(output_down_product, output_down_adapter)
    ).astype(jnp.bfloat16)
    key_pair = jnp.stack([projected_keys, projected_values])

    def step_keys(hop_index, loop_state):
        moving, key_stack = loop_state
        moving = passed_along(moving, "ctx", 1)
        return (moving, lax.dynamic_update_index_in_dim(key_stack, moving, hop_index, 0))

    start_stack = jnp.zeros((chain_span,) + key_pair.shape, key_pair.dtype).at[0].set(key_pair)
    _, key_stack = lax.fori_loop(1, chain_span, step_keys, (key_pair, start_stack))
    q_heads = queries.reshape(row_count, kv_local, group_size, HEAD_SIZE)
    per_head_gradient = flattened_gradient.reshape(row_count, kv_local, group_size, HEAD_SIZE)

    def hop_mask(hop_index):
        k_pos = (device - hop_index) * row_count + offsets
        k_doc = doc_index(k_pos, doc_ends)
        return (k_doc[None, :] == q_doc[:, None]) & (k_pos[None, :] <= q_pos[:, None])

    def hop_scores(hop_index):
        key_block = key_stack[hop_index, 0].reshape(row_count, kv_local, HEAD_SIZE)
        value_block = key_stack[hop_index, 1].reshape(row_count, kv_local, HEAD_SIZE)
        raw_scores = (
            jnp.einsum("qhgd,khd->hgqk", q_heads, key_block, preferred_element_type=jnp.float32)
            * score_scale
        )
        return (key_block, value_block, raw_scores)

    def stats_live(hop_index, loop_state):
        row_top, row_total, weighted = loop_state
        allowed = hop_mask(hop_index)
        key_block, value_block, raw_scores = hop_scores(hop_index)
        masked = jnp.where(allowed, raw_scores, NEG)
        new_top = jnp.maximum(row_top, jnp.max(masked, axis=-1))
        shrink = jnp.exp(row_top - new_top)
        weights = jnp.where(allowed, jnp.exp(masked - new_top[..., None]), 0.0)
        row_total = row_total * shrink + jnp.sum(weights, axis=-1)
        weighted = weighted * shrink[..., None] + jnp.einsum(
            "hgqk,khd->hgqd",
            weights,
            value_block.astype(jnp.float32),
            precision=lax.Precision.HIGHEST,
        )
        return (new_top, row_total, weighted)

    def stats_step(hop_index, loop_state):
        return stats_live(hop_index, loop_state)

    stat_shape = (kv_local, group_size, row_count)
    start_state = (
        jnp.full(stat_shape, NEG, jnp.float32),
        jnp.zeros(stat_shape, jnp.float32),
        jnp.zeros(stat_shape + (HEAD_SIZE,), jnp.float32),
    )
    row_top, row_total, weighted = lax.fori_loop(0, chain_span, stats_step, start_state)
    log_norm = row_top + jnp.log(row_total)
    attn_heads = (weighted / row_total[..., None]).transpose(2, 0, 1, 3).astype(jnp.bfloat16)
    attention_output = attn_heads.reshape(row_count, queries.shape[1])
    row_delta = jnp.einsum(
        "qhgd,qhgd->hgq", per_head_gradient.astype(jnp.float32), attn_heads.astype(jnp.float32)
    )

    def grads_live(hop_index):
        allowed = hop_mask(hop_index)
        key_block, value_block, raw_scores = hop_scores(hop_index)
        attn_prob = jnp.where(
            allowed, jnp.exp(jnp.where(allowed, raw_scores, NEG) - log_norm[..., None]), 0.0
        )
        grad_prob = jnp.einsum(
            "qhgd,khd->hgqk", per_head_gradient, value_block, preferred_element_type=jnp.float32
        )
        grad_score = (attn_prob * (grad_prob - row_delta[..., None])).astype(jnp.bfloat16)
        grad_q = (
            jnp.einsum("hgqk,khd->qhgd", grad_score, key_block, preferred_element_type=jnp.float32)
            * score_scale
        )
        grad_k = (
            jnp.einsum("hgqk,qhgd->khd", grad_score, q_heads, preferred_element_type=jnp.float32)
            * score_scale
        )
        grad_v = jnp.einsum(
            "hgqk,qhgd->khd",
            attn_prob.astype(jnp.bfloat16),
            per_head_gradient,
            preferred_element_type=jnp.float32,
        )
        panel = jnp.concatenate(
            [grad_k.reshape(row_count, width_kv), grad_v.reshape(row_count, width_kv)], axis=1
        )
        return (grad_q, panel)

    def grads_step(hop_index, loop_state):
        query_sum, contribs = loop_state
        grad_q, panel = grads_live(hop_index)
        return (query_sum + grad_q, lax.dynamic_update_index_in_dim(contribs, panel, hop_index, 0))

    start_grads = (
        jnp.zeros(q_heads.shape, jnp.float32),
        jnp.zeros((chain_span, row_count, 2 * width_kv), jnp.float32),
    )
    query_sum, contribs = lax.fori_loop(0, chain_span, grads_step, start_grads)

    def step_panels(step_count, panel):
        arrived = passed_along(panel, "ctx", -1)
        return arrived + contribs[chain_span - 2 - step_count]

    owned = lax.fori_loop(0, chain_span - 1, step_panels, contribs[chain_span - 1])
    query_gradient = query_sum.reshape(row_count, queries.shape[1]).astype(jnp.bfloat16)
    key_gradient = owned[:, :width_kv].astype(jnp.bfloat16)
    value_gradient = owned[:, width_kv:].astype(jnp.bfloat16)
    output_portion = jnp.dot(
        attention_output, output_down_adapter, preferred_element_type=jnp.float32
    )
    query_backward = contract_trailing(query_gradient, query_up_adapter)
    key_backward = contract_trailing(key_gradient, key_up_adapter)
    value_backward = contract_trailing(value_gradient, value_up_adapter)
    summed_back = lax.psum((output_portion, query_backward, key_backward, value_backward), "head")
    output_adapter_term, query_backward, key_backward, value_backward = [
        summed_term.astype(jnp.bfloat16) for summed_term in summed_back
    ]
    totals = lax.psum(
        (
            ADAPTER_SCALE * contract_leading(normalized_layer_input, query_backward),
            ADAPTER_SCALE * contract_leading(query_down_product, query_gradient),
            ADAPTER_SCALE * contract_leading(normalized_layer_input, key_backward),
            ADAPTER_SCALE * contract_leading(key_down_product, key_gradient),
            ADAPTER_SCALE * contract_leading(normalized_layer_input, value_backward),
            ADAPTER_SCALE * contract_leading(value_down_product, value_gradient),
            ADAPTER_SCALE * contract_leading(attention_output, output_down_product),
            ADAPTER_SCALE * contract_leading(output_adapter_term, output_gradient),
        ),
        "ctx",
    )
    return (
        query_gradient,
        key_gradient,
        value_gradient,
        totals[0],
        totals[1],
        totals[2],
        totals[3],
        totals[4],
        totals[5],
        totals[6],
        totals[7],
    )


def solution(mesh):
    placed = (
        P("ctx", "head"),
        P("ctx", "head"),
        P("ctx", "head"),
        P("ctx", "head"),
        P("ctx", "head"),
        P("ctx", "head"),
        P(),
        P("head", None),
        P(None, "head"),
        P("head", None),
        P(None, "head"),
        P("head", None),
        P(None, "head"),
        P("head", None),
        P(None, "head"),
    )
    return jax.shard_map(
        shards,
        mesh=mesh,
        in_specs=placed,
        out_specs=(
            P("ctx", "head"),
            P("ctx", "head"),
            P("ctx", "head"),
            P("head", None),
            P(None, "head"),
            P("head", None),
            P(None, "head"),
            P("head", None),
            P(None, "head"),
            P("head", None),
            P(None, "head"),
        ),
        check_vma=False,
    )
```

profile of v0, /device:TPU:2, one launch (start us, length us, event | category | flops | bytes accessed | tf_op | source)
XLA Modules:
  0.0 953.4 jit_solution(5362543609055109577)
XLA Ops:
  8.3 15.1 %psum.112 = bf16[128,16]{0,1:T(8,128)(2,1)S(1)} all-reduce(f32[128,16]{0,1:T(8,128)S(1)} %fusion.72), channel_id=1, replica_groups=mesh['ctx'=64,'head'=8] {'head'}, use_global_device_ids=true, to_apply=%region_9.10 | all-reduce | flops 2048 | bytes 12288 | tf_op jit(solution)/shard_map/psum | solution.py:74
  27.9 110.3 %while.65 = (s32[]{:T(128)}, bf16[2,128,128]{2,1,0:T(8,128)(2,1)S(1)}, bf16[16,2,128,128]{3,2,1,0:T(8,128)(2,1)S(1)}, s32[]{:T(128)}, s32[]{:T(128)}, /*index=5*/s32[]{:T(128)}) while((s32[]{:T(128)}, bf16[2,128,128]{2,1,0:T(8,128)(2,1)S(1)}, bf16[16,2,128,128]{3,2,1,0:T(8,128)(2,1)S(1)}, s32[]{:T(128)}, s32[]{:T(128)}, ...), condition=%wide.region_3.4_spmd, body=%wide.region_2.3_spmd.sunk | while | flops 5 | bytes 524435 | solution.py:92
  27.9 1.3 collective-permute-start
  29.2 1.9 collective-permute-done
  31.1 4.3 collective-permute-start
  35.4 1.9 collective-permute-done
  37.3 4.3 collective-permute-start
  41.6 1.9 collective-permute-done
  43.5 4.3 collective-permute-start
  47.8 1.9 collective-permute-done
  49.7 4.3 collective-permute-start
  54.0 2.0 collective-permute-done
  56.1 5.0 collective-permute-start
  61.1 1.9 collective-permute-done
  63.0 6.5 collective-permute-start
  69.6 1.9 collective-permute-done
  71.5 6.2 collective-permute-start
  77.7 1.9 collective-permute-done
  79.6 6.5 collective-permute-start
  86.2 1.9 collective-permute-done
  88.1 6.4 collective-permute-start
  94.5 1.9 collective-permute-done
  96.4 6.4 collective-permute-start
  102.8 1.9 collective-permute-done
  104.7 6.4 collective-permute-start
  111.1 2.4 collective-permute-done
  113.5 6.2 collective-permute-start
  119.7 1.9 collective-permute-done
  121.6 6.3 collective-permute-start
  128.0 1.9 collective-permute-done
  129.9 6.4 collective-permute-start
  136.3 1.9 collective-permute-done
  138.2 23.4 %while.67 = (s32[]{:T(128)}, f32[1,8,128]{2,1,0:T(8,128)S(1)}, f32[1,8,128]{2,1,0:T(8,128)S(1)}, f32[1,8,128,128]{3,2,1,0:T(8,128)S(1)}, s32[]{:T(128)}, /*index...) while((s32[]{:T(128)}, f32[1,8,128]{2,1,0:T(8,128)S(1)}, ...), condition=%wide.region_8.9_spmd.clone, body=%wide.region_4.0_spmd.clone.sunk | while | flops 236427776 | bytes 3086013 | solution.py:136
  164.5 36.6 %while.68 = (s32[]{:T(128)}, f32[128,1,8,128]{0,3,2,1:T(8,128)S(1)}, f32[16,128,256]{1,2,0:T(8,128)}, bf16[16,2,128,128]{3,2,1,0:T(8,128)(2,1)S(1)}, s32[]{:T(12...) while((s32[]{:T(128)}, ...), condition=%wide.region_12.13_spmd.clone, body=%wide.region_10.12_spmd.clone.sunk | while | flops 169361920 | bytes 4994771 | solution.py:182
  202.3 138.7 %while.66 = (s32[]{:T(128)}, f32[128,256]{1,0:T(8,128)S(1)}, f32[16,128,256]{1,2,0:T(8,128)}, s32[]{:T(128)}, s32[]{:T(128)}, /*index=5*/s32[]{:T(128)}, s32[]{:T(128)}) while((s32[]{:T(128)}, f32[128,256]{1,0:T(8,128)S(1)}, f32[16,128,256]{1,2,0:T(8,128)}, s32[]{:T(128)}, s32[]{:T(128)}, /*index=5*/s32[]{:T(128)}, s32[]{:T(128)}) %tuple.154), condition=%wide.region_14.15_spmd, body=%wide.region_13.14_spmd.sunk | while | flops 32774 | bytes 1441967 | solution.py:188
  202.3 1.4 collective-permute-start.1
  204.7 7.0 collective-permute-done.1
  214.1 7.0 collective-permute-done.1
  221.1 1.3 collective-permute-start.1
  223.4 7.0 collective-permute-done.1
  232.8 7.0 collective-permute-done.1
  239.8 1.3 collective-permute-start.1
  242.2 7.8 collective-permute-done.1
  252.4 8.0 collective-permute-done.1
  262.8 6.6 collective-permute-done.1
  271.8 6.1 collective-permute-done.1
  280.2 6.4 collective-permute-done.1
  289.0 6.6 collective-permute-done.1
  298.0 6.6 collective-permute-done.1
  307.0 6.6 collective-permute-done.1
  316.0 6.7 collective-permute-done.1
  325.0 7.0 collective-permute-done.1
  334.3 6.6 collective-permute-done.1
  341.5 24.9 %all-reduce.3 = (bf16[128,16]{0,1:T(8,128)(2,1)S(1)}, bf16[128,16]{0,1:T(8,128)(2,1)S(1)}, bf16[128,16]{0,1:T(8,128)(2,1)S(1)}, bf16[128,16]{0,1:T(8,128)(2,1)S(...) all-reduce(f32[128,16]{0,1:T(8,128)S(1)} %fusion.79, ...), channel_id=1, replica_groups=mesh['ctx'=64,'head'=8] {'head'}, use_global_device_ids=true, to_apply=%region_15.16 | all-reduce | flops 14336 | bytes 86016 | tf_op jit(solution)/shard_map/psum | solution.py:198
  372.7 300.6 %all-reduce.9.cloned.1.call-done = (f32[16,1024]{1,0:T(8,128)}, f32[1024,16]{0,1:T(8,128)}) async-done(((f32[16,1024]{1,0:T(8,128)}, f32[1024,16]{0,1:T(8,128)}), (f32[16,1024]{1,0:T(8,128)}, f32[1024,16]{0,1:T(8,128)})) %all-reduce.9.cloned.1.call-update) | async-done | bytes 131088 | tf_op jit(solution)/shard_map/psum | solution.py:202
  673.3 262.1 %all-reduce.7.cloned.1.call-done = (f32[640,16]{0,1:T(8,128)}, f32[640,16]{0,1:T(8,128)}, f32[16,128]{1,0:T(8,128)}, f32[640,16]{0,1:T(8,128)}, f32[16,128]{1,0:T(8,128)}, /*index=5*/f32[16,640]{1,0:T(8,128)}) async-done(((f32[640,16]{0,1:T(8,128)}, f32[640,16]{0,1:T(8,128)}, f32[16,128]{1,0:T(8,128)}, f32[640,16]{0,1:T(8,128)}, f32[16,128]{1,0:T(8,128)}, /*index=5*/f32[16,640]{1,0:T(8,128)}), ...) | async-done | bytes 180240 | tf_op jit(solution)/shard_map/psum | solution.py:202
  935.4 1.4 copy.136
  936.8 1.5 copy.137
  938.3 1.4 copy.138
  939.7 1.3 copy.139
  941.0 1.4 copy.140
  942.4 1.3 copy.141
  943.7 1.5 copy.142
  945.2 1.4 copy.143
  (484 shorter events, 105.0 us)
Async XLA Ops:
  7.2 156.8 %copy-start = (bf16[128,640]{1,0:T(8,128)(2,1)S(1)}, bf16[128,640]{1,0:T(8,128)(2,1)}, u32[]{:S(2)}) copy-start(bf16[128,640]{1,0:T(8,128)(2,1)} %param.25) | copy-start | bytes 491524
  7.2 20.1 %copy-start.4 = (bf16[128,1024]{1,0:T(8,128)(2,1)S(1)}, bf16[128,1024]{1,0:T(8,128)(2,1)}, u32[]{:S(2)}) copy-start(bf16[128,1024]{1,0:T(8,128)(2,1)} %param.26) | copy-start | bytes 786436
  7.2 666.1 %all-reduce.9.cloned.1.call-start = ((), (), s32[]{:S(2)}) async-start(), calls=%async_computation.1 | async-start | bytes 262144 | tf_op jit(solution)/shard_map/psum | solution.py:202
  25.9 1.7 copy-start.7
  25.9 1.7 copy-start.8
  27.9 3.2 collective-permute-start
  31.1 6.2 collective-permute-start
  37.3 6.2 collective-permute-start
  43.5 6.2 collective-permute-start
  49.7 6.3 collective-permute-start
  56.1 6.9 collective-permute-start
  63.0 8.4 collective-permute-start
  71.5 8.1 collective-permute-start
  79.6 8.4 collective-permute-start
  88.1 8.3 collective-permute-start
  96.4 8.3 collective-permute-start
  104.7 8.8 collective-permute-start
  113.5 8.1 collective-permute-start
  121.6 8.2 collective-permute-start
  129.9 8.3 collective-permute-start
  161.6 1.4 copy-start.5
  161.6 2.4 copy-start.9
  161.7 2.5 copy-start.10
  161.7 2.7 copy-start.11
  202.2 138.8 %copy-start.6 = (bf16[16,1024]{1,0:T(8,128)(2,1)S(1)}, bf16[16,1024]{1,0:T(8,128)(2,1)}, u32[]{:S(2)}) copy-start(bf16[16,1024]{1,0:T(8,128)(2,1)} %param.33) | copy-start | bytes 98308
  202.2 139.0 %copy-start.12 = (bf16[16,128]{1,0:T(8,128)(2,1)S(1)}, bf16[16,128]{1,0:T(8,128)(2,1)}, u32[]{:S(2)}) copy-start(bf16[16,128]{1,0:T(8,128)(2,1)} %param.37) | copy-start | bytes 12292
  202.2 139.1 %copy-start.13 = (bf16[16,128]{1,0:T(8,128)(2,1)S(1)}, bf16[16,128]{1,0:T(8,128)(2,1)}, u32[]{:S(2)}) copy-start(bf16[16,128]{1,0:T(8,128)(2,1)} %param.35) | copy-start | bytes 12292
  202.3 168.1 %copy-start.1 = (bf16[128,640]{1,0:T(8,128)(2,1)S(1)}, bf16[128,640]{1,0:T(8,128)(2,1)}, u32[]{:S(2)}) copy-start(bf16[128,640]{1,0:T(8,128)(2,1)} %param.30) | copy-start | bytes 491524
  202.3 9.5 collective-permute-start.1
  211.8 9.3 collective-permute-start.1
  221.1 9.3 collective-permute-start.1
  230.5 9.3 collective-permute-start.1
  239.8 10.2 %collective-permute-start.1 = (f32[128,256]{1,0:T(8,128)S(1)}, f32[128,256]{1,0:T(8,128)S(1)}, u32[]{:S(2)}, u32[]{:S(2)}) collective-permute-start(f32[128,256]{1,0:T(8,128)S(1)} %get-tuple-element.1123), channel_id=1, source_target_pairs={{8,0},{16,8},{24,16},{32,24},{40,32},{48,40},{56,48},{64,56},{72,6... | collective-permute-start | bytes 393224 | tf_op jit(solution)/shard_map/while/body/eval_jaxpr/ppermute | solution.py:16
  250.0 10.3 %collective-permute-start.1 = (f32[128,256]{1,0:T(8,128)S(1)}, f32[128,256]{1,0:T(8,128)S(1)}, u32[]{:S(2)}, u32[]{:S(2)}) collective-permute-start(f32[128,256]{1,0:T(8,128)S(1)} %get-tuple-element.1123), channel_id=1, source_target_pairs={{8,0},{16,8},{24,16},{32,24},{40,32},{48,40},{56,48},{64,56},{72,6... | collective-permute-start | bytes 393224 | tf_op jit(solution)/shard_map/while/body/eval_jaxpr/ppermute | solution.py:16
  260.4 9.0 collective-permute-start.1
  269.4 8.4 collective-permute-start.1
  277.9 8.7 collective-permute-start.1
  286.6 9.0 collective-permute-start.1
  295.6 9.0 collective-permute-start.1
  304.6 9.0 collective-permute-start.1
  313.6 9.0 collective-permute-start.1
  322.7 9.3 collective-permute-start.1
  332.0 9.0 collective-permute-start.1
  341.0 605.5 %copy-start.2 = (bf16[128,128]{1,0:T(8,128)(2,1)}, bf16[128,128]{1,0:T(8,128)(2,1)S(1)}, u32[]{:S(2)}) copy-start(bf16[128,128]{1,0:T(8,128)(2,1)S(1)} %get-tuple-element.1138) | copy-start | bytes 98308
  341.0 605.5 %copy-start.3 = (bf16[128,128]{1,0:T(8,128)(2,1)}, bf16[128,128]{1,0:T(8,128)(2,1)S(1)}, u32[]{:S(2)}) copy-start(bf16[128,128]{1,0:T(8,128)(2,1)S(1)} %get-tuple-element.1137) | copy-start | bytes 98308
  367.3 568.2 %all-reduce.7.cloned.1.call-start = ((), (), s32[]{:S(2)}) async-start(), calls=%async_computation | async-start | bytes 360448 | tf_op jit(solution)/shard_map/psum | solution.py:202
Sparse Core Ops, SparseCore 0:
  367.4 305.8 all-reduce.8
  678.6 256.7 all-reduce.6
where the time goes:
time: 955 us; the launch traced here: 953 us
  waiting for transfers between devices  695 us (73%)
  starting transfers between devices  100 us (10%)
  matrix products  45.2 us (5%)
  blocking collectives  40.1 us (4%)
  local copies, waits for them, and re-layouts  31.4 us (3%)
  other arithmetic  23.9 us (3%)
  between operations  14.4 us (2%)
    psum x2, waiting for transfers between devices, shards(): lax.psum((ADAPTER_SCALE * contract_leading(normalized_layer_input, query_...  563 us
    ppermute x30, waiting for transfers between devices, passed_along(): lax.ppermute(value, axis, [(source, source + steps) for source in range(i...  132 us
    ppermute x30, starting transfers between devices, passed_along(): lax.ppermute(value, axis, [(source, source + steps) for source in range(i...  100 us
    psum x1, blocking collectives, shards(): lax.psum((output_portion, query_backward, key_backward, value_backward),...  24.9 us
  transfers between devices with their start and end apart: 32, of which 32 were waited for; matrix products, arithmetic and copies ran while one was open for 2% of the time, Pallas kernels for 0%

commit v1 on v0

v1 whole, which is shorter than its diff:
```python
import functools

import jax
import jax.numpy as jnp
from jax import lax
from jax.experimental import pallas as pl
from jax.experimental.pallas import tpu as pltpu
from jax.sharding import PartitionSpec as P

HEAD = 128
ROWS = 128
GROUP = 8
RANK = 16
TILES = 40
SCALE = HEAD**-0.5
LOG2E = 1.4426950408889634
ADAPTER_SCALE = 2.0
NEG = -1e30
F32 = jnp.float32
BF16 = jnp.bfloat16

Y_GROUPS = [[4 * z + y for y in range(4)] for z in range(16)]
Z_FOURS = [[16 * zh + 4 * k + y for k in range(4)] for zh in range(4) for y in range(4)]
EIGHTS = [[8 * g + i for i in range(8)] for g in range(8)]
STRIDED = [[g + 8 * i for i in range(8)] for g in range(8)]


def nn(a, b):
    return lax.dot_general(a, b, (((1,), (0,)), ((), ())), preferred_element_type=F32)


def nt(a, b):
    return lax.dot_general(a, b, (((1,), (1,)), ((), ())), preferred_element_type=F32)


def tn(a, b):
    return lax.dot_general(a, b, (((0,), (0,)), ((), ())), preferred_element_type=F32)


def call(body, outs, *args, scratch=(), vmem=32, flops=1 << 20):
    return pl.pallas_call(
        body,
        out_shape=outs,
        in_specs=[pl.BlockSpec(memory_space=pltpu.VMEM)] * len(args),
        out_specs=jax.tree.map(lambda _: pl.BlockSpec(memory_space=pltpu.VMEM), outs),
        scratch_shapes=list(scratch),
        compiler_params=pltpu.CompilerParams(vmem_limit_bytes=vmem << 20),
        cost_estimate=pl.CostEstimate(flops=flops, bytes_accessed=1 << 20, transcendentals=0),
    )(*args)


def shaped(shape, dtype):
    return jax.ShapeDtypeStruct(shape, dtype)


def project_kernel(x_ref, dout_ref, qd_ref, kd_ref, vd_ref, ou_ref, out_ref, wide):
    wide[:, 0:16] = nn(x_ref[...], qd_ref[...])
    wide[:, 16:32] = nn(x_ref[...], kd_ref[...])
    wide[:, 32:48] = nn(x_ref[...], vd_ref[...])
    wide[:, 48:64] = nt(dout_ref[...], ou_ref[...])
    low = wide[...].T.astype(BF16)
    for peer in range(8):
        out_ref[peer] = low[:64]


def spread_z_kernel(own_ref, far_ref, out_ref):
    place = (lax.axis_index("ctx") // 4) % 4
    for dest in range(4):

        @pl.when(dest >= place)
        def _(dest=dest):
            out_ref[dest] = own_ref[...]

        @pl.when(dest < place)
        def _(dest=dest):
            out_ref[dest] = far_ref[...]


def spread_y_kernel(z_ref, far_ref, out_ref):
    index = lax.axis_index("ctx")
    place, y = (index // 4) % 4, index % 4
    for dest in range(4):
        out_ref[dest] = z_ref[...]

        @pl.when(dest < y)
        def _(dest=dest):
            out_ref[dest, place] = far_ref[...]


def gradient_kernel(f_ref, low_ref, od_ref, g_ref, sum_ref):
    low = low_ref[0].astype(F32)
    for peer in range(1, 8):
        low = low + low_ref[peer].astype(F32)
    sum_ref[...] = low
    u = low[48:64].T.astype(BF16)
    for n in range(GROUP):
        cols = slice(n * HEAD, (n + 1) * HEAD)
        g_n = f_ref[:, cols].astype(F32) + ADAPTER_SCALE * nt(u, od_ref[cols, :])
        g_ref[:, cols] = g_n.astype(BF16)


def attention_kernel(
    q_ref, g_ref, low_ref, od_ref, qu_ref, kv_ref, len_ref,
    dq_ref, dkv_ref, back_ref, tot_ref,
    qs, qt, gs, gt, s_ref, ot, dqt, dk, dv, bias, top, total, delta,
):
    index = lax.axis_index("ctx")
    here = index % 16
    xa_q = low_ref[0:16].astype(BF16)
    u_t = low_ref[48:64].astype(BF16)
    doc = lax.broadcasted_iota(jnp.int32, (128, 128), 0)
    lane = lax.broadcasted_iota(jnp.int32, (128, 128), 1)
    lengths = jnp.broadcast_to(len_ref[...].astype(F32), (128, 128))
    ends = jnp.sum(jnp.where(lane <= doc, lengths, 0.0), axis=1, keepdims=True)
    position = (lane + index * ROWS).astype(F32)
    start = jnp.max(jnp.where(ends <= position, ends, 0.0), axis=0, keepdims=True)
    first = jnp.min(start).astype(jnp.int32)
    reach = jnp.maximum(index * ROWS - first + ROWS - 1, 0) // ROWS
    start = start.astype(jnp.int32)
    q_pos = lax.broadcasted_iota(jnp.int32, (1, 128), 1) + index * ROWS
    for n in range(GROUP):
        cols = slice(n * HEAD, (n + 1) * HEAD)
        q_n = q_ref[:, cols]
        qs[cols, :] = q_n
        qt[:, cols] = q_n.T
        g_n = g_ref[:, cols]
        gs[cols, :] = g_n
        gt[:, cols] = g_n.T
    top[...] = jnp.full_like(top, NEG)
    total[...] = jnp.zeros_like(total)
    ot[...] = jnp.zeros_like(ot)
    dqt[...] = jnp.zeros_like(dqt)

    def live(plane):
        nearest = jnp.minimum(
            jnp.minimum((here - 4 * plane) & 15, (here - 4 * plane - 1) & 15),
            jnp.minimum((here - 4 * plane - 2) & 15, (here - 4 * plane - 3) & 15),
        )
        return nearest <= reach

    pairs = [slice(256 * p, 256 * (p + 1)) for p in range(4)]

    def keys(plane, which):
        return kv_ref[:, plane, which].reshape(512, HEAD)

    def scores(plane, _):
        @pl.when(live(plane))
        def _():
            for y in range(4):
                back = (here - 4 * plane - y) & 15
                k_pos = lax.broadcasted_iota(jnp.int32, (128, 128), 0) + (index - back) * ROWS
                bias[y * 128 : (y + 1) * 128, :] = jnp.where(
                    (k_pos >= start) & (k_pos <= q_pos), 0.0, NEG
                )
            key_quad = keys(plane, 0)
            for cols in pairs:
                raw = nn(key_quad, qt[:, cols])
                wide_bias = jnp.concatenate([bias[...], bias[...]], axis=1)
                raw = raw * (SCALE * LOG2E) + wide_bias
                s_ref[plane, :, cols] = raw
                top[:, cols] = jnp.maximum(top[:, cols], jnp.max(raw, axis=0, keepdims=True))

        return 0

    lax.fori_loop(0, 4, scores, 0)

    def weigh(plane, _):
        @pl.when(live(plane))
        def _():
            value_quad = keys(plane, 1)
            for cols in pairs:
                prob = jnp.exp2(s_ref[plane, :, cols] - top[:, cols])
                s_ref[plane, :, cols] = prob
                total[:, cols] += jnp.sum(prob, axis=0, keepdims=True)
                ot[:, cols] += tn(value_quad, prob.astype(BF16))

        return 0

    lax.fori_loop(0, 4, weigh, 0)
    total[...] = 1.0 / total[...]
    for n in range(GROUP):
        cols = slice(n * HEAD, (n + 1) * HEAD)
        o_n = (ot[:, cols] * total[:, cols]).astype(BF16)
        delta[:, cols] = jnp.sum(
            o_n.astype(F32) * gt[:, cols].astype(F32), axis=0, keepdims=True
        )

    def grads(plane, _):
        @pl.when(live(plane))
        def _():
            key_quad = keys(plane, 0)
            value_quad = keys(plane, 1)
            for p, cols in enumerate(pairs):
                prob = s_ref[plane, :, cols] * total[:, cols]
                grad_prob = nn(value_quad, gt[:, cols])
                grad_score = (prob * (grad_prob - delta[:, cols])).astype(BF16)
                dqt[:, cols] += tn(key_quad, grad_score)
                part_k = nn(grad_score, qs[cols, :])
                part_v = nn(prob.astype(BF16), gs[cols, :])
                if p == 0:
                    dk[...] = part_k
                    dv[...] = part_v
                else:
                    dk[...] += part_k
                    dv[...] += part_v
            dkv_ref[:, plane, 0] = (dk[...] * SCALE).astype(BF16).reshape(4, 128, HEAD)
            dkv_ref[:, plane, 1] = dv[...].astype(BF16).reshape(4, 128, HEAD)

        @pl.when(jnp.logical_not(live(plane)))
        def _():
            for y in range(4):
                dkv_ref[y, plane] = jnp.zeros((2, 128, HEAD), BF16)

        return 0

    lax.fori_loop(0, 4, grads, 0)
    out_adapter = jnp.zeros((RANK, ROWS), F32)
    back_q = jnp.zeros((RANK, ROWS), F32)
    for n in range(GROUP):
        cols = slice(n * HEAD, (n + 1) * HEAD)
        dq_t = (dqt[:, cols] * SCALE).astype(BF16)
        dq_n = dq_t.T
        dq_ref[:, cols] = dq_n
        back_q = back_q + nn(qu_ref[:, cols], dq_t)
        tot_ref[GROUP + n] = (ADAPTER_SCALE * nn(xa_q, dq_n)).astype(BF16)
        o_n = (ot[:, cols] * total[:, cols]).astype(BF16)
        out_adapter = out_adapter + tn(od_ref[cols, :], o_n)
        tot_ref[n] = (ADAPTER_SCALE * nt(u_t, o_n)).astype(BF16)
    back_ref[0:16] = out_adapter
    back_ref[16:32] = back_q
    back_ref[32:64] = low_ref[16:48]


def gather_y_kernel(y_ref, out_ref, far_ref):
    index = lax.axis_index("ctx")
    place, y = (index // 4) % 4, index % 4
    for plane in range(4):
        acc = y_ref[0, plane].astype(F32)
        for source in range(1, 4):
            acc = acc + y_ref[source, plane].astype(F32)
        out_ref[plane] = acc.astype(BF16)
    mine = jnp.zeros((2, 128, HEAD), F32)
    far = jnp.zeros((2, 128, HEAD), F32)
    for source in range(4):
        term = y_ref[source, place].astype(F32)
        keep = (source >= y).astype(F32)
        mine = mine + term * keep
        far = far + term * (1.0 - keep)
    out_ref[place] = mine.astype(BF16)
    far_ref[...] = far


def gather_z_kernel(z_ref, far_ref, own_ref, send_ref):
    place = (lax.axis_index("ctx") // 4) % 4
    mine = jnp.zeros((2, 128, HEAD), F32)
    far = far_ref[...]
    for source in range(4):
        term = z_ref[source].astype(F32)
        keep = (source >= place).astype(F32)
        mine = mine + term * keep
        far = far + term * (1.0 - keep)
    own_ref[...] = mine
    send_ref[...] = far.astype(BF16)


def owner_kernel(own_ref, far_ref, back_ref, ku_ref, vu_ref, dk_ref, dv_ref, out_ref, tot_ref):
    d_k = (own_ref[0] + far_ref[0].astype(F32)).astype(BF16)
    d_v = (own_ref[1] + far_ref[1].astype(F32)).astype(BF16)
    dk_ref[...] = d_k
    dv_ref[...] = d_v
    xa_k = back_ref[32:48].astype(BF16)
    xa_v = back_ref[48:64].astype(BF16)
    tot_ref[0] = (ADAPTER_SCALE * nn(xa_k, d_k)).astype(BF16)
    tot_ref[1] = (ADAPTER_SCALE * nn(xa_v, d_v)).astype(BF16)
    back_k = nt(ku_ref[...], d_k)
    back_v = nt(vu_ref[...], d_v)
    sent = jnp.concatenate([back_ref[0:32], back_k, back_v], axis=0).astype(BF16)
    for peer in range(8):
        out_ref[peer] = sent


def down_kernel(low_ref, x_ref, dout_ref, tot_ref, kv_tot_ref, out_ref):
    low = low_ref[0].astype(F32)
    for peer in range(1, 8):
        low = low + low_ref[peer].astype(F32)
    low = low.astype(BF16)
    down = (ADAPTER_SCALE * nn(low[16:64], x_ref[...])).astype(BF16)
    up = (ADAPTER_SCALE * nn(low[0:16], dout_ref[...])).astype(BF16)
    tiles = []
    for which in range(3):
        for t in range(5):
            tiles.append(down[which * 16 : (which + 1) * 16, t * 128 : (t + 1) * 128])
    for t in range(5):
        tiles.append(up[:, t * 128 : (t + 1) * 128])
    for t in range(16):
        tiles.append(tot_ref[t])
    tiles.append(kv_tot_ref[0])
    tiles.append(kv_tot_ref[1])
    zero = jnp.zeros((16, 128), BF16)
    tiles += [zero, zero]
    for t, tile in enumerate(tiles):
        out_ref[t // 5, t % 5] = tile


def sum_spread_kernel(in_ref, out_ref):
    acc = in_ref[0].astype(F32)
    for peer in range(1, 8):
        acc = acc + in_ref[peer].astype(F32)
    acc = acc.astype(BF16)
    for peer in range(8):
        out_ref[peer] = acc


def unpack_kernel(in_ref, qd_ref, qu_ref, kd_ref, ku_ref, vd_ref, vu_ref, od_ref, ou_ref):
    def tile(t):
        return in_ref[t // 5, t % 5].astype(F32)

    for which, ref in enumerate((qd_ref, kd_ref, vd_ref)):
        for t in range(5):
            ref[t * 128 : (t + 1) * 128, :] = tile(which * 5 + t).T
    for t in range(5):
        ou_ref[:, t * 128 : (t + 1) * 128] = tile(15 + t)
    for t in range(8):
        od_ref[t * 128 : (t + 1) * 128, :] = tile(20 + t).T
        qu_ref[:, t * 128 : (t + 1) * 128] = tile(28 + t)
    ku_ref[...] = tile(36)
    vu_ref[...] = tile(37)


def shift(value, steps):
    count = lax.axis_size("ctx")
    first, last = max(0, -steps), min(count, count - steps)
    return lax.ppermute(value, "ctx", [(i, i + steps) for i in range(first, last)])


def exchange(value, groups):
    return lax.all_to_all(value, "ctx", 0, 0, tiled=True, axis_index_groups=groups)


def exchange_head(value):
    return lax.all_to_all(value, "head", 0, 0, tiled=True)


def shards(x, q, keys, values, frozen, dout, lengths, qd, qu, kd, ku, vd, vu, od, ou):
    pair = jnp.stack([keys, values])
    far = shift(pair, 16)
    low = call(
        project_kernel, shaped((8, 64, 128), BF16), x, dout, qd, kd, vd, ou,
        scratch=[pltpu.VMEM((128, 128), F32)],
    )
    grad_heads, low = call(
        gradient_kernel,
        (shaped((128, 1024), BF16), shaped((64, 128), F32)),
        frozen, exchange_head(low), od,
    )
    by_z = exchange(call(spread_z_kernel, shaped((4, 2, 128, 128), BF16), pair, far), Z_FOURS)
    window = call(spread_y_kernel, shaped((4, 4, 2, 128, 128), BF16), by_z, far)
    window = exchange(window, Y_GROUPS)
    dq, dkv, back, totals = call(
        attention_kernel,
        (
            shaped((128, 1024), BF16),
            shaped((4, 4, 2, 128, 128), BF16),
            shaped((64, 128), F32),
            shaped((16, 16, 128), BF16),
        ),
        q, grad_heads, low, od, qu, window, lengths.reshape(1, 128),
        scratch=[
            pltpu.VMEM((1024, 128), BF16),
            pltpu.VMEM((128, 1024), BF16),
            pltpu.VMEM((1024, 128), BF16),
            pltpu.VMEM((128, 1024), BF16),
            pltpu.VMEM((4, 512, 1024), F32),
            pltpu.VMEM((128, 1024), F32),
            pltpu.VMEM((128, 1024), F32),
            pltpu.VMEM((512, 128), F32),
            pltpu.VMEM((512, 128), F32),
            pltpu.VMEM((512, 128), F32),
            pltpu.VMEM((1, 1024), F32),
            pltpu.VMEM((1, 1024), F32),
            pltpu.VMEM((1, 1024), F32),
        ],
        vmem=48,
        flops=3 << 30,
    )
    dkv = exchange(dkv, Y_GROUPS)
    dkv, far_sum = call(
        gather_y_kernel, (shaped((4, 2, 128, 128), BF16), shaped((2, 128, 128), F32)), dkv
    )
    dkv = exchange(dkv, Z_FOURS)
    own, far_send = call(
        gather_z_kernel,
        (shaped((2, 128, 128), F32), shaped((2, 128, 128), BF16)),
        dkv, far_sum,
    )
    arrived = shift(far_send, -16)
    dk, dv, low_back, kv_totals = call(
        owner_kernel,
        (
            shaped((128, 128), BF16),
            shaped((128, 128), BF16),
            shaped((8, 64, 128), BF16),
            shaped((2, 16, 128), BF16),
        ),
        own, arrived, back, ku, vu,
    )
    low_back = exchange_head(low_back)
    packed = shaped((8, 5, 16, 128), BF16)
    sums = call(down_kernel, packed, low_back, x, dout, totals, kv_totals)
    sums = call(sum_spread_kernel, packed, exchange(sums, EIGHTS))
    sums = call(sum_spread_kernel, packed, exchange(sums, STRIDED))
    sums = exchange(sums, EIGHTS)
    grads = call(
        unpack_kernel,
        (
            shaped((640, 16), F32),
            shaped((16, 1024), F32),
            shaped((640, 16), F32),
            shaped((16, 128), F32),
            shaped((640, 16), F32),
            shaped((16, 128), F32),
            shaped((1024, 16), F32),
            shaped((16, 640), F32),
        ),
        sums,
    )
    return (dq, dk, dv, *grads)


def solution(mesh):
    rows, cols, tokens = P("head", None), P(None, "head"), P("ctx", "head")
    return jax.shard_map(
        shards,
        mesh=mesh,
        in_specs=(tokens,) * 6 + (P(),) + (rows, cols) * 4,
        out_specs=(tokens,) * 3 + (rows, cols) * 4,
        check_vma=False,
    )
```

time: 955 us -> 167 us (0.17)
  waiting for transfers between devices: 695 us -> 42.3 us
  starting transfers between devices: 100 us -> 28 us
  matrix products: 45.2 us -> 0 us
  blocking collectives: 40.1 us -> 78.1 us
  local copies, waits for them, and re-layouts: 31.4 us -> 6.38 us
  other arithmetic: 23.9 us -> 0.78 us
  between operations: 14.4 us -> 0.74 us
  Pallas kernels: 0 us -> 9.96 us
    psum x2 -> x0, waiting for transfers between devices: 563 us -> none  [shards(): lax.psum((ADAPTER_SCALE * contract_leading(normalized_layer_input, query_...]
    ppermute x30 -> x2, waiting for transfers between devices: 132 us -> 19 us  [shift(): lax.ppermute(value, 'ctx', [(i, i + steps) for i in range(first, last)])]
    ppermute x30 -> x2, starting transfers between devices: 100 us -> 10.4 us  [shift(): lax.ppermute(value, 'ctx', [(i, i + steps) for i in range(first, last)])]
    all_to_all x0 -> x6, blocking collectives: none -> 78.1 us  [the longest x5 69.6 us: exchange(): lax.all_to_all(value, 'ctx', 0, 0, tiled=True, axis_index_groups=groups)]
    dot_general x129 -> x0, matrix products: 45.2 us -> none  [the longest x16 11.4 us: stats_live(): jnp.einsum('hgqk,khd->hgqd', weights, value_block.astype(jnp.float32), pr...]
    psum x2 -> x0, blocking collectives: 40.1 us -> none  [the longest x1 24.9 us: shards(): lax.psum((output_portion, query_backward, key_backward, value_backward),...]
    all_to_all x0 -> x3, waiting for transfers between devices: none -> 23.3 us  [the longest x2 19.7 us: exchange(): lax.all_to_all(value, 'ctx', 0, 0, tiled=True, axis_index_groups=groups)]
    all_to_all x0 -> x3, starting transfers between devices: none -> 17.7 us  [the longest x2 12.8 us: exchange(): lax.all_to_all(value, 'ctx', 0, 0, tiled=True, axis_index_groups=groups)]
  transfers between devices with their start and end apart: 32 -> 5, of which waited for: 32 -> 5; matrix products, arithmetic and copies ran while one was open for 2% -> 0% of each run, Pallas kernels for 0% -> 2%
where the time goes in v1:
time: 167 us; the launch traced here: 166 us
  blocking collectives  78.1 us (47%)
  waiting for transfers between devices  42.3 us (25%)
  starting transfers between devices  28 us (17%)
  Pallas kernels  9.96 us (6%)
  local copies, waits for them, and re-layouts  6.38 us (4%)
    all_to_all x5, blocking collectives, exchange(): lax.all_to_all(value, 'ctx', 0, 0, tiled=True, axis_index_groups=groups)  69.6 us
    all_to_all x2, waiting for transfers between devices, exchange(): lax.all_to_all(value, 'ctx', 0, 0, tiled=True, axis_index_groups=groups)  19.7 us
    ppermute x2, waiting for transfers between devices, shift(): lax.ppermute(value, 'ctx', [(i, i + steps) for i in range(first, last)])  19 us
    all_to_all x2, starting transfers between devices, exchange(): lax.all_to_all(value, 'ctx', 0, 0, tiled=True, axis_index_groups=groups)  12.8 us
    ppermute x2, starting transfers between devices, shift(): lax.ppermute(value, 'ctx', [(i, i + steps) for i in range(first, last)])  10.4 us
    pallas_call x12, Pallas kernels, call(): pl.pallas_call(body, out_shape=outs, in_specs=[pl.BlockSpec(memory_space=...  9.96 us
    all_to_all x1, blocking collectives, exchange_head(): return lax.all_to_all(value, 'head', 0, 0, tiled=True)  8.5 us
    unnamed x34, local copies, waits for them, and re-layouts  6.38 us
  transfers between devices with their start and end apart: 5, of which 5 were waited for; matrix products, arithmetic and copies ran while one was open for 0% of the time, Pallas kernels for 2%

profile of v1, /device:TPU:2, one launch (start us, length us, event | category | flops | bytes accessed | tf_op | source)
XLA Modules:
  0.0 166.3 jit_solution(9944557352030701099)
XLA Ops:
  0.6 0.8 pad_maximum_fusion.own_ref
  1.4 9.1 %collective-permute-start = (bf16[2,128,128]{2,1,0:T(8,128)(2,1)S(1)}, bf16[2,128,128]{2,1,0:T(8,128)(2,1)S(1)}, u32[]{:S(2)}, u32[]{:S(2)}) collective-permute-start(bf16[2,128,128]{2,1,0:T(8,128)(2,1)S(1)} %pad_maximum_fusion.own_ref), channel_id=1, source_target_pairs={{0,128},{8,136},{16,144},{24,152},{32,160},{40,168},{48,176},{56,1... | collective-permute-start | bytes 196616 | tf_op jit(solution)/shard_map/ppermute | solution.py:333
  10.5 1.9 %collective-permute-done.far_ref = bf16[2,128,128]{2,1,0:T(8,128)(2,1)S(1)} collective-permute-done((bf16[2,128,128]{2,1,0:T(8,128)(2,1)S(1)}, bf16[2,128,128]{2,1,0:T(8,128)(2,1)S(1)}, u32[]{:S(2)}, u32[]{:S(2)}) %collective-permute-start) | collective-permute-done | bytes 65568 | tf_op jit(solution)/shard_map/ppermute | solution.py:333
  12.4 0.7 shard_map.232
  13.1 0.0 copy-start.10
  13.1 8.4 %all-to-all-start.1 = ((bf16[4,2,128,128]{3,2,1,0:T(8,128)(2,1)}), bf16[4,2,128,128]{3,2,1,0:T(8,128)(2,1)S(1)}, u32[]{:S(2)}, u32[]{:S(2)}) async-start(bf16[4,2,128,128]{3,2,1,0:T(8,128)(2,1)} %shard_map.232), calls=%async_computation.1 | async-start | bytes 524288 | tf_op jit(solution)/shard_map/all_to_all | solution.py:337
  21.5 0.0 copy-done.10
  21.5 0.0 copy-start.11
  21.5 0.0 copy-start.12
  21.5 0.2 copy.26.qd_ref
  21.7 0.6 copy-done.11
  22.2 0.0 copy-start
  22.2 0.0 copy-start.1
  22.2 0.2 copy.27.kd_ref
  22.4 0.0 copy-done.12
  22.4 0.0 copy-start.3
  22.4 0.2 copy.28.vd_ref
  22.6 0.6 copy-done
  23.1 0.1 copy-done.1
  23.2 0.0 copy-done.3
  23.2 1.1 shard_map.230
  24.3 6.1 %all-to-all-done.1.z_ref = bf16[4,2,128,128]{3,2,1,0:T(8,128)(2,1)S(1)} async-done(((bf16[4,2,128,128]{3,2,1,0:T(8,128)(2,1)}), bf16[4,2,128,128]{3,2,1,0:T(8,128)(2,1)S(1)}, u32[]{:S(2)}, u32[]{:S(2)}) %all-to-all-start.1) | async-done | bytes 262176 | tf_op jit(solution)/shard_map/all_to_all | solution.py:337
  30.5 4.8 %all-to-all-start = ((bf16[8,64,128]{2,1,0:T(8,128)(2,1)}), bf16[8,64,128]{2,1,0:T(8,128)(2,1)S(1)}, u32[]{:S(2)}, u32[]{:S(2)}) async-start(bf16[8,64,128]{2,1,0:T(8,128)(2,1)} %shard_map.230), calls=%async_computation | async-start | bytes 262144 | tf_op jit(solution)/shard_map/all_to_all | solution.py:341
  35.3 1.1 shard_map.233
  36.4 0.0 copy-start.9
  36.4 3.6 %all-to-all-done.low_ref = bf16[8,64,128]{2,1,0:T(8,128)(2,1)S(1)} async-done(((bf16[8,64,128]{2,1,0:T(8,128)(2,1)}), bf16[8,64,128]{2,1,0:T(8,128)(2,1)S(1)}, u32[]{:S(2)}, u32[]{:S(2)}) %all-to-all-start) | async-done | bytes 131104 | tf_op jit(solution)/shard_map/all_to_all | solution.py:341
  40.0 4.5 %all-to-all-start.2 = ((bf16[4,4,2,128,128]{4,3,2,1,0:T(8,128)(2,1)}), bf16[4,4,2,128,128]{4,3,2,1,0:T(8,128)(2,1)S(1)}, u32[]{:S(2)}, u32[]{:S(2)}) async-start(bf16[4,4,2,128,128]{4,3,2,1,0:T(8,128)(2,1)} %shard_map.233), calls=%async_computation.2 | async-start | bytes 2097152 | tf_op jit(solution)/shard_map/all_to_all | solution.py:337
  44.4 0.0 copy-done.9
  44.4 0.0 copy-start.2
  44.4 0.2 copy.29.od_ref
  44.6 0.8 copy-done.2
  45.4 0.0 copy-start.6
  45.4 0.0 copy-start.7
  45.4 0.3 shard_map.231
  45.7 13.6 %all-to-all-done.2.kv_ref = bf16[4,4,2,128,128]{4,3,2,1,0:T(8,128)(2,1)S(1)} async-done(((bf16[4,4,2,128,128]{4,3,2,1,0:T(8,128)(2,1)}), bf16[4,4,2,128,128]{4,3,2,1,0:T(8,128)(2,1)S(1)}, u32[]{:S(2)}, u32[]{:S(2)}) %all-to-all-start.2) | async-done | bytes 1048608 | tf_op jit(solution)/shard_map/all_to_all | solution.py:337
  59.3 0.0 copy-start.8
  59.3 0.0 copy-done.6
  59.3 0.0 copy-done.7
  59.3 0.6 copy-done.8
  60.0 4.6 %shard_map.234 = (bf16[128,1024]{1,0:T(8,128)(2,1)}, bf16[4,4,2,128,128]{4,3,2,1,0:T(8,128)(2,1)S(1)}, f32[64,128]{1,0:T(8,128)S(1)}, bf16[16,16,128]{2,1,0:T(8,128)(2,1)S(1)}) custom-call(bf16[128,1024]{1,0:T(8,128)(2,1)S(1)} %copy-done.6, bf16[128,1024]{1,0:T(8,128)(2,1)S(1)} %get-tuple-element.33.g_ref, f32[64,128]{1,0:T(8,128)S(1)} %get-tuple-element.34.low_ref, ...), custom_call_target="tpu_custom_call" | custom-call | flops 3221225472 | bytes 1048576 | tf_op jit(solution)/shard_map/pallas_call | solution.py:41
  64.6 16.4 %all_to_all.45.y_ref = bf16[4,4,2,128,128]{4,3,2,1,0:T(8,128)(2,1)S(1)} all-to-all(bf16[4,4,2,128,128]{4,3,2,1,0:T(8,128)(2,1)S(1)} %get-tuple-element.36), channel_id=1, replica_groups={{0,8,16,24},{32,40,48,56},{64,72,80,88},{96,104,112,120},{128,136,144,1..., dimensions={0} | all-to-all | bytes 2097152 | tf_op jit(solution)/shard_map/all_to_all | solution.py:337
  81.0 0.2 shard_map.235
  81.2 12.4 %all_to_all.46.z_ref = bf16[4,2,128,128]{3,2,1,0:T(8,128)(2,1)S(1)} all-to-all(bf16[4,2,128,128]{3,2,1,0:T(8,128)(2,1)S(1)} %get-tuple-element.37), channel_id=1, replica_groups={{0,32,64,96},{8,40,72,104},{16,48,80,112},{24,56,88,120},{128,160,192,2..., dimensions={0} | all-to-all | bytes 524288 | tf_op jit(solution)/shard_map/all_to_all | solution.py:337
  93.6 0.0 copy-start.5
  93.6 0.1 shard_map.236
  93.7 0.0 copy-start.4
  93.7 1.3 collective-permute-start.1
  95.0 17.1 %collective-permute-done.1.far_ref = bf16[2,128,128]{2,1,0:T(8,128)(2,1)S(1)} collective-permute-done((bf16[2,128,128]{2,1,0:T(8,128)(2,1)S(1)}, bf16[2,128,128]{2,1,0:T(8,128)(2,1)S(1)}, u32[]{:S(2)}, u32[]{:S(2)}) %collective-permute-start.1) | collective-permute-done | bytes 65568 | tf_op jit(solution)/shard_map/ppermute | solution.py:333
  112.1 0.0 copy-done.5
  112.1 0.0 copy-done.4
  112.1 0.6 shard_map.237
  112.8 8.5 %all_to_all.47.low_ref = bf16[8,64,128]{2,1,0:T(8,128)(2,1)S(1)} all-to-all(bf16[8,64,128]{2,1,0:T(8,128)(2,1)S(1)} %get-tuple-element.44), channel_id=1, replica_groups=mesh['ctx'=64,'head'=8] {'head'}, dimensions={0} | all-to-all | bytes 262144 | tf_op jit(solution)/shard_map/all_to_all | solution.py:341
  121.3 0.2 shard_map.238
  121.4 9.2 %all_to_all.48.in_ref = bf16[8,5,16,128]{3,2,1,0:T(8,128)(2,1)S(1)} all-to-all(bf16[8,5,16,128]{3,2,1,0:T(8,128)(2,1)S(1)} %shard_map.238), channel_id=1, replica_groups={{0,8,16,24,32,40,48,56},{64,72,80,88,96,104,112,120},{128,136,144,152,1..., dimensions={0} | all-to-all | bytes 327680 | tf_op jit(solution)/shard_map/all_to_all | solution.py:337
  130.6 21.7 %all_to_all.49.in_ref = bf16[8,5,16,128]{3,2,1,0:T(8,128)(2,1)S(1)} all-to-all(bf16[8,5,16,128]{3,2,1,0:T(8,128)(2,1)S(1)} %shard_map.239), channel_id=1, replica_groups={{0,64,128,192,256,320,384,448},{8,72,136,200,264,328,392,456},{16,80,14..., dimensions={0} | all-to-all | bytes 327680 | tf_op jit(solution)/shard_map/all_to_all | solution.py:337
  152.3 10.1 %all_to_all.50.in_ref = bf16[8,5,16,128]{3,2,1,0:T(8,128)(2,1)S(1)} all-to-all(bf16[8,5,16,128]{3,2,1,0:T(8,128)(2,1)S(1)} %shard_map.240), channel_id=1, replica_groups={{0,8,16,24,32,40,48,56},{64,72,80,88,96,104,112,120},{128,136,144,152,1..., dimensions={0} | all-to-all | bytes 327680 | tf_op jit(solution)/shard_map/all_to_all | solution.py:337
  162.4 0.8 shard_map.241
  163.2 0.8 copy.31
  164.0 0.8 copy.32
  164.8 0.8 copy.33
  165.5 0.8 copy.34
  (2 shorter events, 0.1 us)
Async XLA Ops:
  1.4 11.0 %collective-permute-start = (bf16[2,128,128]{2,1,0:T(8,128)(2,1)S(1)}, bf16[2,128,128]{2,1,0:T(8,128)(2,1)S(1)}, u32[]{:S(2)}, u32[]{:S(2)}) collective-permute-start(bf16[2,128,128]{2,1,0:T(8,128)(2,1)S(1)} %pad_maximum_fusion.own_ref), channel_id=1, source_target_pairs={{0,128},{8,136},{16,144},{24,152},{32,160},{40,168},{48,176},{56,1... | collective-permute-start | bytes 196616 | tf_op jit(solution)/shard_map/ppermute | solution.py:333
  13.1 8.4 %copy-start.10 = (bf16[640,16]{0,1:T(8,128)(2,1)S(1)}, bf16[640,16]{0,1:T(8,128)(2,1)}, u32[]{:S(2)}) copy-start(bf16[640,16]{0,1:T(8,128)(2,1)} %param.22) | copy-start | bytes 61444
  13.1 17.3 %all-to-all-start.1 = ((bf16[4,2,128,128]{3,2,1,0:T(8,128)(2,1)}), bf16[4,2,128,128]{3,2,1,0:T(8,128)(2,1)S(1)}, u32[]{:S(2)}, u32[]{:S(2)}) async-start(bf16[4,2,128,128]{3,2,1,0:T(8,128)(2,1)} %shard_map.232), calls=%async_computation.1 | async-start | bytes 524288 | tf_op jit(solution)/shard_map/all_to_all | solution.py:337
  21.5 0.7 copy-start.11
  21.5 0.9 copy-start.12
  22.2 0.9 copy-start
  22.2 1.0 copy-start.1
  22.4 0.8 copy-start.3
  30.5 9.5 %all-to-all-start = ((bf16[8,64,128]{2,1,0:T(8,128)(2,1)}), bf16[8,64,128]{2,1,0:T(8,128)(2,1)S(1)}, u32[]{:S(2)}, u32[]{:S(2)}) async-start(bf16[8,64,128]{2,1,0:T(8,128)(2,1)} %shard_map.230), calls=%async_computation | async-start | bytes 262144 | tf_op jit(solution)/shard_map/all_to_all | solution.py:341
  36.4 8.1 %copy-start.9 = (bf16[1024,16]{0,1:T(8,128)(2,1)S(1)}, bf16[1024,16]{0,1:T(8,128)(2,1)}, u32[]{:S(2)}) copy-start(bf16[1024,16]{0,1:T(8,128)(2,1)} %param.28) | copy-start | bytes 98308
  40.0 19.4 %all-to-all-start.2 = ((bf16[4,4,2,128,128]{4,3,2,1,0:T(8,128)(2,1)}), bf16[4,4,2,128,128]{4,3,2,1,0:T(8,128)(2,1)S(1)}, u32[]{:S(2)}, u32[]{:S(2)}) async-start(bf16[4,4,2,128,128]{4,3,2,1,0:T(8,128)(2,1)} %shard_map.233), calls=%async_computation.2 | async-start | bytes 2097152 | tf_op jit(solution)/shard_map/all_to_all | solution.py:337
  44.4 1.0 copy-start.2
  45.4 14.0 %copy-start.6 = (bf16[128,1024]{1,0:T(8,128)(2,1)S(1)}, bf16[128,1024]{1,0:T(8,128)(2,1)}, u32[]{:S(2)}) copy-start(bf16[128,1024]{1,0:T(8,128)(2,1)} %q_ref.1) | copy-start | bytes 786436
  45.4 14.0 %copy-start.7 = (bf16[16,1024]{1,0:T(8,128)(2,1)S(1)}, bf16[16,1024]{1,0:T(8,128)(2,1)}, u32[]{:S(2)}) copy-start(bf16[16,1024]{1,0:T(8,128)(2,1)} %qu_ref.1) | copy-start | bytes 98308
  59.3 0.7 copy-start.8
  93.6 18.5 %copy-start.5 = (bf16[16,128]{1,0:T(8,128)(2,1)S(1)}, bf16[16,128]{1,0:T(8,128)(2,1)}, u32[]{:S(2)}) copy-start(bf16[16,128]{1,0:T(8,128)(2,1)} %vu_ref.1) | copy-start | bytes 12292
  93.7 18.4 %copy-start.4 = (bf16[16,128]{1,0:T(8,128)(2,1)S(1)}, bf16[16,128]{1,0:T(8,128)(2,1)}, u32[]{:S(2)}) copy-start(bf16[16,128]{1,0:T(8,128)(2,1)} %ku_ref.1) | copy-start | bytes 12292
  93.7 18.4 %collective-permute-start.1 = (bf16[2,128,128]{2,1,0:T(8,128)(2,1)S(1)}, bf16[2,128,128]{2,1,0:T(8,128)(2,1)S(1)}, u32[]{:S(2)}, u32[]{:S(2)}) collective-permute-start(bf16[2,128,128]{2,1,0:T(8,128)(2,1)S(1)} %get-tuple-element.40), channel_id=1, source_target_pairs={{128,0},{136,8},{144,16},{152,24},{160,32},{168,40},{176,48},{184,... | collective-permute-start | bytes 196616 | tf_op jit(solution)/shard_map/ppermute | solution.py:333

commit v2 on v1

v2 whole, which is shorter than its diff:
```python
import functools

import jax
import jax.numpy as jnp
from jax import lax
from jax.experimental import pallas as pl
from jax.experimental.pallas import tpu as pltpu
from jax.sharding import PartitionSpec as P

HEAD = 128
ROWS = 128
GROUP = 8
RANK = 16
TILES = 40
SCALE = HEAD**-0.5
LOG2E = 1.4426950408889634
ADAPTER_SCALE = 2.0
NEG = -1e30
F32 = jnp.float32
BF16 = jnp.bfloat16

Y_GROUPS = [[4 * z + y for y in range(4)] for z in range(16)]
EIGHTS = [[8 * g + i for i in range(8)] for g in range(8)]
STRIDED = [[g + 8 * i for i in range(8)] for g in range(8)]


def nn(a, b):
    return lax.dot_general(a, b, (((1,), (0,)), ((), ())), preferred_element_type=F32)


def nt(a, b):
    return lax.dot_general(a, b, (((1,), (1,)), ((), ())), preferred_element_type=F32)


def tn(a, b):
    return lax.dot_general(a, b, (((0,), (0,)), ((), ())), preferred_element_type=F32)


def call(body, outs, *args, scratch=(), vmem=32, flops=1 << 20):
    return pl.pallas_call(
        body,
        out_shape=outs,
        scratch_shapes=list(scratch),
        compiler_params=pltpu.CompilerParams(vmem_limit_bytes=vmem << 20),
        cost_estimate=pl.CostEstimate(flops=flops, bytes_accessed=1 << 20, transcendentals=0),
    )(*args)


def shaped(shape, dtype):
    return jax.ShapeDtypeStruct(shape, dtype)


def project_kernel(x_ref, dout_ref, qd_ref, kd_ref, vd_ref, ou_ref, out_ref):
    parts = [nt(ref[...], x_ref[...]) for ref in (qd_ref, kd_ref, vd_ref)]
    parts.append(nt(ou_ref[...], dout_ref[...]))
    low = jnp.concatenate(parts, axis=0).astype(BF16)
    for peer in range(8):
        out_ref[peer] = low


def spread_kernel(
    pair_ref, one_ref, two_ref, four_ref, low_ref, x_ref, out_ref, x_out, sum_ref
):
    y = lax.axis_index("ctx") % 4
    for dest in range(4):

        @pl.when(dest >= y)
        def _(dest=dest):
            out_ref[dest, 0] = pair_ref[...]

        @pl.when(dest < y)
        def _(dest=dest):
            out_ref[dest, 0] = four_ref[...]

        out_ref[dest, 1] = one_ref[...]
        out_ref[dest, 2] = two_ref[0]
        out_ref[dest, 3] = two_ref[1]
    low = low_ref[0].astype(F32)
    for peer in range(1, 8):
        low = low + low_ref[peer].astype(F32)
    low = low.astype(BF16)
    sum_ref[...] = low
    for t in range(5):
        x_out[t * 128 : (t + 1) * 128, :] = x_ref[:, t * 128 : (t + 1) * 128]
    x_out[640:672, :] = low[16:48]


def prepare_kernel(q_ref, f_ref, low_ref, od_ref, qs_ref, qt_ref, gs_ref, gt_ref):
    u = low_ref[48:64]
    for n in range(GROUP):
        cols = slice(n * HEAD, (n + 1) * HEAD)
        q_n = q_ref[:, cols]
        qs_ref[cols, :] = q_n
        qt_ref[:, cols] = q_n.T
        g_n = f_ref[:, cols].astype(F32) + ADAPTER_SCALE * tn(u, od_ref[:, cols])
        g_n = g_n.astype(BF16)
        gs_ref[cols, :] = g_n
        gt_ref[:, cols] = g_n.T


def attention_kernel(
    qs, qt, gs, gt, kv_ref, len_ref,
    dqt_ref, ot_ref, dkv_ref,
    s_ref, ot, dqt, dk, dv, bias, top, total, delta,
):
    index = lax.axis_index("ctx")
    y_place = index % 4
    doc = lax.broadcasted_iota(jnp.int32, (128, 128), 0)
    lane = lax.broadcasted_iota(jnp.int32, (128, 128), 1)
    lengths = jnp.broadcast_to(len_ref[...].astype(F32), (128, 128))
    ends = jnp.sum(jnp.where(lane <= doc, lengths, 0.0), axis=1, keepdims=True)
    position = (lane + index * ROWS).astype(F32)
    start = jnp.max(jnp.where(ends <= position, ends, 0.0), axis=0, keepdims=True)
    first = jnp.min(start).astype(jnp.int32)
    reach = jnp.maximum(index * ROWS - first + ROWS - 1, 0) // ROWS
    start = start.astype(jnp.int32)
    q_pos = lax.broadcasted_iota(jnp.int32, (1, 128), 1) + index * ROWS
    top[...] = jnp.full_like(top, NEG)
    total[...] = jnp.zeros_like(total)
    ot[...] = jnp.zeros_like(ot)
    dqt[...] = jnp.zeros_like(dqt)

    def live(plane):
        return jnp.maximum(4 * plane + y_place - 3, 0) <= reach

    pairs = [slice(256 * p, 256 * (p + 1)) for p in range(4)]

    def keys(plane, which):
        return kv_ref[:, plane, which].reshape(512, HEAD)

    def scores(plane, _):
        @pl.when(live(plane))
        def _():
            for y in range(4):
                back = (4 * plane + y_place - y) & 15
                k_pos = lax.broadcasted_iota(jnp.int32, (128, 128), 0) + (index - back) * ROWS
                bias[y * 128 : (y + 1) * 128, :] = jnp.where(
                    (k_pos >= start) & (k_pos <= q_pos), 0.0, NEG
                )
            key_quad = keys(plane, 0)
            for cols in pairs:
                raw = nn(key_quad, qt[:, cols])
                wide_bias = jnp.concatenate([bias[...], bias[...]], axis=1)
                raw = raw * (SCALE * LOG2E) + wide_bias
                s_ref[plane, :, cols] = raw
                top[:, cols] = jnp.maximum(top[:, cols], jnp.max(raw, axis=0, keepdims=True))

        return 0

    lax.fori_loop(0, 4, scores, 0)

    def weigh(plane, _):
        @pl.when(live(plane))
        def _():
            value_quad = keys(plane, 1)
            for cols in pairs:
                prob = jnp.exp2(s_ref[plane, :, cols] - top[:, cols])
                s_ref[plane, :, cols] = prob
                total[:, cols] += jnp.sum(prob, axis=0, keepdims=True)
                ot[:, cols] += tn(value_quad, prob.astype(BF16))

        return 0

    lax.fori_loop(0, 4, weigh, 0)
    total[...] = 1.0 / total[...]
    for n in range(GROUP):
        cols = slice(n * HEAD, (n + 1) * HEAD)
        o_n = (ot[:, cols] * total[:, cols]).astype(BF16)
        ot_ref[:, cols] = o_n
        delta[:, cols] = jnp.sum(
            o_n.astype(F32) * gt[:, cols].astype(F32), axis=0, keepdims=True
        )

    def grads(plane, _):
        @pl.when(live(plane))
        def _():
            key_quad = keys(plane, 0)
            value_quad = keys(plane, 1)
            for p, cols in enumerate(pairs):
                prob = s_ref[plane, :, cols] * total[:, cols]
                grad_prob = nn(value_quad, gt[:, cols])
                grad_score = (prob * (grad_prob - delta[:, cols])).astype(BF16)
                dqt[:, cols] += tn(key_quad, grad_score)
                part_k = nn(grad_score, qs[cols, :])
                part_v = nn(prob.astype(BF16), gs[cols, :])
                if p == 0:
                    dk[...] = part_k
                    dv[...] = part_v
                else:
                    dk[...] += part_k
                    dv[...] += part_v
            dkv_ref[:, plane, 0] = (dk[...] * SCALE).astype(BF16).reshape(4, 128, HEAD)
            dkv_ref[:, plane, 1] = dv[...].astype(BF16).reshape(4, 128, HEAD)

        @pl.when(jnp.logical_not(live(plane)))
        def _():
            for y in range(4):
                dkv_ref[y, plane] = jnp.zeros((2, 128, HEAD), BF16)

        return 0

    lax.fori_loop(0, 4, grads, 0)
    dqt_ref[...] = (dqt[...] * SCALE).astype(BF16)


def finish_kernel(dqt_ref, ot_ref, low_ref, od_ref, qu_ref, dq_ref, back_ref, tot_ref):
    xa_q = low_ref[0:16]
    u = low_ref[48:64]
    out_adapter = jnp.zeros((RANK, ROWS), F32)
    back_q = jnp.zeros((RANK, ROWS), F32)
    for n in range(GROUP):
        cols = slice(n * HEAD, (n + 1) * HEAD)
        dq_t = dqt_ref[:, cols]
        dq_n = dq_t.T
        dq_ref[:, cols] = dq_n
        back_q = back_q + nn(qu_ref[:, cols], dq_t)
        tot_ref[GROUP + n] = (ADAPTER_SCALE * nn(xa_q, dq_n)).astype(BF16)
        o_n = ot_ref[:, cols]
        out_adapter = out_adapter + nn(od_ref[:, cols], o_n)
        tot_ref[n] = (ADAPTER_SCALE * nt(u, o_n)).astype(BF16)
    back_ref[0:16] = out_adapter.astype(BF16)
    back_ref[16:32] = back_q.astype(BF16)


def gather_kernel(y_ref, back_ref, ku_ref, vu_ref, part_ref, out_ref):
    y = lax.axis_index("ctx") % 4
    parts = []
    for plane in range(5):
        term = [y_ref[source, plane % 4].astype(F32) for source in range(4)]
        if plane == 0:
            term = [term[source] * (source >= y).astype(F32) for source in range(4)]
        if plane == 4:
            term = [term[source] * (source < y).astype(F32) for source in range(4)]
        acc = (term[0] + term[1] + term[2] + term[3]).astype(BF16)
        part_ref[plane] = acc
        parts += [nt(ku_ref[...], acc[0]), nt(vu_ref[...], acc[1])]
    parts = jnp.concatenate(parts, axis=0).astype(BF16)
    for peer in range(8):
        out_ref[peer, 0:32] = back_ref[...]
        out_ref[peer, 32:192] = parts


def down_kernel(
    low_ref, x_ref, one_ref, two_ref, four_ref, dout_ref, part_ref, sum_ref, tot_ref, out_ref
):
    low = low_ref[0].astype(F32)
    for peer in range(1, 8):
        low = low + low_ref[peer].astype(F32)
    low = low.astype(BF16)
    near = nn(low[16:64], x_ref[...])
    fars = (one_ref[...], two_ref[0], two_ref[1], four_ref[...])
    tiles = [near[0:16, t * 128 : (t + 1) * 128] for t in range(5)]
    down = []
    for t in range(5):
        acc = near[16:48, t * 128 : (t + 1) * 128]
        for p, far in enumerate(fars):
            acc = acc + nn(low[64 + 32 * p : 96 + 32 * p], far[t * 128 : (t + 1) * 128])
        down.append(acc)
    tiles += [acc[0:16] for acc in down] + [acc[16:32] for acc in down]
    up = nn(low[0:16], dout_ref[...])
    tiles += [up[:, t * 128 : (t + 1) * 128] for t in range(5)]
    tiles = [(ADAPTER_SCALE * tile).astype(BF16) for tile in tiles]
    tiles += [tot_ref[t] for t in range(16)]
    for which in range(2):
        rows = slice(16 * which, 16 * which + 16)
        acc = nn(sum_ref[16 + 16 * which : 32 + 16 * which], part_ref[0, which])
        for p, far in enumerate(fars):
            acc = acc + nn(far[640:672][rows], part_ref[p + 1, which])
        tiles.append((ADAPTER_SCALE * acc).astype(BF16))
    zero = jnp.zeros((16, 128), BF16)
    tiles += [zero, zero]
    for t, tile in enumerate(tiles):
        out_ref[t // 5, t % 5] = tile


def pass_two_kernel(part_ref, four_ref, out_ref):
    out_ref[0] = part_ref[2]
    out_ref[1] = (part_ref[3].astype(F32) + four_ref[...].astype(F32)).astype(BF16)


def pass_kernel(part_ref, two_ref, out_ref):
    out_ref[...] = (part_ref[1].astype(F32) + two_ref[1].astype(F32)).astype(BF16)


def owner_kernel(part_ref, one_ref, two_ref, dk_ref, dv_ref):
    for which, ref in enumerate((dk_ref, dv_ref)):
        acc = part_ref[0, which].astype(F32) + one_ref[which].astype(F32)
        ref[...] = (acc + two_ref[0, which].astype(F32)).astype(BF16)


def sum_spread_kernel(in_ref, out_ref):
    acc = in_ref[0].astype(F32)
    for peer in range(1, 8):
        acc = acc + in_ref[peer].astype(F32)
    acc = acc.astype(BF16)
    for peer in range(8):
        out_ref[peer] = acc


def unpack_kernel(in_ref, qd_ref, qu_ref, kd_ref, ku_ref, vd_ref, vu_ref, od_ref, ou_ref):
    def tile(t):
        return in_ref[t // 5, t % 5].astype(F32)

    for which, ref in enumerate((qd_ref, kd_ref, vd_ref, ou_ref)):
        for t in range(5):
            ref[:, t * 128 : (t + 1) * 128] = tile(which * 5 + t)
    for t in range(8):
        od_ref[:, t * 128 : (t + 1) * 128] = tile(20 + t)
        qu_ref[:, t * 128 : (t + 1) * 128] = tile(28 + t)
    ku_ref[...] = tile(36)
    vu_ref[...] = tile(37)


def shift(value, steps):
    count = lax.axis_size("ctx")
    first, last = max(0, -steps), min(count, count - steps)
    return lax.ppermute(value, "ctx", [(i, i + steps) for i in range(first, last)])


def exchange(value, groups):
    return lax.all_to_all(value, "ctx", 0, 0, tiled=True, axis_index_groups=groups)


def exchange_head(value):
    return lax.all_to_all(value, "head", 0, 0, tiled=True)


def after(value, *others):
    return lax.optimization_barrier((value, *others))[0]


def shards(x, q, keys, values, frozen, dout, lengths, qd, qu, kd, ku, vd, vu, od, ou):
    qd, kd, vd, od = qd.T, kd.T, vd.T, od.T
    wide = shaped((128, 1024), BF16)
    tall = shaped((1024, 128), BF16)
    block = shaped((2, 128, 128), BF16)
    pair = jnp.stack([keys, values])
    four = shift(pair, 16)
    one = shift(pair, 4)
    low = call(project_kernel, shaped((8, 64, 128), BF16), x, dout, qd, kd, vd, ou, vmem=60)
    low = exchange_head(after(low, one))
    two = shift(jnp.stack([pair, one]), 8)
    window, x_rows, low = call(
        spread_kernel,
        (shaped((4, 4, 2, 128, 128), BF16), shaped((672, 128), BF16), shaped((64, 128), BF16)),
        pair, one, two, four, low, x,
    )
    window = exchange(window, Y_GROUPS)
    x_one = shift(x_rows, 4)
    qs, qt, gs, gt = call(prepare_kernel, (tall, wide, tall, wide), q, frozen, low, od)
    x_two = shift(jnp.stack([x_rows, x_one]), 8)
    x_four = shift(x_two[1], 4)
    dqt, ot, dkv = call(
        attention_kernel,
        (wide, wide, shaped((4, 4, 2, 128, 128), BF16)),
        after(qs, x_one), qt, gs, gt, window, lengths.reshape(1, 128),
        scratch=[
            pltpu.VMEM((4, 512, 1024), F32),
            pltpu.VMEM((128, 1024), F32),
            pltpu.VMEM((128, 1024), F32),
            pltpu.VMEM((512, 128), F32),
            pltpu.VMEM((512, 128), F32),
            pltpu.VMEM((512, 128), F32),
            pltpu.VMEM((1, 1024), F32),
            pltpu.VMEM((1, 1024), F32),
            pltpu.VMEM((1, 1024), F32),
        ],
        vmem=24,
        flops=3 << 30,
    )
    dkv = exchange(after(dkv, x_two), Y_GROUPS)
    dq, back, totals = call(
        finish_kernel,
        (wide, shaped((32, 128), BF16), shaped((16, 16, 128), BF16)),
        dqt, ot, low, od, qu,
    )
    parts, low_back = call(
        gather_kernel,
        (shaped((5, 2, 128, 128), BF16), shaped((8, 192, 128), BF16)),
        dkv, back, ku, vu,
    )
    four_back = shift(parts[4], -4)
    low_back = exchange_head(after(low_back, x_four))
    packed = shaped((8, 5, 16, 128), BF16)
    sums = call(
        down_kernel, packed, low_back, x, x_one, x_two, x_four, dout, parts, low, totals
    )
    sums = after(exchange(sums, EIGHTS), four_back)
    sums = call(sum_spread_kernel, packed, sums)
    two_back = shift(call(pass_two_kernel, shaped((2, 2, 128, 128), BF16), parts, four_back), -8)
    sums = after(exchange(sums, STRIDED), two_back)
    sums = call(sum_spread_kernel, packed, sums)
    sums = exchange(sums, EIGHTS)
    one_back = shift(call(pass_kernel, block, parts, two_back), -4)
    dk, dv = call(
        owner_kernel,
        (shaped((128, 128), BF16), shaped((128, 128), BF16)),
        parts, one_back, two_back,
    )
    narrow, small = shaped((16, 640), F32), shaped((16, 128), F32)
    broad = shaped((16, 1024), F32)
    g_qd, g_qu, g_kd, g_ku, g_vd, g_vu, g_od, g_ou = call(
        unpack_kernel, (narrow, broad, narrow, small, narrow, small, broad, narrow), sums
    )
    return dq, dk, dv, g_qd.T, g_qu, g_kd.T, g_ku, g_vd.T, g_vu, g_od.T, g_ou


def solution(mesh):
    rows, cols, tokens = P("head", None), P(None, "head"), P("ctx", "head")
    return jax.shard_map(
        shards,
        mesh=mesh,
        in_specs=(tokens,) * 6 + (P(),) + (rows, cols) * 4,
        out_specs=(tokens,) * 3 + (rows, cols) * 4,
        check_vma=False,
    )
```

time: 167 us -> 156 us (0.934)
  the two profiles are of different devices: /device:TPU:2 before, /device:TPU:8 now
where the time goes in v2:
time: 156 us; the launch traced here: 155 us
  starting transfers between devices  90.9 us (58%)
  waiting for transfers between devices  34 us (22%)
  blocking collectives  13.4 us (9%)
  Pallas kernels  13.2 us (8%)
  local copies, waits for them, and re-layouts  2.35 us (2%)
    ppermute x9, starting transfers between devices, shift(): lax.ppermute(value, 'ctx', [(i, i + steps) for i in range(first, last)])  43.9 us
    all_to_all x5, starting transfers between devices, exchange(): lax.all_to_all(value, 'ctx', 0, 0, tiled=True, axis_index_groups=groups)  42.6 us
    ppermute x9, waiting for transfers between devices, shift(): lax.ppermute(value, 'ctx', [(i, i + steps) for i in range(first, last)])  29.9 us
    all_to_all x1, blocking collectives, exchange_head(): return lax.all_to_all(value, 'head', 0, 0, tiled=True)  13.4 us
    pallas_call x13, Pallas kernels, call(): pl.pallas_call(body, out_shape=outs, scratch_shapes=list(scratch), compil...  13.2 us
    all_to_all x1, starting transfers between devices, exchange_head(): return lax.all_to_all(value, 'head', 0, 0, tiled=True)  4.43 us
    all_to_all x5, waiting for transfers between devices, exchange(): lax.all_to_all(value, 'ctx', 0, 0, tiled=True, axis_index_groups=groups)  4.07 us
  transfers between devices with their start and end apart: 15, of which 9 were waited for; matrix products, arithmetic and copies ran while one was open for 0% of the time, Pallas kernels for 6%

profile of v2, /device:TPU:8, one launch (start us, length us, event | category | flops | bytes accessed | tf_op | source)
XLA Modules:
  0.0 155.4 jit_solution(6913018137485463850)
XLA Ops:
  0.6 0.8 fusion
  1.4 3.8 %collective-permute-start = (bf16[2,128,128]{2,1,0:T(8,128)(2,1)S(1)}, bf16[2,128,128]{2,1,0:T(8,128)(2,1)S(1)}, u32[]{:S(2)}, u32[]{:S(2)}) collective-permute-start(bf16[2,128,128]{2,1,0:T(8,128)(2,1)S(1)} %get-tuple-element.74.pair_ref), channel_id=1, source_target_pairs={{0,32},{8,40},{16,48},{24,56},{32,64},{40,72},{48,80},{56,88},{64,... | collective-permute-start | bytes 196616 | tf_op jit(solution)/shard_map/ppermute | solution.py:317
  5.3 1.9 %collective-permute-done.one_ref = bf16[2,128,128]{2,1,0:T(8,128)(2,1)S(1)} collective-permute-done((bf16[2,128,128]{2,1,0:T(8,128)(2,1)S(1)}, bf16[2,128,128]{2,1,0:T(8,128)(2,1)S(1)}, u32[]{:S(2)}, u32[]{:S(2)}) %collective-permute-start) | collective-permute-done | bytes 65568 | tf_op jit(solution)/shard_map/ppermute | solution.py:317
  7.2 5.6 %collective-permute-start.1 = (bf16[2,2,128,128]{3,2,1,0:T(8,128)(2,1)S(1)}, bf16[2,2,128,128]{3,2,1,0:T(8,128)(2,1)S(1)}, u32[]{:S(2)}, u32[]{:S(2)}) collective-permute-start(bf16[2,2,128,128]{3,2,1,0:T(8,128)(2,1)S(1)} %pad_maximum_fusion.1), channel_id=1, source_target_pairs={{0,64},{8,72},{16,80},{24,88},{32,96},{40,104},{48,112},{56,120},{... | collective-permute-start | bytes 393224 | tf_op jit(solution)/shard_map/ppermute | solution.py:317
  12.8 2.0 %shard_map.230 = bf16[8,64,128]{2,1,0:T(8,128)(2,1)} custom-call(bf16[128,640]{1,0:T(8,128)(2,1)} %x_ref.5, bf16[128,640]{1,0:T(8,128)(2,1)} %dout_ref.3, bf16[16,640]{1,0:T(8,128)(2,1)} %bitcast.28, bf16[16,640]{1,0:T(8,128)(2,1)} %bitcast.29, bf16[16,640]{1,0:T(8,128)(2,1)} %bitcast.30, bf16[16,640]{1,0:T(8,128)(2,1)} %ou_ref.1), custom_call_target="tpu_custom_call" | custom-call | flops 1048576 | bytes 1048576 | tf_op jit(solution)/shard_map/pallas_call | solution.py:40
  14.8 0.0 copy-start
  14.8 4.4 %all-to-all-start = ((bf16[8,64,128]{2,1,0:T(8,128)(2,1)}), bf16[8,64,128]{2,1,0:T(8,128)(2,1)S(1)}, u32[]{:S(2)}, u32[]{:S(2)}) async-start(bf16[8,64,128]{2,1,0:T(8,128)(2,1)} %shard_map.230), calls=%async_computation | async-start | bytes 262144 | tf_op jit(solution)/shard_map/all_to_all | solution.py:325
  19.2 9.1 %collective-permute-start.2 = (bf16[2,128,128]{2,1,0:T(8,128)(2,1)S(1)}, bf16[2,128,128]{2,1,0:T(8,128)(2,1)S(1)}, u32[]{:S(2)}, u32[]{:S(2)}) collective-permute-start(bf16[2,128,128]{2,1,0:T(8,128)(2,1)S(1)} %get-tuple-element.74.pair_ref), channel_id=1, source_target_pairs={{0,128},{8,136},{16,144},{24,152},{32,160},{40,168},{48,176},{56,1... | collective-permute-start | bytes 196616 | tf_op jit(solution)/shard_map/ppermute | solution.py:317
  28.3 2.0 %collective-permute-done.2.four_ref = bf16[2,128,128]{2,1,0:T(8,128)(2,1)S(1)} collective-permute-done((bf16[2,128,128]{2,1,0:T(8,128)(2,1)S(1)}, bf16[2,128,128]{2,1,0:T(8,128)(2,1)S(1)}, u32[]{:S(2)}, u32[]{:S(2)}) %collective-permute-start.2) | collective-permute-done | bytes 65568 | tf_op jit(solution)/shard_map/ppermute | solution.py:317
  30.3 0.0 all-to-all-done.low_ref
  30.3 0.0 collective-permute-done.1.two_ref
  30.3 0.0 copy-done
  30.3 1.1 shard_map.231
  31.5 4.9 %all-to-all-start.1 = ((bf16[4,4,2,128,128]{4,3,2,1,0:T(8,128)(2,1)}), bf16[4,4,2,128,128]{4,3,2,1,0:T(8,128)(2,1)S(1)}, u32[]{:S(2)}, u32[]{:S(2)}) async-start(bf16[4,4,2,128,128]{4,3,2,1,0:T(8,128)(2,1)} %get-tuple-element.50), calls=%async_computation.1 | async-start | bytes 2097152 | tf_op jit(solution)/shard_map/all_to_all | solution.py:321
  36.4 4.8 %collective-permute-start.3 = (bf16[672,128]{1,0:T(8,128)(2,1)S(1)}, bf16[672,128]{1,0:T(8,128)(2,1)S(1)}, u32[]{:S(2)}, u32[]{:S(2)}) collective-permute-start(bf16[672,128]{1,0:T(8,128)(2,1)S(1)} %get-tuple-element.45), channel_id=1, source_target_pairs={{0,32},{8,40},{16,48},{24,56},{32,64},{40,72},{48,80},{56,88},{64,... | collective-permute-start | bytes 516104 | tf_op jit(solution)/shard_map/ppermute | solution.py:317
  41.1 3.0 %collective-permute-done.3.one_ref = bf16[672,128]{1,0:T(8,128)(2,1)S(1)} collective-permute-done((bf16[672,128]{1,0:T(8,128)(2,1)S(1)}, bf16[672,128]{1,0:T(8,128)(2,1)S(1)}, u32[]{:S(2)}, u32[]{:S(2)}) %collective-permute-start.3) | collective-permute-done | bytes 172064 | tf_op jit(solution)/shard_map/ppermute | solution.py:317
  44.2 0.0 copy-start.2
  44.2 0.0 copy-start.3
  44.2 0.0 copy-start.4
  44.2 7.3 %collective-permute-start.4 = (bf16[2,672,128]{2,1,0:T(8,128)(2,1)S(1)}, bf16[2,672,128]{2,1,0:T(8,128)(2,1)S(1)}, u32[]{:S(2)}, u32[]{:S(2)}) collective-permute-start(bf16[2,672,128]{2,1,0:T(8,128)(2,1)S(1)} %pad_maximum_fusion), channel_id=1, source_target_pairs={{0,64},{8,72},{16,80},{24,88},{32,96},{40,104},{48,112},{56,120},{... | collective-permute-start | bytes 1032200 | tf_op jit(solution)/shard_map/ppermute | solution.py:317
  51.6 0.0 copy-done.2
  51.6 0.0 copy-done.3
  51.6 0.0 copy-done.4
  51.6 0.4 shard_map.232
  52.0 0.0 copy-start.8
  52.0 0.7 copy-done.8
  52.7 0.0 all-to-all-done.1.kv_ref
  52.7 0.0 copy-start.10
  52.7 0.7 copy-done.10
  53.3 0.0 copy-start.9
  53.3 0.9 copy-done.9
  54.3 4.4 %shard_map.233 = (bf16[128,1024]{1,0:T(8,128)(2,1)S(1)}, bf16[128,1024]{1,0:T(8,128)(2,1)S(1)}, bf16[4,4,2,128,128]{4,3,2,1,0:T(8,128)(2,1)}) custom-call(bf16[1024,128]{1,0:T(8,128)(2,1)S(1)} %get-tuple-element.46.qs, bf16[128,1024]{1,0:T(8,128)(2,1)S(1)} %get-tuple-element.47.qt, bf16[1024,128]{1,0:T(8,128)(2,1)S(1)} %get-tuple-element.48.gs, ...), custom_call_target="tpu_custom_call" | custom-call | flops 3221225472 | bytes 1048576 | tf_op jit(solution)/shard_map/pallas_call | solution.py:40
  58.7 0.0 collective-permute-done.4.two_ref
  58.7 4.8 %all-to-all-start.2 = ((bf16[4,4,2,128,128]{4,3,2,1,0:T(8,128)(2,1)}), bf16[4,4,2,128,128]{4,3,2,1,0:T(8,128)(2,1)S(1)}, u32[]{:S(2)}, u32[]{:S(2)}) async-start(bf16[4,4,2,128,128]{4,3,2,1,0:T(8,128)(2,1)} %get-tuple-element.55), calls=%async_computation.2 | async-start | bytes 2097152 | tf_op jit(solution)/shard_map/all_to_all | solution.py:321
  63.5 0.0 copy-start.5
  63.6 9.3 %collective-permute-start.8 = (bf16[672,128]{1,0:T(8,128)(2,1)S(1)}, bf16[672,128]{1,0:T(8,128)(2,1)S(1)}, u32[]{:S(2)}, u32[]{:S(2)}) collective-permute-start(bf16[672,128]{1,0:T(8,128)(2,1)S(1)} %slice_bitcast_fusion), channel_id=1, source_target_pairs={{0,32},{8,40},{16,48},{24,56},{32,64},{40,72},{48,80},{56,88},{64,... | collective-permute-start | bytes 516104 | tf_op jit(solution)/shard_map/ppermute | solution.py:317
  72.9 0.0 copy-done.5
  72.9 0.0 copy-start.6
  72.9 0.0 copy-start.7
  72.9 1.0 shard_map.234
  74.0 1.4 all-to-all-done.2.y_ref
  75.3 0.0 copy-done.6
  75.3 0.0 copy-done.7
  75.3 0.3 shard_map.235
  75.7 0.5 collective-permute-done.8.four_ref
  76.1 13.4 %all_to_all.35.low_ref = bf16[8,192,128]{2,1,0:T(8,128)(2,1)S(1)} all-to-all(bf16[8,192,128]{2,1,0:T(8,128)(2,1)S(1)} %get-tuple-element.61), channel_id=1, replica_groups=mesh['ctx'=64,'head'=8] {'head'}, dimensions={0} | all-to-all | bytes 786432 | tf_op jit(solution)/shard_map/all_to_all | solution.py:325
  89.5 0.0 copy-done.1
  89.5 1.1 shard_map.239
  90.6 12.4 %all-to-all-start.4 = ((bf16[8,5,16,128]{3,2,1,0:T(8,128)(2,1)}), bf16[8,5,16,128]{3,2,1,0:T(8,128)(2,1)S(1)}, u32[]{:S(2)}, u32[]{:S(2)}) async-start(bf16[8,5,16,128]{3,2,1,0:T(8,128)(2,1)} %shard_map.239), calls=%async_computation.4 | async-start | bytes 327680 | tf_op jit(solution)/shard_map/all_to_all | solution.py:321
  103.0 1.3 collective-permute-start.5
  104.3 4.9 %collective-permute-done.5.four_ref = bf16[2,128,128]{2,1,0:T(8,128)(2,1)S(1)} collective-permute-done((bf16[2,128,128]{2,1,0:T(8,128)(2,1)S(1)}, bf16[2,128,128]{2,1,0:T(8,128)(2,1)S(1)}, u32[]{:S(2)}, u32[]{:S(2)}) %collective-permute-start.5) | collective-permute-done | bytes 65568 | tf_op jit(solution)/shard_map/ppermute | solution.py:317
  109.2 0.0 all-to-all-done.4.in_ref
  109.2 0.7 shard_map.240
  109.8 14.4 %all-to-all-start.5 = ((bf16[8,5,16,128]{3,2,1,0:T(8,128)(2,1)}), bf16[8,5,16,128]{3,2,1,0:T(8,128)(2,1)S(1)}, u32[]{:S(2)}, u32[]{:S(2)}) async-start(bf16[8,5,16,128]{3,2,1,0:T(8,128)(2,1)} %shard_map.240), calls=%async_computation.5 | async-start | bytes 327680 | tf_op jit(solution)/shard_map/all_to_all | solution.py:321
  124.3 1.3 collective-permute-start.6
  125.6 12.8 %collective-permute-done.6.two_ref = bf16[2,2,128,128]{3,2,1,0:T(8,128)(2,1)S(1)} collective-permute-done((bf16[2,2,128,128]{3,2,1,0:T(8,128)(2,1)S(1)}, bf16[2,2,128,128]{3,2,1,0:T(8,128)(2,1)S(1)}, u32[]{:S(2)}, u32[]{:S(2)}) %collective-permute-start.6) | collective-permute-done | bytes 131104 | tf_op jit(solution)/shard_map/ppermute | solution.py:317
  138.3 2.7 %all-to-all-done.5.in_ref = bf16[8,5,16,128]{3,2,1,0:T(8,128)(2,1)S(1)} async-done(((bf16[8,5,16,128]{3,2,1,0:T(8,128)(2,1)}), bf16[8,5,16,128]{3,2,1,0:T(8,128)(2,1)S(1)}, u32[]{:S(2)}, u32[]{:S(2)}) %all-to-all-start.5) | async-done | bytes 163872 | tf_op jit(solution)/shard_map/all_to_all | solution.py:321
  141.0 0.7 shard_map.241
  141.7 6.2 %all-to-all-start.6 = ((bf16[8,5,16,128]{3,2,1,0:T(8,128)(2,1)}), bf16[8,5,16,128]{3,2,1,0:T(8,128)(2,1)S(1)}, u32[]{:S(2)}, u32[]{:S(2)}) async-start(bf16[8,5,16,128]{3,2,1,0:T(8,128)(2,1)} %shard_map.241), calls=%async_computation.6 | async-start | bytes 327680 | tf_op jit(solution)/shard_map/all_to_all | solution.py:321
  147.9 1.3 collective-permute-start.7
  149.2 4.9 %collective-permute-done.7.one_ref = bf16[2,128,128]{2,1,0:T(8,128)(2,1)S(1)} collective-permute-done((bf16[2,128,128]{2,1,0:T(8,128)(2,1)S(1)}, bf16[2,128,128]{2,1,0:T(8,128)(2,1)S(1)}, u32[]{:S(2)}, u32[]{:S(2)}) %collective-permute-start.7) | collective-permute-done | bytes 65568 | tf_op jit(solution)/shard_map/ppermute | solution.py:317
  154.0 0.6 shard_map.238
  154.7 0.0 all-to-all-done.6.in_ref
  154.7 0.7 shard_map.242
  (7 shorter events, 0.1 us)
Async XLA Ops:
  1.4 5.7 %collective-permute-start = (bf16[2,128,128]{2,1,0:T(8,128)(2,1)S(1)}, bf16[2,128,128]{2,1,0:T(8,128)(2,1)S(1)}, u32[]{:S(2)}, u32[]{:S(2)}) collective-permute-start(bf16[2,128,128]{2,1,0:T(8,128)(2,1)S(1)} %get-tuple-element.74.pair_ref), channel_id=1, source_target_pairs={{0,32},{8,40},{16,48},{24,56},{32,64},{40,72},{48,80},{56,88},{64,... | collective-permute-start | bytes 196616 | tf_op jit(solution)/shard_map/ppermute | solution.py:317
  7.2 23.2 %collective-permute-start.1 = (bf16[2,2,128,128]{3,2,1,0:T(8,128)(2,1)S(1)}, bf16[2,2,128,128]{3,2,1,0:T(8,128)(2,1)S(1)}, u32[]{:S(2)}, u32[]{:S(2)}) collective-permute-start(bf16[2,2,128,128]{3,2,1,0:T(8,128)(2,1)S(1)} %pad_maximum_fusion.1), channel_id=1, source_target_pairs={{0,64},{8,72},{16,80},{24,88},{32,96},{40,104},{48,112},{56,120},{... | collective-permute-start | bytes 393224 | tf_op jit(solution)/shard_map/ppermute | solution.py:317
  14.8 15.5 %copy-start = (bf16[128,640]{1,0:T(8,128)(2,1)S(1)}, bf16[128,640]{1,0:T(8,128)(2,1)}, u32[]{:S(2)}) copy-start(bf16[128,640]{1,0:T(8,128)(2,1)} %x_ref.5) | copy-start | bytes 491524
  14.8 15.5 %all-to-all-start = ((bf16[8,64,128]{2,1,0:T(8,128)(2,1)}), bf16[8,64,128]{2,1,0:T(8,128)(2,1)S(1)}, u32[]{:S(2)}, u32[]{:S(2)}) async-start(bf16[8,64,128]{2,1,0:T(8,128)(2,1)} %shard_map.230), calls=%async_computation | async-start | bytes 262144 | tf_op jit(solution)/shard_map/all_to_all | solution.py:325
  19.2 11.1 %collective-permute-start.2 = (bf16[2,128,128]{2,1,0:T(8,128)(2,1)S(1)}, bf16[2,128,128]{2,1,0:T(8,128)(2,1)S(1)}, u32[]{:S(2)}, u32[]{:S(2)}) collective-permute-start(bf16[2,128,128]{2,1,0:T(8,128)(2,1)S(1)} %get-tuple-element.74.pair_ref), channel_id=1, source_target_pairs={{0,128},{8,136},{16,144},{24,152},{32,160},{40,168},{48,176},{56,1... | collective-permute-start | bytes 196616 | tf_op jit(solution)/shard_map/ppermute | solution.py:317
  31.5 21.2 %all-to-all-start.1 = ((bf16[4,4,2,128,128]{4,3,2,1,0:T(8,128)(2,1)}), bf16[4,4,2,128,128]{4,3,2,1,0:T(8,128)(2,1)S(1)}, u32[]{:S(2)}, u32[]{:S(2)}) async-start(bf16[4,4,2,128,128]{4,3,2,1,0:T(8,128)(2,1)} %get-tuple-element.50), calls=%async_computation.1 | async-start | bytes 2097152 | tf_op jit(solution)/shard_map/all_to_all | solution.py:321
  36.4 7.8 %collective-permute-start.3 = (bf16[672,128]{1,0:T(8,128)(2,1)S(1)}, bf16[672,128]{1,0:T(8,128)(2,1)S(1)}, u32[]{:S(2)}, u32[]{:S(2)}) collective-permute-start(bf16[672,128]{1,0:T(8,128)(2,1)S(1)} %get-tuple-element.45), channel_id=1, source_target_pairs={{0,32},{8,40},{16,48},{24,56},{32,64},{40,72},{48,80},{56,88},{64,... | collective-permute-start | bytes 516104 | tf_op jit(solution)/shard_map/ppermute | solution.py:317
  44.2 7.4 %copy-start.2 = (bf16[128,1024]{1,0:T(8,128)(2,1)S(1)}, bf16[128,1024]{1,0:T(8,128)(2,1)}, u32[]{:S(2)}) copy-start(bf16[128,1024]{1,0:T(8,128)(2,1)} %q_ref.1) | copy-start | bytes 786436
  44.2 7.4 %copy-start.3 = (bf16[128,1024]{1,0:T(8,128)(2,1)S(1)}, bf16[128,1024]{1,0:T(8,128)(2,1)}, u32[]{:S(2)}) copy-start(bf16[128,1024]{1,0:T(8,128)(2,1)} %f_ref.1) | copy-start | bytes 786436
  44.2 7.4 %copy-start.4 = (bf16[1024,16]{0,1:T(8,128)(2,1)S(1)}, bf16[1024,16]{0,1:T(8,128)(2,1)}, u32[]{:S(2)}) copy-start(bf16[1024,16]{0,1:T(8,128)(2,1)} %param.28) | copy-start | bytes 98308
  44.2 14.5 %collective-permute-start.4 = (bf16[2,672,128]{2,1,0:T(8,128)(2,1)S(1)}, bf16[2,672,128]{2,1,0:T(8,128)(2,1)S(1)}, u32[]{:S(2)}, u32[]{:S(2)}) collective-permute-start(bf16[2,672,128]{2,1,0:T(8,128)(2,1)S(1)} %pad_maximum_fusion), channel_id=1, source_target_pairs={{0,64},{8,72},{16,80},{24,88},{32,96},{40,104},{48,112},{56,120},{... | collective-permute-start | bytes 1032200 | tf_op jit(solution)/shard_map/ppermute | solution.py:317
  52.0 0.7 copy-start.8
  52.7 0.7 copy-start.10
  53.3 0.9 copy-start.9
  58.7 16.6 %all-to-all-start.2 = ((bf16[4,4,2,128,128]{4,3,2,1,0:T(8,128)(2,1)}), bf16[4,4,2,128,128]{4,3,2,1,0:T(8,128)(2,1)S(1)}, u32[]{:S(2)}, u32[]{:S(2)}) async-start(bf16[4,4,2,128,128]{4,3,2,1,0:T(8,128)(2,1)} %get-tuple-element.55), calls=%async_computation.2 | async-start | bytes 2097152 | tf_op jit(solution)/shard_map/all_to_all | solution.py:321
  63.5 9.4 %copy-start.5 = (bf16[16,1024]{1,0:T(8,128)(2,1)S(1)}, bf16[16,1024]{1,0:T(8,128)(2,1)}, u32[]{:S(2)}) copy-start(bf16[16,1024]{1,0:T(8,128)(2,1)} %qu_ref.1) | copy-start | bytes 98308
  63.6 12.6 %collective-permute-start.8 = (bf16[672,128]{1,0:T(8,128)(2,1)S(1)}, bf16[672,128]{1,0:T(8,128)(2,1)S(1)}, u32[]{:S(2)}, u32[]{:S(2)}) collective-permute-start(bf16[672,128]{1,0:T(8,128)(2,1)S(1)} %slice_bitcast_fusion), channel_id=1, source_target_pairs={{0,32},{8,40},{16,48},{24,56},{32,64},{40,72},{48,80},{56,88},{64,... | collective-permute-start | bytes 516104 | tf_op jit(solution)/shard_map/ppermute | solution.py:317
  72.9 2.4 %copy-start.6 = (bf16[16,128]{1,0:T(8,128)(2,1)S(1)}, bf16[16,128]{1,0:T(8,128)(2,1)}, u32[]{:S(2)}) copy-start(bf16[16,128]{1,0:T(8,128)(2,1)} %ku_ref.1) | copy-start | bytes 12292
  72.9 2.4 %copy-start.7 = (bf16[16,128]{1,0:T(8,128)(2,1)S(1)}, bf16[16,128]{1,0:T(8,128)(2,1)}, u32[]{:S(2)}) copy-start(bf16[16,128]{1,0:T(8,128)(2,1)} %vu_ref.1) | copy-start | bytes 12292
  76.1 13.4 %copy-start.1 = (bf16[128,640]{1,0:T(8,128)(2,1)S(1)}, bf16[128,640]{1,0:T(8,128)(2,1)}, u32[]{:S(2)}) copy-start(bf16[128,640]{1,0:T(8,128)(2,1)} %dout_ref.3) | copy-start | bytes 491524
  90.6 18.5 %all-to-all-start.4 = ((bf16[8,5,16,128]{3,2,1,0:T(8,128)(2,1)}), bf16[8,5,16,128]{3,2,1,0:T(8,128)(2,1)S(1)}, u32[]{:S(2)}, u32[]{:S(2)}) async-start(bf16[8,5,16,128]{3,2,1,0:T(8,128)(2,1)} %shard_map.239), calls=%async_computation.4 | async-start | bytes 327680 | tf_op jit(solution)/shard_map/all_to_all | solution.py:321
  103.0 6.2 %collective-permute-start.5 = (bf16[2,128,128]{2,1,0:T(8,128)(2,1)S(1)}, bf16[2,128,128]{2,1,0:T(8,128)(2,1)S(1)}, u32[]{:S(2)}, u32[]{:S(2)}) collective-permute-start(bf16[2,128,128]{2,1,0:T(8,128)(2,1)S(1)} %slice_bitcast_fusion.1), channel_id=1, source_target_pairs={{32,0},{40,8},{48,16},{56,24},{64,32},{72,40},{80,48},{88,56},{96,... | collective-permute-start | bytes 196616 | tf_op jit(solution)/shard_map/ppermute | solution.py:317
  109.8 31.2 %all-to-all-start.5 = ((bf16[8,5,16,128]{3,2,1,0:T(8,128)(2,1)}), bf16[8,5,16,128]{3,2,1,0:T(8,128)(2,1)S(1)}, u32[]{:S(2)}, u32[]{:S(2)}) async-start(bf16[8,5,16,128]{3,2,1,0:T(8,128)(2,1)} %shard_map.240), calls=%async_computation.5 | async-start | bytes 327680 | tf_op jit(solution)/shard_map/all_to_all | solution.py:321
  124.3 14.1 %collective-permute-start.6 = (bf16[2,2,128,128]{3,2,1,0:T(8,128)(2,1)S(1)}, bf16[2,2,128,128]{3,2,1,0:T(8,128)(2,1)S(1)}, u32[]{:S(2)}, u32[]{:S(2)}) collective-permute-start(bf16[2,2,128,128]{3,2,1,0:T(8,128)(2,1)S(1)} %shard_map.236), channel_id=1, source_target_pairs={{64,0},{72,8},{80,16},{88,24},{96,32},{104,40},{112,48},{120,56},{... | collective-permute-start | bytes 393224 | tf_op jit(solution)/shard_map/ppermute | solution.py:317
  141.7 13.0 %all-to-all-start.6 = ((bf16[8,5,16,128]{3,2,1,0:T(8,128)(2,1)}), bf16[8,5,16,128]{3,2,1,0:T(8,128)(2,1)S(1)}, u32[]{:S(2)}, u32[]{:S(2)}) async-start(bf16[8,5,16,128]{3,2,1,0:T(8,128)(2,1)} %shard_map.241), calls=%async_computation.6 | async-start | bytes 327680 | tf_op jit(solution)/shard_map/all_to_all | solution.py:321
  147.9 6.2 %collective-permute-start.7 = (bf16[2,128,128]{2,1,0:T(8,128)(2,1)S(1)}, bf16[2,128,128]{2,1,0:T(8,128)(2,1)S(1)}, u32[]{:S(2)}, u32[]{:S(2)}) collective-permute-start(bf16[2,128,128]{2,1,0:T(8,128)(2,1)S(1)} %shard_map.237), channel_id=1, source_target_pairs={{32,0},{40,8},{48,16},{56,24},{64,32},{72,40},{80,48},{88,56},{96,... | collective-permute-start | bytes 196616 | tf_op jit(solution)/shard_map/ppermute | solution.py:317

commit v3 on v2

v3 whole, which is shorter than its diff:
```python
import functools

import jax
import jax.numpy as jnp
from jax import lax
from jax.experimental import pallas as pl
from jax.experimental.pallas import tpu as pltpu
from jax.sharding import PartitionSpec as P

HEAD = 128
ROWS = 128
GROUP = 8
RANK = 16
TILES = 40
SCALE = HEAD**-0.5
LOG2E = 1.4426950408889634
ADAPTER_SCALE = 2.0
NEG = -1e30
F32 = jnp.float32
BF16 = jnp.bfloat16

Y_GROUPS = [[4 * z + y for y in range(4)] for z in range(16)]
EIGHTS = [[8 * g + i for i in range(8)] for g in range(8)]
STRIDED = [[g + 8 * i for i in range(8)] for g in range(8)]


def nn(a, b):
    return lax.dot_general(a, b, (((1,), (0,)), ((), ())), preferred_element_type=F32)


def nt(a, b):
    return lax.dot_general(a, b, (((1,), (1,)), ((), ())), preferred_element_type=F32)


def tn(a, b):
    return lax.dot_general(a, b, (((0,), (0,)), ((), ())), preferred_element_type=F32)


def call(body, outs, *args, scratch=(), vmem=32, flops=1 << 20):
    return pl.pallas_call(
        body,
        out_shape=outs,
        scratch_shapes=list(scratch),
        compiler_params=pltpu.CompilerParams(vmem_limit_bytes=vmem << 20),
        cost_estimate=pl.CostEstimate(flops=flops, bytes_accessed=1 << 20, transcendentals=0),
    )(*args)


def shaped(shape, dtype):
    return jax.ShapeDtypeStruct(shape, dtype)


def project_kernel(x_ref, dout_ref, qd_ref, kd_ref, vd_ref, ou_ref, out_ref):
    parts = [nt(ref[...], x_ref[...]) for ref in (qd_ref, kd_ref, vd_ref)]
    parts.append(nt(ou_ref[...], dout_ref[...]))
    low = jnp.concatenate(parts, axis=0).astype(BF16)
    for peer in range(8):
        out_ref[peer] = low


def spread_kernel(
    pair_ref, one_ref, two_ref, back_ref, low_ref, x_ref, out_ref, x_out, sum_ref
):
    y = lax.axis_index("ctx") % 4
    for dest in range(4):

        @pl.when(dest >= y)
        def _(dest=dest):
            out_ref[dest, 0] = pair_ref[...]

        @pl.when(dest < y)
        def _(dest=dest):
            out_ref[dest, 0] = back_ref[1]

        out_ref[dest, 1] = one_ref[...]
        out_ref[dest, 2] = two_ref[...]
        out_ref[dest, 3] = back_ref[0]
    low = low_ref[0].astype(F32)
    for peer in range(1, 8):
        low = low + low_ref[peer].astype(F32)
    low = low.astype(BF16)
    sum_ref[...] = low
    for t in range(5):
        x_out[t * 128 : (t + 1) * 128, :] = x_ref[:, t * 128 : (t + 1) * 128]
    x_out[640:672, :] = low[16:48]


def prepare_kernel(
    q_ref, f_ref, low_ref, od_ref, len_ref, qs_ref, qt_ref, gs_ref, gt_ref, start_ref
):
    doc = lax.broadcasted_iota(jnp.int32, (128, 128), 0)
    lane = lax.broadcasted_iota(jnp.int32, (128, 128), 1)
    lengths = jnp.broadcast_to(len_ref[...].astype(F32), (128, 128))
    ends = jnp.sum(jnp.where(lane <= doc, lengths, 0.0), axis=1, keepdims=True)
    position = (lane + lax.axis_index("ctx") * ROWS).astype(F32)
    start = jnp.max(jnp.where(ends <= position, ends, 0.0), axis=0, keepdims=True)
    start_ref[...] = jnp.broadcast_to(start, (8, 128))
    u = low_ref[48:64]
    for n in range(GROUP):
        cols = slice(n * HEAD, (n + 1) * HEAD)
        q_n = q_ref[:, cols]
        qs_ref[cols, :] = q_n
        qt_ref[:, cols] = q_n.T
        g_n = f_ref[:, cols].astype(F32) + ADAPTER_SCALE * tn(u, od_ref[:, cols])
        g_n = g_n.astype(BF16)
        gs_ref[cols, :] = g_n
        gt_ref[:, cols] = g_n.T


def attention_kernel(
    qs, qt, gs, gt, kv_ref, start_ref,
    dqt_ref, ot_ref, dkv_ref,
    s_ref, ot, dqt, ds, low_prob, bias, top, total, delta,
):
    index = lax.axis_index("ctx")
    y_place = index % 4
    start = start_ref[0:1]
    start = start.astype(jnp.int32)
    q_pos = lax.broadcasted_iota(jnp.int32, (1, 128), 1) + index * ROWS
    top[...] = jnp.full_like(top, NEG)
    total[...] = jnp.zeros_like(total)
    ot[...] = jnp.zeros_like(ot)
    dqt[...] = jnp.zeros_like(dqt)

    def keys(plane, which):
        return kv_ref[:, plane, which].reshape(512, HEAD)

    for plane in range(4):
        for y in range(4):
            back = (4 * plane + y_place - y) & 15
            k_pos = lax.broadcasted_iota(jnp.int32, (128, 128), 0) + (index - back) * ROWS
            bias[y * 128 : (y + 1) * 128, :] = jnp.where(
                (k_pos >= start) & (k_pos <= q_pos), 0.0, NEG
            )
        raw = nn(keys(plane, 0), qt[...])
        raw = raw * (SCALE * LOG2E) + jnp.concatenate([bias[...]] * GROUP, axis=1)
        s_ref[plane] = raw
        top[...] = jnp.maximum(top[...], jnp.max(raw, axis=0, keepdims=True))
    for plane in range(4):
        prob = jnp.exp2(s_ref[plane] - top[...])
        s_ref[plane] = prob
        total[...] += jnp.sum(prob, axis=0, keepdims=True)
        ot[...] += nn(keys(plane, 1).T, prob.astype(BF16))
    total[...] = 1.0 / total[...]
    for n in range(GROUP):
        cols = slice(n * HEAD, (n + 1) * HEAD)
        o_n = (ot[:, cols] * total[:, cols]).astype(BF16)
        ot_ref[:, cols] = o_n
        delta[:, cols] = jnp.sum(
            o_n.astype(F32) * gt[:, cols].astype(F32), axis=0, keepdims=True
        )
    for plane in range(4):
        prob = s_ref[plane] * total[...]
        grad_prob = nn(keys(plane, 1), gt[...])
        grad_score = (prob * (grad_prob - delta[...])).astype(BF16)
        ds[...] = grad_score
        low_prob[...] = prob.astype(BF16)
        dqt[...] += nn(keys(plane, 0).T, grad_score)
        dk = (nn(ds[...], qs[...]) * SCALE).astype(BF16)
        dv = nn(low_prob[...], gs[...]).astype(BF16)
        dkv_ref[:, plane, 0] = dk.reshape(4, 128, HEAD)
        dkv_ref[:, plane, 1] = dv.reshape(4, 128, HEAD)
    dqt_ref[...] = (dqt[...] * SCALE).astype(BF16)


def finish_kernel(dqt_ref, ot_ref, low_ref, od_ref, qu_ref, dq_ref, back_ref, tot_ref):
    xa_q = low_ref[0:16]
    u = low_ref[48:64]
    out_adapter = jnp.zeros((RANK, ROWS), F32)
    back_q = jnp.zeros((RANK, ROWS), F32)
    for n in range(GROUP):
        cols = slice(n * HEAD, (n + 1) * HEAD)
        dq_t = dqt_ref[:, cols]
        dq_n = dq_t.T
        dq_ref[:, cols] = dq_n
        back_q = back_q + nn(qu_ref[:, cols], dq_t)
        tot_ref[GROUP + n] = (ADAPTER_SCALE * nn(xa_q, dq_n)).astype(BF16)
        o_n = ot_ref[:, cols]
        out_adapter = out_adapter + nn(od_ref[:, cols], o_n)
        tot_ref[n] = (ADAPTER_SCALE * nt(u, o_n)).astype(BF16)
    back_ref[0:16] = out_adapter.astype(BF16)
    back_ref[16:32] = back_q.astype(BF16)


def gather_kernel(y_ref, back_ref, ku_ref, vu_ref, part_ref, send_ref, out_ref):
    y = lax.axis_index("ctx") % 4
    parts = []
    for plane in range(5):
        term = [y_ref[source, plane % 4].astype(F32) for source in range(4)]
        if plane == 0:
            term = [term[source] * (source >= y).astype(F32) for source in range(4)]
        if plane == 4:
            term = [term[source] * (source < y).astype(F32) for source in range(4)]
        acc = (term[0] + term[1] + term[2] + term[3]).astype(BF16)
        part_ref[plane] = acc
        if plane in (2, 4):
            send_ref[plane // 2 - 1] = acc
        parts += [nt(ku_ref[...], acc[0]), nt(vu_ref[...], acc[1])]
    parts = jnp.concatenate(parts, axis=0).astype(BF16)
    for peer in range(8):
        out_ref[peer, 0:32] = back_ref[...]
        out_ref[peer, 32:192] = parts


def down_kernel(
    low_ref, x_ref, one_ref, two_ref, three_ref, four_ref, dout_ref, part_ref, sum_ref, tot_ref, out_ref
):
    low = low_ref[0].astype(F32)
    for peer in range(1, 8):
        low = low + low_ref[peer].astype(F32)
    low = low.astype(BF16)
    near = nn(low[16:64], x_ref[...])
    fars = (one_ref, two_ref, three_ref, four_ref)
    tiles = [near[0:16, t * 128 : (t + 1) * 128] for t in range(5)]
    down = []
    for t in range(5):
        acc = near[16:48, t * 128 : (t + 1) * 128]
        for p, far in enumerate(fars):
            acc = acc + nn(low[64 + 32 * p : 96 + 32 * p], far[t * 128 : (t + 1) * 128])
        down.append(acc)
    tiles += [acc[0:16] for acc in down] + [acc[16:32] for acc in down]
    up = nn(low[0:16], dout_ref[...])
    tiles += [up[:, t * 128 : (t + 1) * 128] for t in range(5)]
    tiles = [(ADAPTER_SCALE * tile).astype(BF16) for tile in tiles]
    tiles += [tot_ref[t] for t in range(16)]
    for which in range(2):
        rows = slice(16 * which, 16 * which + 16)
        acc = nn(sum_ref[16 + 16 * which : 32 + 16 * which], part_ref[0, which])
        for p, far in enumerate(fars):
            acc = acc + nn(far[640 + rows.start : 640 + rows.stop], part_ref[p + 1, which])
        tiles.append((ADAPTER_SCALE * acc).astype(BF16))
    zero = jnp.zeros((16, 128), BF16)
    tiles += [zero, zero]
    for t, tile in enumerate(tiles):
        out_ref[t // 5, t % 5] = tile


def pass_kernel(part_ref, near_ref, one_ref, three_ref):
    one_ref[...] = (part_ref[1].astype(F32) + near_ref[0].astype(F32)).astype(BF16)
    three_ref[...] = (part_ref[3].astype(F32) + near_ref[1].astype(F32)).astype(BF16)


def owner_kernel(part_ref, one_ref, three_ref, dk_ref, dv_ref):
    for which, ref in enumerate((dk_ref, dv_ref)):
        acc = part_ref[0, which].astype(F32) + one_ref[which].astype(F32)
        ref[...] = (acc + three_ref[which].astype(F32)).astype(BF16)


def sum_spread_kernel(in_ref, out_ref):
    acc = in_ref[0].astype(F32)
    for peer in range(1, 8):
        acc = acc + in_ref[peer].astype(F32)
    acc = acc.astype(BF16)
    for peer in range(8):
        out_ref[peer] = acc


def unpack_kernel(in_ref, qd_ref, qu_ref, kd_ref, ku_ref, vd_ref, vu_ref, od_ref, ou_ref):
    def tile(t):
        return in_ref[t // 5, t % 5].astype(F32)

    for which, ref in enumerate((qd_ref, kd_ref, vd_ref, ou_ref)):
        for t in range(5):
            ref[:, t * 128 : (t + 1) * 128] = tile(which * 5 + t)
    for t in range(8):
        od_ref[:, t * 128 : (t + 1) * 128] = tile(20 + t)
        qu_ref[:, t * 128 : (t + 1) * 128] = tile(28 + t)
    ku_ref[...] = tile(36)
    vu_ref[...] = tile(37)


def shift(value, steps):
    count = lax.axis_size("ctx")
    first, last = max(0, -steps), min(count, count - steps)
    return lax.ppermute(value, "ctx", [(i, i + steps) for i in range(first, last)])


def exchange(value, groups):
    return lax.all_to_all(value, "ctx", 0, 0, tiled=True, axis_index_groups=groups)


def exchange_head(value):
    return lax.all_to_all(value, "head", 0, 0, tiled=True)


def after(value, *others):
    return lax.optimization_barrier((value, *others))[0]


def shards(x, q, keys, values, frozen, dout, lengths, qd, qu, kd, ku, vd, vu, od, ou):
    qd, kd, vd, od = qd.T, kd.T, vd.T, od.T
    wide = shaped((128, 1024), BF16)
    tall = shaped((1024, 128), BF16)
    block = shaped((2, 128, 128), BF16)
    pair = jnp.stack([keys, values])
    one = shift(pair, 4)
    low = call(project_kernel, shaped((8, 64, 128), BF16), x, dout, qd, kd, vd, ou)
    low = exchange_head(after(low, one))
    two, back = shift(one, 4), shift(jnp.stack([pair, one]), 12)
    window, x_rows, low = call(
        spread_kernel,
        (shaped((4, 4, 2, 128, 128), BF16), shaped((672, 128), BF16), shaped((64, 128), BF16)),
        pair, one, two, back, low, x,
    )
    window = exchange(window, Y_GROUPS)
    x_one = shift(x_rows, 4)
    x_two = shift(x_rows, 8)
    x_three, x_four = shift(x_two, 4), shift(x_two, 8)
    qs, qt, gs, gt, starts = call(
        prepare_kernel,
        (tall, wide, tall, wide, shaped((8, 128), F32)),
        q, frozen, low, od, lengths.reshape(1, 128),
    )
    dqt, ot, dkv = call(
        attention_kernel,
        (wide, wide, shaped((4, 4, 2, 128, 128), BF16)),
        qs, qt, gs, gt, window, starts,
        scratch=[
            pltpu.VMEM((4, 512, 1024), F32),
            pltpu.VMEM((128, 1024), F32),
            pltpu.VMEM((128, 1024), F32),
            pltpu.VMEM((512, 1024), BF16),
            pltpu.VMEM((512, 1024), BF16),
            pltpu.VMEM((512, 128), F32),
            pltpu.VMEM((1, 1024), F32),
            pltpu.VMEM((1, 1024), F32),
            pltpu.VMEM((1, 1024), F32),
        ],
        vmem=40,
        flops=3 << 30,
    )
    dkv = exchange(after(dkv, x_one, x_two), Y_GROUPS)
    dq, back, totals = call(
        finish_kernel,
        (wide, shaped((32, 128), BF16), shaped((16, 16, 128), BF16)),
        dqt, ot, low, od, qu,
    )
    parts, near, low_back = call(
        gather_kernel,
        (
            shaped((5, 2, 128, 128), BF16),
            shaped((2, 2, 128, 128), BF16),
            shaped((8, 192, 128), BF16),
        ),
        dkv, back, ku, vu,
    )
    near = shift(near, -4)
    low_back = exchange_head(after(low_back, x_three, x_four))
    low_back = after(low_back, near)
    packed = shaped((8, 5, 16, 128), BF16)
    sums = call(
        down_kernel, packed, low_back, x, x_one, x_two, x_three, x_four, dout, parts, low, totals
    )
    sums = call(sum_spread_kernel, packed, exchange(sums, EIGHTS))
    one_back, three_back = call(pass_kernel, (block, block), parts, near)
    one_back, three_back = shift(one_back, -4), shift(three_back, -12)
    sums = after(exchange(sums, STRIDED), one_back, three_back)
    sums = call(sum_spread_kernel, packed, sums)
    sums = exchange(sums, EIGHTS)
    dk, dv = call(
        owner_kernel,
        (shaped((128, 128), BF16), shaped((128, 128), BF16)),
        parts, one_back, three_back,
    )
    narrow, small = shaped((16, 640), F32), shaped((16, 128), F32)
    broad = shaped((16, 1024), F32)
    g_qd, g_qu, g_kd, g_ku, g_vd, g_vu, g_od, g_ou = call(
        unpack_kernel, (narrow, broad, narrow, small, narrow, small, broad, narrow), sums
    )
    return dq, dk, dv, g_qd.T, g_qu, g_kd.T, g_ku, g_vd.T, g_vu, g_od.T, g_ou


def solution(mesh):
    rows, cols, tokens = P("head", None), P(None, "head"), P("ctx", "head")
    return jax.shard_map(
        shards,
        mesh=mesh,
        in_specs=(tokens,) * 6 + (P(),) + (rows, cols) * 4,
        out_specs=(tokens,) * 3 + (rows, cols) * 4,
        check_vma=False,
    )
```

time: 156 us -> 144 us (0.923)
  the two profiles are of different devices: /device:TPU:8 before, /device:TPU:2 now
where the time goes in v3:
time: 144 us; the launch traced here: 143 us
  starting transfers between devices  72.8 us (51%)
  waiting for transfers between devices  38 us (26%)
  Pallas kernels  16.5 us (11%)
  blocking collectives  13.1 us (9%)
    ppermute x10, starting transfers between devices, shift(): lax.ppermute(value, 'ctx', [(i, i + steps) for i in range(first, last)])  38.3 us
    all_to_all x4, starting transfers between devices, exchange(): lax.all_to_all(value, 'ctx', 0, 0, tiled=True, axis_index_groups=groups)  24.8 us
    ppermute x10, waiting for transfers between devices, shift(): lax.ppermute(value, 'ctx', [(i, i + steps) for i in range(first, last)])  22.3 us
    pallas_call x12, Pallas kernels, call(): pl.pallas_call(body, out_shape=outs, scratch_shapes=list(scratch), compil...  16.5 us
    all_to_all x4, waiting for transfers between devices, exchange(): lax.all_to_all(value, 'ctx', 0, 0, tiled=True, axis_index_groups=groups)  15.7 us
    all_to_all x1, blocking collectives, exchange(): lax.all_to_all(value, 'ctx', 0, 0, tiled=True, axis_index_groups=groups)  13.1 us
    all_to_all x2, starting transfers between devices, exchange_head(): return lax.all_to_all(value, 'head', 0, 0, tiled=True)  9.64 us
  transfers between devices with their start and end apart: 16, of which 9 were waited for; matrix products, arithmetic and copies ran while one was open for 0% of the time, Pallas kernels for 9%

profile of v3, /device:TPU:2, one launch (start us, length us, event | category | flops | bytes accessed | tf_op | source)
XLA Modules:
  0.0 142.7 jit_solution(1678327188427821758)
XLA Ops:
  0.6 0.0 copy-start.1
  0.7 0.8 fusion
  1.5 0.0 copy-start
  1.5 4.0 %collective-permute-start = (bf16[2,128,128]{2,1,0:T(8,128)(2,1)S(1)}, bf16[2,128,128]{2,1,0:T(8,128)(2,1)S(1)}, u32[]{:S(2)}, u32[]{:S(2)}) collective-permute-start(bf16[2,128,128]{2,1,0:T(8,128)(2,1)S(1)} %get-tuple-element.80.pair_ref), channel_id=1, source_target_pairs={{0,32},{8,40},{16,48},{24,56},{32,64},{40,72},{48,80},{56,88},{64,... | collective-permute-start | bytes 196616 | tf_op jit(solution)/shard_map/ppermute | solution.py:275
  5.5 1.9 %collective-permute-done.one_ref = bf16[2,128,128]{2,1,0:T(8,128)(2,1)S(1)} collective-permute-done((bf16[2,128,128]{2,1,0:T(8,128)(2,1)S(1)}, bf16[2,128,128]{2,1,0:T(8,128)(2,1)S(1)}, u32[]{:S(2)}, u32[]{:S(2)}) %collective-permute-start) | collective-permute-done | bytes 65568 | tf_op jit(solution)/shard_map/ppermute | solution.py:275
  7.3 0.0 copy-start.6
  7.4 7.9 %collective-permute-start.2 = (bf16[2,2,128,128]{3,2,1,0:T(8,128)(2,1)S(1)}, bf16[2,2,128,128]{3,2,1,0:T(8,128)(2,1)S(1)}, u32[]{:S(2)}, u32[]{:S(2)}) collective-permute-start(bf16[2,2,128,128]{3,2,1,0:T(8,128)(2,1)S(1)} %pad_maximum_fusion), channel_id=1, source_target_pairs={{0,96},{8,104},{16,112},{24,120},{32,128},{40,136},{48,144},{56,15... | collective-permute-start | bytes 393224 | tf_op jit(solution)/shard_map/ppermute | solution.py:275
  15.3 0.0 copy-done.1
  15.3 0.0 copy-done
  15.3 0.0 copy-done.6
  15.3 0.0 copy-done.7
  15.3 0.0 copy-done.8
  15.3 0.0 copy-done.9
  15.3 1.0 shard_map.230
  16.3 4.8 %all-to-all-start = ((bf16[8,64,128]{2,1,0:T(8,128)(2,1)}), bf16[8,64,128]{2,1,0:T(8,128)(2,1)S(1)}, u32[]{:S(2)}, u32[]{:S(2)}) async-start(bf16[8,64,128]{2,1,0:T(8,128)(2,1)} %shard_map.230), calls=%async_computation | async-start | bytes 262144 | tf_op jit(solution)/shard_map/all_to_all | solution.py:283
  21.1 5.5 %collective-permute-start.1 = (bf16[2,128,128]{2,1,0:T(8,128)(2,1)S(1)}, bf16[2,128,128]{2,1,0:T(8,128)(2,1)S(1)}, u32[]{:S(2)}, u32[]{:S(2)}) collective-permute-start(bf16[2,128,128]{2,1,0:T(8,128)(2,1)S(1)} %collective-permute-done.one_ref), channel_id=1, source_target_pairs={{0,32},{8,40},{16,48},{24,56},{32,64},{40,72},{48,80},{56,88},{64,... | collective-permute-start | bytes 196616 | tf_op jit(solution)/shard_map/ppermute | solution.py:275
  26.6 1.9 %collective-permute-done.1.two_ref = bf16[2,128,128]{2,1,0:T(8,128)(2,1)S(1)} collective-permute-done((bf16[2,128,128]{2,1,0:T(8,128)(2,1)S(1)}, bf16[2,128,128]{2,1,0:T(8,128)(2,1)S(1)}, u32[]{:S(2)}, u32[]{:S(2)}) %collective-permute-start.1) | collective-permute-done | bytes 65568 | tf_op jit(solution)/shard_map/ppermute | solution.py:275
  28.5 0.0 all-to-all-done.low_ref
  28.5 0.0 collective-permute-done.2.back_ref
  28.5 1.1 shard_map.231
  29.6 4.6 %all-to-all-start.1 = ((bf16[4,4,2,128,128]{4,3,2,1,0:T(8,128)(2,1)}), bf16[4,4,2,128,128]{4,3,2,1,0:T(8,128)(2,1)S(1)}, u32[]{:S(2)}, u32[]{:S(2)}) async-start(bf16[4,4,2,128,128]{4,3,2,1,0:T(8,128)(2,1)} %get-tuple-element.51), calls=%async_computation.1 | async-start | bytes 2097152 | tf_op jit(solution)/shard_map/all_to_all | solution.py:279
  34.2 4.4 %collective-permute-start.4 = (bf16[672,128]{1,0:T(8,128)(2,1)}, bf16[672,128]{1,0:T(8,128)(2,1)S(1)}, u32[]{:S(2)}, u32[]{:S(2)}) collective-permute-start(bf16[672,128]{1,0:T(8,128)(2,1)} %get-tuple-element.57), channel_id=1, source_target_pairs={{0,64},{8,72},{16,80},{24,88},{32,96},{40,104},{48,112},{56,120},{... | collective-permute-start | bytes 516104 | tf_op jit(solution)/shard_map/ppermute | solution.py:275
  38.7 4.1 %collective-permute-start.3 = (bf16[672,128]{1,0:T(8,128)(2,1)}, bf16[672,128]{1,0:T(8,128)(2,1)S(1)}, u32[]{:S(2)}, u32[]{:S(2)}) collective-permute-start(bf16[672,128]{1,0:T(8,128)(2,1)} %get-tuple-element.57), channel_id=1, source_target_pairs={{0,32},{8,40},{16,48},{24,56},{32,64},{40,72},{48,80},{56,88},{64,... | collective-permute-start | bytes 516104 | tf_op jit(solution)/shard_map/ppermute | solution.py:275
  42.8 0.0 copy-start.12
  42.8 0.0 copy-done.2
  42.8 0.0 copy-done.3
  42.8 0.0 copy-done.4
  42.8 0.6 copy-done.12
  43.5 0.4 shard_map.232
  43.8 4.9 %all-to-all-done.1.kv_ref = bf16[4,4,2,128,128]{4,3,2,1,0:T(8,128)(2,1)S(1)} async-done(((bf16[4,4,2,128,128]{4,3,2,1,0:T(8,128)(2,1)}), bf16[4,4,2,128,128]{4,3,2,1,0:T(8,128)(2,1)S(1)}, u32[]{:S(2)}, u32[]{:S(2)}) %all-to-all-start.1) | async-done | bytes 1048608 | tf_op jit(solution)/shard_map/all_to_all | solution.py:279
  48.8 8.7 %shard_map.233 = (bf16[128,1024]{1,0:T(8,128)(2,1)S(1)}, bf16[128,1024]{1,0:T(8,128)(2,1)S(1)}, bf16[4,4,2,128,128]{4,3,2,1,0:T(8,128)(2,1)}) custom-call(bf16[1024,128]{1,0:T(8,128)(2,1)S(1)} %get-tuple-element.47.qs, bf16[128,1024]{1,0:T(8,128)(2,1)S(1)} %get-tuple-element.48.qt, bf16[1024,128]{1,0:T(8,128)(2,1)S(1)} %get-tuple-element.49.gs, ...), custom_call_target="tpu_custom_call" | custom-call | flops 3221225472 | bytes 1048576 | tf_op jit(solution)/shard_map/pallas_call | solution.py:40
  57.5 0.0 collective-permute-done.4.two_ref
  57.5 0.0 collective-permute-done.3.one_ref
  57.5 3.7 %all-to-all-start.2 = ((bf16[4,4,2,128,128]{4,3,2,1,0:T(8,128)(2,1)}), bf16[4,4,2,128,128]{4,3,2,1,0:T(8,128)(2,1)S(1)}, u32[]{:S(2)}, u32[]{:S(2)}) async-start(bf16[4,4,2,128,128]{4,3,2,1,0:T(8,128)(2,1)} %get-tuple-element.58), calls=%async_computation.2 | async-start | bytes 2097152 | tf_op jit(solution)/shard_map/all_to_all | solution.py:279
  61.2 4.0 %collective-permute-start.8 = (bf16[672,128]{1,0:T(8,128)(2,1)S(1)}, bf16[672,128]{1,0:T(8,128)(2,1)S(1)}, u32[]{:S(2)}, u32[]{:S(2)}) collective-permute-start(bf16[672,128]{1,0:T(8,128)(2,1)S(1)} %collective-permute-done.4.two_ref), channel_id=1, source_target_pairs={{0,32},{8,40},{16,48},{24,56},{32,64},{40,72},{48,80},{56,88},{64,... | collective-permute-start | bytes 516104 | tf_op jit(solution)/shard_map/ppermute | solution.py:275
  65.2 4.5 %collective-permute-start.9 = (bf16[672,128]{1,0:T(8,128)(2,1)S(1)}, bf16[672,128]{1,0:T(8,128)(2,1)S(1)}, u32[]{:S(2)}, u32[]{:S(2)}) collective-permute-start(bf16[672,128]{1,0:T(8,128)(2,1)S(1)} %collective-permute-done.4.two_ref), channel_id=1, source_target_pairs={{0,64},{8,72},{16,80},{24,88},{32,96},{40,104},{48,112},{56,120},{... | collective-permute-start | bytes 516104 | tf_op jit(solution)/shard_map/ppermute | solution.py:275
  69.8 0.0 copy-done.5
  69.8 0.0 copy-start.10
  69.8 0.0 copy-start.11
  69.8 1.0 shard_map.234
  70.8 4.0 %all-to-all-done.2.y_ref = bf16[4,4,2,128,128]{4,3,2,1,0:T(8,128)(2,1)S(1)} async-done(((bf16[4,4,2,128,128]{4,3,2,1,0:T(8,128)(2,1)}), bf16[4,4,2,128,128]{4,3,2,1,0:T(8,128)(2,1)S(1)}, u32[]{:S(2)}, u32[]{:S(2)}) %all-to-all-start.2) | async-done | bytes 1048608 | tf_op jit(solution)/shard_map/all_to_all | solution.py:279
  74.8 0.0 copy-done.10
  74.8 0.0 copy-done.11
  74.8 1.1 shard_map.235
  75.9 0.0 collective-permute-done.8.three_ref
  75.9 0.0 collective-permute-done.9.four_ref
  75.9 4.8 %all-to-all-start.3 = ((bf16[8,192,128]{2,1,0:T(8,128)(2,1)}), bf16[8,192,128]{2,1,0:T(8,128)(2,1)S(1)}, u32[]{:S(2)}, u32[]{:S(2)}) async-start(bf16[8,192,128]{2,1,0:T(8,128)(2,1)} %get-tuple-element.67), calls=%async_computation.3 | async-start | bytes 786432 | tf_op jit(solution)/shard_map/all_to_all | solution.py:283
  80.7 1.3 collective-permute-start.5
  82.0 6.4 %collective-permute-done.5.near_ref = bf16[2,2,128,128]{3,2,1,0:T(8,128)(2,1)S(1)} collective-permute-done((bf16[2,2,128,128]{3,2,1,0:T(8,128)(2,1)S(1)}, bf16[2,2,128,128]{3,2,1,0:T(8,128)(2,1)S(1)}, u32[]{:S(2)}, u32[]{:S(2)}) %collective-permute-start.5) | collective-permute-done | bytes 131104 | tf_op jit(solution)/shard_map/ppermute | solution.py:275
  88.4 0.0 all-to-all-done.3.low_ref
  88.4 0.4 shard_map.238
  88.9 13.1 %all_to_all.35.in_ref = bf16[8,5,16,128]{3,2,1,0:T(8,128)(2,1)S(1)} all-to-all(bf16[8,5,16,128]{3,2,1,0:T(8,128)(2,1)S(1)} %shard_map.238), channel_id=1, replica_groups={{0,8,16,24,32,40,48,56},{64,72,80,88,96,104,112,120},{128,136,144,152,1..., dimensions={0} | all-to-all | bytes 327680 | tf_op jit(solution)/shard_map/all_to_all | solution.py:279
  101.9 0.7 shard_map.239
  102.6 11.4 %all-to-all-start.5 = ((bf16[8,5,16,128]{3,2,1,0:T(8,128)(2,1)}), bf16[8,5,16,128]{3,2,1,0:T(8,128)(2,1)S(1)}, u32[]{:S(2)}, u32[]{:S(2)}) async-start(bf16[8,5,16,128]{3,2,1,0:T(8,128)(2,1)} %shard_map.239), calls=%async_computation.5 | async-start | bytes 327680 | tf_op jit(solution)/shard_map/all_to_all | solution.py:279
  114.1 1.3 collective-permute-start.6
  115.4 1.3 collective-permute-start.7
  116.7 5.2 %collective-permute-done.6.one_ref = bf16[2,128,128]{2,1,0:T(8,128)(2,1)S(1)} collective-permute-done((bf16[2,128,128]{2,1,0:T(8,128)(2,1)S(1)}, bf16[2,128,128]{2,1,0:T(8,128)(2,1)S(1)}, u32[]{:S(2)}, u32[]{:S(2)}) %collective-permute-start.6) | collective-permute-done | bytes 65568 | tf_op jit(solution)/shard_map/ppermute | solution.py:275
  121.9 6.8 %collective-permute-done.7.three_ref = bf16[2,128,128]{2,1,0:T(8,128)(2,1)S(1)} collective-permute-done((bf16[2,128,128]{2,1,0:T(8,128)(2,1)S(1)}, bf16[2,128,128]{2,1,0:T(8,128)(2,1)S(1)}, u32[]{:S(2)}, u32[]{:S(2)}) %collective-permute-start.7) | collective-permute-done | bytes 65568 | tf_op jit(solution)/shard_map/ppermute | solution.py:275
  128.8 0.6 all-to-all-done.5.in_ref
  129.4 0.7 shard_map.240
  130.1 5.2 %all-to-all-start.6 = ((bf16[8,5,16,128]{3,2,1,0:T(8,128)(2,1)}), bf16[8,5,16,128]{3,2,1,0:T(8,128)(2,1)S(1)}, u32[]{:S(2)}, u32[]{:S(2)}) async-start(bf16[8,5,16,128]{3,2,1,0:T(8,128)(2,1)} %shard_map.240), calls=%async_computation.6 | async-start | bytes 327680 | tf_op jit(solution)/shard_map/all_to_all | solution.py:279
  135.2 0.6 shard_map.237
  135.9 6.1 %all-to-all-done.6.in_ref = bf16[8,5,16,128]{3,2,1,0:T(8,128)(2,1)S(1)} async-done(((bf16[8,5,16,128]{3,2,1,0:T(8,128)(2,1)}), bf16[8,5,16,128]{3,2,1,0:T(8,128)(2,1)S(1)}, u32[]{:S(2)}, u32[]{:S(2)}) %all-to-all-start.6) | async-done | bytes 163872 | tf_op jit(solution)/shard_map/all_to_all | solution.py:279
  142.0 0.7 shard_map.241
  (9 shorter events, 0.1 us)
Async XLA Ops:
  0.6 14.6 %copy-start.1 = (bf16[128,640]{1,0:T(8,128)(2,1)S(1)}, bf16[128,640]{1,0:T(8,128)(2,1)}, u32[]{:S(2)}) copy-start(bf16[128,640]{1,0:T(8,128)(2,1)} %dout_ref.3) | copy-start | bytes 491524
  1.5 13.8 %copy-start = (bf16[128,640]{1,0:T(8,128)(2,1)S(1)}, bf16[128,640]{1,0:T(8,128)(2,1)}, u32[]{:S(2)}) copy-start(bf16[128,640]{1,0:T(8,128)(2,1)} %x_ref.5) | copy-start | bytes 491524
  1.5 5.8 %collective-permute-start = (bf16[2,128,128]{2,1,0:T(8,128)(2,1)S(1)}, bf16[2,128,128]{2,1,0:T(8,128)(2,1)S(1)}, u32[]{:S(2)}, u32[]{:S(2)}) collective-permute-start(bf16[2,128,128]{2,1,0:T(8,128)(2,1)S(1)} %get-tuple-element.80.pair_ref), channel_id=1, source_target_pairs={{0,32},{8,40},{16,48},{24,56},{32,64},{40,72},{48,80},{56,88},{64,... | collective-permute-start | bytes 196616 | tf_op jit(solution)/shard_map/ppermute | solution.py:275
  7.3 7.9 %copy-start.6 = (bf16[640,16]{0,1:T(8,128)(2,1)S(1)}, bf16[640,16]{0,1:T(8,128)(2,1)}, u32[]{:S(2)}) copy-start(bf16[640,16]{0,1:T(8,128)(2,1)} %param.22) | copy-start | bytes 61444
  7.3 7.9 %copy-start.7 = (bf16[640,16]{0,1:T(8,128)(2,1)S(1)}, bf16[640,16]{0,1:T(8,128)(2,1)}, u32[]{:S(2)}) copy-start(bf16[640,16]{0,1:T(8,128)(2,1)} %param.24) | copy-start | bytes 61444
  7.3 8.0 %copy-start.8 = (bf16[640,16]{0,1:T(8,128)(2,1)S(1)}, bf16[640,16]{0,1:T(8,128)(2,1)}, u32[]{:S(2)}) copy-start(bf16[640,16]{0,1:T(8,128)(2,1)} %param.26) | copy-start | bytes 61444
  7.3 8.0 %copy-start.9 = (bf16[16,640]{1,0:T(8,128)(2,1)S(1)}, bf16[16,640]{1,0:T(8,128)(2,1)}, u32[]{:S(2)}) copy-start(bf16[16,640]{1,0:T(8,128)(2,1)} %ou_ref.1) | copy-start | bytes 61444
  7.4 21.1 %collective-permute-start.2 = (bf16[2,2,128,128]{3,2,1,0:T(8,128)(2,1)S(1)}, bf16[2,2,128,128]{3,2,1,0:T(8,128)(2,1)S(1)}, u32[]{:S(2)}, u32[]{:S(2)}) collective-permute-start(bf16[2,2,128,128]{3,2,1,0:T(8,128)(2,1)S(1)} %pad_maximum_fusion), channel_id=1, source_target_pairs={{0,96},{8,104},{16,112},{24,120},{32,128},{40,136},{48,144},{56,15... | collective-permute-start | bytes 393224 | tf_op jit(solution)/shard_map/ppermute | solution.py:275
  16.3 12.2 %all-to-all-start = ((bf16[8,64,128]{2,1,0:T(8,128)(2,1)}), bf16[8,64,128]{2,1,0:T(8,128)(2,1)S(1)}, u32[]{:S(2)}, u32[]{:S(2)}) async-start(bf16[8,64,128]{2,1,0:T(8,128)(2,1)} %shard_map.230), calls=%async_computation | async-start | bytes 262144 | tf_op jit(solution)/shard_map/all_to_all | solution.py:283
  21.1 7.4 %collective-permute-start.1 = (bf16[2,128,128]{2,1,0:T(8,128)(2,1)S(1)}, bf16[2,128,128]{2,1,0:T(8,128)(2,1)S(1)}, u32[]{:S(2)}, u32[]{:S(2)}) collective-permute-start(bf16[2,128,128]{2,1,0:T(8,128)(2,1)S(1)} %collective-permute-done.one_ref), channel_id=1, source_target_pairs={{0,32},{8,40},{16,48},{24,56},{32,64},{40,72},{48,80},{56,88},{64,... | collective-permute-start | bytes 196616 | tf_op jit(solution)/shard_map/ppermute | solution.py:275
  29.6 13.2 %copy-start.2 = (bf16[128,1024]{1,0:T(8,128)(2,1)S(1)}, bf16[128,1024]{1,0:T(8,128)(2,1)}, u32[]{:S(2)}) copy-start(bf16[128,1024]{1,0:T(8,128)(2,1)} %q_ref.1) | copy-start | bytes 786436
  29.6 13.2 %copy-start.3 = (bf16[128,1024]{1,0:T(8,128)(2,1)S(1)}, bf16[128,1024]{1,0:T(8,128)(2,1)}, u32[]{:S(2)}) copy-start(bf16[128,1024]{1,0:T(8,128)(2,1)} %f_ref.1) | copy-start | bytes 786436
  29.6 13.2 %copy-start.4 = (bf16[1024,16]{0,1:T(8,128)(2,1)S(1)}, bf16[1024,16]{0,1:T(8,128)(2,1)}, u32[]{:S(2)}) copy-start(bf16[1024,16]{0,1:T(8,128)(2,1)} %param.28) | copy-start | bytes 98308
  29.6 19.1 %all-to-all-start.1 = ((bf16[4,4,2,128,128]{4,3,2,1,0:T(8,128)(2,1)}), bf16[4,4,2,128,128]{4,3,2,1,0:T(8,128)(2,1)S(1)}, u32[]{:S(2)}, u32[]{:S(2)}) async-start(bf16[4,4,2,128,128]{4,3,2,1,0:T(8,128)(2,1)} %get-tuple-element.51), calls=%async_computation.1 | async-start | bytes 2097152 | tf_op jit(solution)/shard_map/all_to_all | solution.py:279
  34.2 23.3 %collective-permute-start.4 = (bf16[672,128]{1,0:T(8,128)(2,1)}, bf16[672,128]{1,0:T(8,128)(2,1)S(1)}, u32[]{:S(2)}, u32[]{:S(2)}) collective-permute-start(bf16[672,128]{1,0:T(8,128)(2,1)} %get-tuple-element.57), channel_id=1, source_target_pairs={{0,64},{8,72},{16,80},{24,88},{32,96},{40,104},{48,112},{56,120},{... | collective-permute-start | bytes 516104 | tf_op jit(solution)/shard_map/ppermute | solution.py:275
  38.7 18.9 %collective-permute-start.3 = (bf16[672,128]{1,0:T(8,128)(2,1)}, bf16[672,128]{1,0:T(8,128)(2,1)S(1)}, u32[]{:S(2)}, u32[]{:S(2)}) collective-permute-start(bf16[672,128]{1,0:T(8,128)(2,1)} %get-tuple-element.57), channel_id=1, source_target_pairs={{0,32},{8,40},{16,48},{24,56},{32,64},{40,72},{48,80},{56,88},{64,... | collective-permute-start | bytes 516104 | tf_op jit(solution)/shard_map/ppermute | solution.py:275
  42.8 0.7 copy-start.12
  57.5 12.2 %copy-start.5 = (bf16[16,1024]{1,0:T(8,128)(2,1)S(1)}, bf16[16,1024]{1,0:T(8,128)(2,1)}, u32[]{:S(2)}) copy-start(bf16[16,1024]{1,0:T(8,128)(2,1)} %qu_ref.1) | copy-start | bytes 98308
  57.5 17.3 %all-to-all-start.2 = ((bf16[4,4,2,128,128]{4,3,2,1,0:T(8,128)(2,1)}), bf16[4,4,2,128,128]{4,3,2,1,0:T(8,128)(2,1)S(1)}, u32[]{:S(2)}, u32[]{:S(2)}) async-start(bf16[4,4,2,128,128]{4,3,2,1,0:T(8,128)(2,1)} %get-tuple-element.58), calls=%async_computation.2 | async-start | bytes 2097152 | tf_op jit(solution)/shard_map/all_to_all | solution.py:279
  61.2 14.7 %collective-permute-start.8 = (bf16[672,128]{1,0:T(8,128)(2,1)S(1)}, bf16[672,128]{1,0:T(8,128)(2,1)S(1)}, u32[]{:S(2)}, u32[]{:S(2)}) collective-permute-start(bf16[672,128]{1,0:T(8,128)(2,1)S(1)} %collective-permute-done.4.two_ref), channel_id=1, source_target_pairs={{0,32},{8,40},{16,48},{24,56},{32,64},{40,72},{48,80},{56,88},{64,... | collective-permute-start | bytes 516104 | tf_op jit(solution)/shard_map/ppermute | solution.py:275
  65.2 10.7 %collective-permute-start.9 = (bf16[672,128]{1,0:T(8,128)(2,1)S(1)}, bf16[672,128]{1,0:T(8,128)(2,1)S(1)}, u32[]{:S(2)}, u32[]{:S(2)}) collective-permute-start(bf16[672,128]{1,0:T(8,128)(2,1)S(1)} %collective-permute-done.4.two_ref), channel_id=1, source_target_pairs={{0,64},{8,72},{16,80},{24,88},{32,96},{40,104},{48,112},{56,120},{... | collective-permute-start | bytes 516104 | tf_op jit(solution)/shard_map/ppermute | solution.py:275
  69.8 5.0 %copy-start.10 = (bf16[16,128]{1,0:T(8,128)(2,1)S(1)}, bf16[16,128]{1,0:T(8,128)(2,1)}, u32[]{:S(2)}) copy-start(bf16[16,128]{1,0:T(8,128)(2,1)} %ku_ref.1) | copy-start | bytes 12292
  69.8 5.0 %copy-start.11 = (bf16[16,128]{1,0:T(8,128)(2,1)S(1)}, bf16[16,128]{1,0:T(8,128)(2,1)}, u32[]{:S(2)}) copy-start(bf16[16,128]{1,0:T(8,128)(2,1)} %vu_ref.1) | copy-start | bytes 12292
  75.9 12.5 %all-to-all-start.3 = ((bf16[8,192,128]{2,1,0:T(8,128)(2,1)}), bf16[8,192,128]{2,1,0:T(8,128)(2,1)S(1)}, u32[]{:S(2)}, u32[]{:S(2)}) async-start(bf16[8,192,128]{2,1,0:T(8,128)(2,1)} %get-tuple-element.67), calls=%async_computation.3 | async-start | bytes 786432 | tf_op jit(solution)/shard_map/all_to_all | solution.py:283
  80.7 7.7 %collective-permute-start.5 = (bf16[2,2,128,128]{3,2,1,0:T(8,128)(2,1)S(1)}, bf16[2,2,128,128]{3,2,1,0:T(8,128)(2,1)S(1)}, u32[]{:S(2)}, u32[]{:S(2)}) collective-permute-start(bf16[2,2,128,128]{3,2,1,0:T(8,128)(2,1)S(1)} %get-tuple-element.61), channel_id=1, source_target_pairs={{32,0},{40,8},{48,16},{56,24},{64,32},{72,40},{80,48},{88,56},{96,... | collective-permute-start | bytes 393224 | tf_op jit(solution)/shard_map/ppermute | solution.py:275
  102.6 26.8 %all-to-all-start.5 = ((bf16[8,5,16,128]{3,2,1,0:T(8,128)(2,1)}), bf16[8,5,16,128]{3,2,1,0:T(8,128)(2,1)S(1)}, u32[]{:S(2)}, u32[]{:S(2)}) async-start(bf16[8,5,16,128]{3,2,1,0:T(8,128)(2,1)} %shard_map.239), calls=%async_computation.5 | async-start | bytes 327680 | tf_op jit(solution)/shard_map/all_to_all | solution.py:279
  114.1 7.8 %collective-permute-start.6 = (bf16[2,128,128]{2,1,0:T(8,128)(2,1)S(1)}, bf16[2,128,128]{2,1,0:T(8,128)(2,1)S(1)}, u32[]{:S(2)}, u32[]{:S(2)}) collective-permute-start(bf16[2,128,128]{2,1,0:T(8,128)(2,1)S(1)} %get-tuple-element.62), channel_id=1, source_target_pairs={{32,0},{40,8},{48,16},{56,24},{64,32},{72,40},{80,48},{88,56},{96,... | collective-permute-start | bytes 196616 | tf_op jit(solution)/shard_map/ppermute | solution.py:275
  115.4 13.4 %collective-permute-start.7 = (bf16[2,128,128]{2,1,0:T(8,128)(2,1)S(1)}, bf16[2,128,128]{2,1,0:T(8,128)(2,1)S(1)}, u32[]{:S(2)}, u32[]{:S(2)}) collective-permute-start(bf16[2,128,128]{2,1,0:T(8,128)(2,1)S(1)} %get-tuple-element.63), channel_id=1, source_target_pairs={{96,0},{104,8},{112,16},{120,24},{128,32},{136,40},{144,48},{152,5... | collective-permute-start | bytes 196616 | tf_op jit(solution)/shard_map/ppermute | solution.py:275
  130.1 11.9 %all-to-all-start.6 = ((bf16[8,5,16,128]{3,2,1,0:T(8,128)(2,1)}), bf16[8,5,16,128]{3,2,1,0:T(8,128)(2,1)S(1)}, u32[]{:S(2)}, u32[]{:S(2)}) async-start(bf16[8,5,16,128]{3,2,1,0:T(8,128)(2,1)} %shard_map.240), calls=%async_computation.6 | async-start | bytes 327680 | tf_op jit(solution)/shard_map/all_to_all | solution.py:279

commit v4 on v3

--- a/solution.py
+++ b/solution.py
@@ -110,17 +110,13 @@
 def attention_kernel(
     qs, qt, gs, gt, kv_ref, start_ref,
     dqt_ref, ot_ref, dkv_ref,
-    s_ref, ot, dqt, ds, low_prob, bias, top, total, delta,
+    s_ref, wide_low, bias, total, delta,
 ):
     index = lax.axis_index("ctx")
     y_place = index % 4
     start = start_ref[0:1]
     start = start.astype(jnp.int32)
     q_pos = lax.broadcasted_iota(jnp.int32, (1, 128), 1) + index * ROWS
-    top[...] = jnp.full_like(top, NEG)
-    total[...] = jnp.zeros_like(total)
-    ot[...] = jnp.zeros_like(ot)
-    dqt[...] = jnp.zeros_like(dqt)
 
     def keys(plane, which):
         return kv_ref[:, plane, which].reshape(512, HEAD)
@@ -135,16 +131,20 @@
         raw = nn(keys(plane, 0), qt[...])
         raw = raw * (SCALE * LOG2E) + jnp.concatenate([bias[...]] * GROUP, axis=1)
         s_ref[plane] = raw
-        top[...] = jnp.maximum(top[...], jnp.max(raw, axis=0, keepdims=True))
+        best = jnp.max(raw, axis=0, keepdims=True)
+        peak = best if plane == 0 else jnp.maximum(peak, best)
+    values_t = jnp.concatenate([keys(plane, 1).T for plane in range(4)], axis=1)
+    norm = jnp.zeros((1, 1024), F32)
     for plane in range(4):
-        prob = jnp.exp2(s_ref[plane] - top[...])
+        prob = jnp.exp2(s_ref[plane] - peak)
         s_ref[plane] = prob
-        total[...] += jnp.sum(prob, axis=0, keepdims=True)
-        ot[...] += nn(keys(plane, 1).T, prob.astype(BF16))
-    total[...] = 1.0 / total[...]
+        norm = norm + jnp.sum(prob, axis=0, keepdims=True)
+        wide_low[plane * 512 : plane * 512 + 512, :] = prob.astype(BF16)
+    weighted = nn(values_t, wide_low[...])
+    total[...] = 1.0 / norm
     for n in range(GROUP):
         cols = slice(n * HEAD, (n + 1) * HEAD)
-        o_n = (ot[:, cols] * total[:, cols]).astype(BF16)
+        o_n = (weighted[:, cols] * total[:, cols]).astype(BF16)
         ot_ref[:, cols] = o_n
         delta[:, cols] = jnp.sum(
             o_n.astype(F32) * gt[:, cols].astype(F32), axis=0, keepdims=True
@@ -153,14 +153,13 @@
         prob = s_ref[plane] * total[...]
         grad_prob = nn(keys(plane, 1), gt[...])
         grad_score = (prob * (grad_prob - delta[...])).astype(BF16)
-        ds[...] = grad_score
-        low_prob[...] = prob.astype(BF16)
-        dqt[...] += nn(keys(plane, 0).T, grad_score)
-        dk = (nn(ds[...], qs[...]) * SCALE).astype(BF16)
-        dv = nn(low_prob[...], gs[...]).astype(BF16)
+        wide_low[plane * 512 : plane * 512 + 512, :] = grad_score
+        dk = (nn(grad_score, qs[...]) * SCALE).astype(BF16)
+        dv = nn(prob.astype(BF16), gs[...]).astype(BF16)
         dkv_ref[:, plane, 0] = dk.reshape(4, 128, HEAD)
         dkv_ref[:, plane, 1] = dv.reshape(4, 128, HEAD)
-    dqt_ref[...] = (dqt[...] * SCALE).astype(BF16)
+    keys_t = jnp.concatenate([keys(plane, 0).T for plane in range(4)], axis=1)
+    dqt_ref[...] = (nn(keys_t, wide_low[...]) * SCALE).astype(BF16)
 
 
 def finish_kernel(dqt_ref, ot_ref, low_ref, od_ref, qu_ref, dq_ref, back_ref, tot_ref):
@@ -305,7 +304,7 @@
     window = exchange(window, Y_GROUPS)
     x_one = shift(x_rows, 4)
     x_two = shift(x_rows, 8)
-    x_three, x_four = shift(x_two, 4), shift(x_two, 8)
+    x_four, x_three = shift(x_two, 8), shift(x_two, 4)
     qs, qt, gs, gt, starts = call(
         prepare_kernel,
         (tall, wide, tall, wide, shaped((8, 128), F32)),
@@ -317,12 +316,8 @@
         qs, qt, gs, gt, window, starts,
         scratch=[
             pltpu.VMEM((4, 512, 1024), F32),
-            pltpu.VMEM((128, 1024), F32),
-            pltpu.VMEM((128, 1024), F32),
-            pltpu.VMEM((512, 1024), BF16),
-            pltpu.VMEM((512, 1024), BF16),
+            pltpu.VMEM((2048, 1024), BF16),
             pltpu.VMEM((512, 128), F32),
-            pltpu.VMEM((1, 1024), F32),
             pltpu.VMEM((1, 1024), F32),
             pltpu.VMEM((1, 1024), F32),
         ],
@@ -345,7 +340,7 @@
         dkv, back, ku, vu,
     )
     near = shift(near, -4)
-    low_back = exchange_head(after(low_back, x_three, x_four))
+    low_back = exchange_head(after(low_back, x_four, x_three))
     low_back = after(low_back, near)
     packed = shaped((8, 5, 16, 128), BF16)
     sums = call(
@@ -353,8 +348,8 @@
     )
     sums = call(sum_spread_kernel, packed, exchange(sums, EIGHTS))
     one_back, three_back = call(pass_kernel, (block, block), parts, near)
-    one_back, three_back = shift(one_back, -4), shift(three_back, -12)
-    sums = after(exchange(sums, STRIDED), one_back, three_back)
+    three_back, one_back = shift(three_back, -12), shift(one_back, -4)
+    sums = after(exchange(sums, STRIDED), three_back, one_back)
     sums = call(sum_spread_kernel, packed, sums)
     sums = exchange(sums, EIGHTS)
     dk, dv = call(

time: 144 us -> 141 us (0.979)
  transfers between devices with their start and end apart: 16 -> 16, of which waited for: 9 -> 9; matrix products, arithmetic and copies ran while one was open for 0% -> 0% of each run, Pallas kernels for 9% -> 8%
where the time goes in v4:
time: 141 us; the launch traced here: 140 us
  starting transfers between devices  72.1 us (51%)
  waiting for transfers between devices  38 us (27%)
  Pallas kernels  15.3 us (11%)
  blocking collectives  11.9 us (8%)
    ppermute x10, starting transfers between devices, shift(): lax.ppermute(value, 'ctx', [(i, i + steps) for i in range(first, last)])  38.3 us
    all_to_all x4, starting transfers between devices, exchange(): lax.all_to_all(value, 'ctx', 0, 0, tiled=True, axis_index_groups=groups)  24.2 us
    ppermute x10, waiting for transfers between devices, shift(): lax.ppermute(value, 'ctx', [(i, i + steps) for i in range(first, last)])  22.3 us
    all_to_all x4, waiting for transfers between devices, exchange(): lax.all_to_all(value, 'ctx', 0, 0, tiled=True, axis_index_groups=groups)  15.7 us
    pallas_call x12, Pallas kernels, call(): pl.pallas_call(body, out_shape=outs, scratch_shapes=list(scratch), compil...  15.3 us
    all_to_all x1, blocking collectives, exchange(): lax.all_to_all(value, 'ctx', 0, 0, tiled=True, axis_index_groups=groups)  11.9 us
    all_to_all x2, starting transfers between devices, exchange_head(): return lax.all_to_all(value, 'head', 0, 0, tiled=True)  9.64 us
  transfers between devices with their start and end apart: 16, of which 9 were waited for; matrix products, arithmetic and copies ran while one was open for 0% of the time, Pallas kernels for 8%

profile of v4, /device:TPU:2, one launch (start us, length us, event | category | flops | bytes accessed | tf_op | source)
XLA Modules:
  0.0 139.7 jit_solution(8443265077582192114)
XLA Ops:
  0.6 0.0 copy-start.1
  0.7 0.8 fusion
  1.5 0.0 copy-start
  1.5 4.0 %collective-permute-start = (bf16[2,128,128]{2,1,0:T(8,128)(2,1)S(1)}, bf16[2,128,128]{2,1,0:T(8,128)(2,1)S(1)}, u32[]{:S(2)}, u32[]{:S(2)}) collective-permute-start(bf16[2,128,128]{2,1,0:T(8,128)(2,1)S(1)} %get-tuple-element.80.pair_ref), channel_id=1, source_target_pairs={{0,32},{8,40},{16,48},{24,56},{32,64},{40,72},{48,80},{56,88},{64,... | collective-permute-start | bytes 196616 | tf_op jit(solution)/shard_map/ppermute | solution.py:274
  5.5 1.9 %collective-permute-done.one_ref = bf16[2,128,128]{2,1,0:T(8,128)(2,1)S(1)} collective-permute-done((bf16[2,128,128]{2,1,0:T(8,128)(2,1)S(1)}, bf16[2,128,128]{2,1,0:T(8,128)(2,1)S(1)}, u32[]{:S(2)}, u32[]{:S(2)}) %collective-permute-start) | collective-permute-done | bytes 65568 | tf_op jit(solution)/shard_map/ppermute | solution.py:274
  7.3 0.0 copy-start.6
  7.4 7.9 %collective-permute-start.2 = (bf16[2,2,128,128]{3,2,1,0:T(8,128)(2,1)S(1)}, bf16[2,2,128,128]{3,2,1,0:T(8,128)(2,1)S(1)}, u32[]{:S(2)}, u32[]{:S(2)}) collective-permute-start(bf16[2,2,128,128]{3,2,1,0:T(8,128)(2,1)S(1)} %pad_maximum_fusion), channel_id=1, source_target_pairs={{0,96},{8,104},{16,112},{24,120},{32,128},{40,136},{48,144},{56,15... | collective-permute-start | bytes 393224 | tf_op jit(solution)/shard_map/ppermute | solution.py:274
  15.3 0.0 copy-done.1
  15.3 0.0 copy-done
  15.3 0.0 copy-done.6
  15.3 0.0 copy-done.7
  15.3 0.0 copy-done.8
  15.3 0.0 copy-done.9
  15.3 1.0 shard_map.230
  16.3 4.8 %all-to-all-start = ((bf16[8,64,128]{2,1,0:T(8,128)(2,1)}), bf16[8,64,128]{2,1,0:T(8,128)(2,1)S(1)}, u32[]{:S(2)}, u32[]{:S(2)}) async-start(bf16[8,64,128]{2,1,0:T(8,128)(2,1)} %shard_map.230), calls=%async_computation | async-start | bytes 262144 | tf_op jit(solution)/shard_map/all_to_all | solution.py:282
  21.1 5.5 %collective-permute-start.1 = (bf16[2,128,128]{2,1,0:T(8,128)(2,1)S(1)}, bf16[2,128,128]{2,1,0:T(8,128)(2,1)S(1)}, u32[]{:S(2)}, u32[]{:S(2)}) collective-permute-start(bf16[2,128,128]{2,1,0:T(8,128)(2,1)S(1)} %collective-permute-done.one_ref), channel_id=1, source_target_pairs={{0,32},{8,40},{16,48},{24,56},{32,64},{40,72},{48,80},{56,88},{64,... | collective-permute-start | bytes 196616 | tf_op jit(solution)/shard_map/ppermute | solution.py:274
  26.6 1.9 %collective-permute-done.1.two_ref = bf16[2,128,128]{2,1,0:T(8,128)(2,1)S(1)} collective-permute-done((bf16[2,128,128]{2,1,0:T(8,128)(2,1)S(1)}, bf16[2,128,128]{2,1,0:T(8,128)(2,1)S(1)}, u32[]{:S(2)}, u32[]{:S(2)}) %collective-permute-start.1) | collective-permute-done | bytes 65568 | tf_op jit(solution)/shard_map/ppermute | solution.py:274
  28.5 0.0 all-to-all-done.low_ref
  28.5 0.0 collective-permute-done.2.back_ref
  28.5 1.1 shard_map.231
  29.6 4.6 %all-to-all-start.1 = ((bf16[4,4,2,128,128]{4,3,2,1,0:T(8,128)(2,1)}), bf16[4,4,2,128,128]{4,3,2,1,0:T(8,128)(2,1)S(1)}, u32[]{:S(2)}, u32[]{:S(2)}) async-start(bf16[4,4,2,128,128]{4,3,2,1,0:T(8,128)(2,1)} %get-tuple-element.51), calls=%async_computation.1 | async-start | bytes 2097152 | tf_op jit(solution)/shard_map/all_to_all | solution.py:278
  34.2 4.4 %collective-permute-start.4 = (bf16[672,128]{1,0:T(8,128)(2,1)}, bf16[672,128]{1,0:T(8,128)(2,1)S(1)}, u32[]{:S(2)}, u32[]{:S(2)}) collective-permute-start(bf16[672,128]{1,0:T(8,128)(2,1)} %get-tuple-element.57), channel_id=1, source_target_pairs={{0,64},{8,72},{16,80},{24,88},{32,96},{40,104},{48,112},{56,120},{... | collective-permute-start | bytes 516104 | tf_op jit(solution)/shard_map/ppermute | solution.py:274
  38.7 4.1 %collective-permute-start.3 = (bf16[672,128]{1,0:T(8,128)(2,1)}, bf16[672,128]{1,0:T(8,128)(2,1)S(1)}, u32[]{:S(2)}, u32[]{:S(2)}) collective-permute-start(bf16[672,128]{1,0:T(8,128)(2,1)} %get-tuple-element.57), channel_id=1, source_target_pairs={{0,32},{8,40},{16,48},{24,56},{32,64},{40,72},{48,80},{56,88},{64,... | collective-permute-start | bytes 516104 | tf_op jit(solution)/shard_map/ppermute | solution.py:274
  42.8 0.0 copy-start.12
  42.8 0.0 copy-done.2
  42.8 0.0 copy-done.3
  42.8 0.0 copy-done.4
  42.8 0.6 copy-done.12
  43.5 0.4 shard_map.232
  43.8 4.9 %all-to-all-done.1.kv_ref = bf16[4,4,2,128,128]{4,3,2,1,0:T(8,128)(2,1)S(1)} async-done(((bf16[4,4,2,128,128]{4,3,2,1,0:T(8,128)(2,1)}), bf16[4,4,2,128,128]{4,3,2,1,0:T(8,128)(2,1)S(1)}, u32[]{:S(2)}, u32[]{:S(2)}) %all-to-all-start.1) | async-done | bytes 1048608 | tf_op jit(solution)/shard_map/all_to_all | solution.py:278
  48.8 7.5 %shard_map.233 = (bf16[128,1024]{1,0:T(8,128)(2,1)S(1)}, bf16[128,1024]{1,0:T(8,128)(2,1)S(1)}, bf16[4,4,2,128,128]{4,3,2,1,0:T(8,128)(2,1)}) custom-call(bf16[1024,128]{1,0:T(8,128)(2,1)S(1)} %get-tuple-element.47.qs, bf16[128,1024]{1,0:T(8,128)(2,1)S(1)} %get-tuple-element.48.qt, bf16[1024,128]{1,0:T(8,128)(2,1)S(1)} %get-tuple-element.49.gs, ...), custom_call_target="tpu_custom_call" | custom-call | flops 3221225472 | bytes 1048576 | tf_op jit(solution)/shard_map/pallas_call | solution.py:40
  56.3 0.0 collective-permute-done.4.two_ref
  56.3 0.0 collective-permute-done.3.one_ref
  56.3 3.7 %all-to-all-start.2 = ((bf16[4,4,2,128,128]{4,3,2,1,0:T(8,128)(2,1)}), bf16[4,4,2,128,128]{4,3,2,1,0:T(8,128)(2,1)S(1)}, u32[]{:S(2)}, u32[]{:S(2)}) async-start(bf16[4,4,2,128,128]{4,3,2,1,0:T(8,128)(2,1)} %get-tuple-element.58), calls=%async_computation.2 | async-start | bytes 2097152 | tf_op jit(solution)/shard_map/all_to_all | solution.py:278
  60.0 4.1 %collective-permute-start.8 = (bf16[672,128]{1,0:T(8,128)(2,1)S(1)}, bf16[672,128]{1,0:T(8,128)(2,1)S(1)}, u32[]{:S(2)}, u32[]{:S(2)}) collective-permute-start(bf16[672,128]{1,0:T(8,128)(2,1)S(1)} %collective-permute-done.4.two_ref), channel_id=1, source_target_pairs={{0,64},{8,72},{16,80},{24,88},{32,96},{40,104},{48,112},{56,120},{... | collective-permute-start | bytes 516104 | tf_op jit(solution)/shard_map/ppermute | solution.py:274
  64.1 4.4 %collective-permute-start.9 = (bf16[672,128]{1,0:T(8,128)(2,1)S(1)}, bf16[672,128]{1,0:T(8,128)(2,1)S(1)}, u32[]{:S(2)}, u32[]{:S(2)}) collective-permute-start(bf16[672,128]{1,0:T(8,128)(2,1)S(1)} %collective-permute-done.4.two_ref), channel_id=1, source_target_pairs={{0,32},{8,40},{16,48},{24,56},{32,64},{40,72},{48,80},{56,88},{64,... | collective-permute-start | bytes 516104 | tf_op jit(solution)/shard_map/ppermute | solution.py:274
  68.5 0.0 copy-done.5
  68.5 0.0 copy-start.10
  68.6 0.0 copy-start.11
  68.6 1.0 shard_map.234
  69.6 4.0 %all-to-all-done.2.y_ref = bf16[4,4,2,128,128]{4,3,2,1,0:T(8,128)(2,1)S(1)} async-done(((bf16[4,4,2,128,128]{4,3,2,1,0:T(8,128)(2,1)}), bf16[4,4,2,128,128]{4,3,2,1,0:T(8,128)(2,1)S(1)}, u32[]{:S(2)}, u32[]{:S(2)}) %all-to-all-start.2) | async-done | bytes 1048608 | tf_op jit(solution)/shard_map/all_to_all | solution.py:278
  73.6 0.0 copy-done.10
  73.6 0.0 copy-done.11
  73.6 1.1 shard_map.235
  74.6 0.0 collective-permute-done.8.four_ref
  74.6 0.0 collective-permute-done.9.three_ref
  74.6 4.8 %all-to-all-start.3 = ((bf16[8,192,128]{2,1,0:T(8,128)(2,1)}), bf16[8,192,128]{2,1,0:T(8,128)(2,1)S(1)}, u32[]{:S(2)}, u32[]{:S(2)}) async-start(bf16[8,192,128]{2,1,0:T(8,128)(2,1)} %get-tuple-element.67), calls=%async_computation.3 | async-start | bytes 786432 | tf_op jit(solution)/shard_map/all_to_all | solution.py:282
  79.4 1.3 collective-permute-start.5
  80.7 6.4 %collective-permute-done.5.near_ref = bf16[2,2,128,128]{3,2,1,0:T(8,128)(2,1)S(1)} collective-permute-done((bf16[2,2,128,128]{3,2,1,0:T(8,128)(2,1)S(1)}, bf16[2,2,128,128]{3,2,1,0:T(8,128)(2,1)S(1)}, u32[]{:S(2)}, u32[]{:S(2)}) %collective-permute-start.5) | collective-permute-done | bytes 131104 | tf_op jit(solution)/shard_map/ppermute | solution.py:274
  87.2 0.0 all-to-all-done.3.low_ref
  87.2 0.4 shard_map.238
  87.6 11.9 %all_to_all.35.in_ref = bf16[8,5,16,128]{3,2,1,0:T(8,128)(2,1)S(1)} all-to-all(bf16[8,5,16,128]{3,2,1,0:T(8,128)(2,1)S(1)} %shard_map.238), channel_id=1, replica_groups={{0,8,16,24,32,40,48,56},{64,72,80,88,96,104,112,120},{128,136,144,152,1..., dimensions={0} | all-to-all | bytes 327680 | tf_op jit(solution)/shard_map/all_to_all | solution.py:278
  99.5 0.7 shard_map.239
  100.2 10.8 %all-to-all-start.5 = ((bf16[8,5,16,128]{3,2,1,0:T(8,128)(2,1)}), bf16[8,5,16,128]{3,2,1,0:T(8,128)(2,1)S(1)}, u32[]{:S(2)}, u32[]{:S(2)}) async-start(bf16[8,5,16,128]{3,2,1,0:T(8,128)(2,1)} %shard_map.239), calls=%async_computation.5 | async-start | bytes 327680 | tf_op jit(solution)/shard_map/all_to_all | solution.py:278
  111.1 1.3 collective-permute-start.6
  112.4 1.3 collective-permute-start.7
  113.7 5.2 %collective-permute-done.6.one_ref = bf16[2,128,128]{2,1,0:T(8,128)(2,1)S(1)} collective-permute-done((bf16[2,128,128]{2,1,0:T(8,128)(2,1)S(1)}, bf16[2,128,128]{2,1,0:T(8,128)(2,1)S(1)}, u32[]{:S(2)}, u32[]{:S(2)}) %collective-permute-start.6) | collective-permute-done | bytes 65568 | tf_op jit(solution)/shard_map/ppermute | solution.py:274
  118.9 6.8 %collective-permute-done.7.three_ref = bf16[2,128,128]{2,1,0:T(8,128)(2,1)S(1)} collective-permute-done((bf16[2,128,128]{2,1,0:T(8,128)(2,1)S(1)}, bf16[2,128,128]{2,1,0:T(8,128)(2,1)S(1)}, u32[]{:S(2)}, u32[]{:S(2)}) %collective-permute-start.7) | collective-permute-done | bytes 65568 | tf_op jit(solution)/shard_map/ppermute | solution.py:274
  125.8 0.6 all-to-all-done.5.in_ref
  126.4 0.7 shard_map.240
  127.1 5.1 %all-to-all-start.6 = ((bf16[8,5,16,128]{3,2,1,0:T(8,128)(2,1)}), bf16[8,5,16,128]{3,2,1,0:T(8,128)(2,1)S(1)}, u32[]{:S(2)}, u32[]{:S(2)}) async-start(bf16[8,5,16,128]{3,2,1,0:T(8,128)(2,1)} %shard_map.240), calls=%async_computation.6 | async-start | bytes 327680 | tf_op jit(solution)/shard_map/all_to_all | solution.py:278
  132.2 0.6 shard_map.237
  132.9 6.1 %all-to-all-done.6.in_ref = bf16[8,5,16,128]{3,2,1,0:T(8,128)(2,1)S(1)} async-done(((bf16[8,5,16,128]{3,2,1,0:T(8,128)(2,1)}), bf16[8,5,16,128]{3,2,1,0:T(8,128)(2,1)S(1)}, u32[]{:S(2)}, u32[]{:S(2)}) %all-to-all-start.6) | async-done | bytes 163872 | tf_op jit(solution)/shard_map/all_to_all | solution.py:278
  139.0 0.7 shard_map.241
  (9 shorter events, 0.1 us)
Async XLA Ops:
  0.6 14.6 %copy-start.1 = (bf16[128,640]{1,0:T(8,128)(2,1)S(1)}, bf16[128,640]{1,0:T(8,128)(2,1)}, u32[]{:S(2)}) copy-start(bf16[128,640]{1,0:T(8,128)(2,1)} %dout_ref.3) | copy-start | bytes 491524
  1.5 13.8 %copy-start = (bf16[128,640]{1,0:T(8,128)(2,1)S(1)}, bf16[128,640]{1,0:T(8,128)(2,1)}, u32[]{:S(2)}) copy-start(bf16[128,640]{1,0:T(8,128)(2,1)} %x_ref.5) | copy-start | bytes 491524
  1.5 5.8 %collective-permute-start = (bf16[2,128,128]{2,1,0:T(8,128)(2,1)S(1)}, bf16[2,128,128]{2,1,0:T(8,128)(2,1)S(1)}, u32[]{:S(2)}, u32[]{:S(2)}) collective-permute-start(bf16[2,128,128]{2,1,0:T(8,128)(2,1)S(1)} %get-tuple-element.80.pair_ref), channel_id=1, source_target_pairs={{0,32},{8,40},{16,48},{24,56},{32,64},{40,72},{48,80},{56,88},{64,... | collective-permute-start | bytes 196616 | tf_op jit(solution)/shard_map/ppermute | solution.py:274
  7.3 7.9 %copy-start.6 = (bf16[640,16]{0,1:T(8,128)(2,1)S(1)}, bf16[640,16]{0,1:T(8,128)(2,1)}, u32[]{:S(2)}) copy-start(bf16[640,16]{0,1:T(8,128)(2,1)} %param.22) | copy-start | bytes 61444
  7.3 7.9 %copy-start.7 = (bf16[640,16]{0,1:T(8,128)(2,1)S(1)}, bf16[640,16]{0,1:T(8,128)(2,1)}, u32[]{:S(2)}) copy-start(bf16[640,16]{0,1:T(8,128)(2,1)} %param.24) | copy-start | bytes 61444
  7.3 8.0 %copy-start.8 = (bf16[640,16]{0,1:T(8,128)(2,1)S(1)}, bf16[640,16]{0,1:T(8,128)(2,1)}, u32[]{:S(2)}) copy-start(bf16[640,16]{0,1:T(8,128)(2,1)} %param.26) | copy-start | bytes 61444
  7.3 8.0 %copy-start.9 = (bf16[16,640]{1,0:T(8,128)(2,1)S(1)}, bf16[16,640]{1,0:T(8,128)(2,1)}, u32[]{:S(2)}) copy-start(bf16[16,640]{1,0:T(8,128)(2,1)} %ou_ref.1) | copy-start | bytes 61444
  7.4 21.1 %collective-permute-start.2 = (bf16[2,2,128,128]{3,2,1,0:T(8,128)(2,1)S(1)}, bf16[2,2,128,128]{3,2,1,0:T(8,128)(2,1)S(1)}, u32[]{:S(2)}, u32[]{:S(2)}) collective-permute-start(bf16[2,2,128,128]{3,2,1,0:T(8,128)(2,1)S(1)} %pad_maximum_fusion), channel_id=1, source_target_pairs={{0,96},{8,104},{16,112},{24,120},{32,128},{40,136},{48,144},{56,15... | collective-permute-start | bytes 393224 | tf_op jit(solution)/shard_map/ppermute | solution.py:274
  16.3 12.2 %all-to-all-start = ((bf16[8,64,128]{2,1,0:T(8,128)(2,1)}), bf16[8,64,128]{2,1,0:T(8,128)(2,1)S(1)}, u32[]{:S(2)}, u32[]{:S(2)}) async-start(bf16[8,64,128]{2,1,0:T(8,128)(2,1)} %shard_map.230), calls=%async_computation | async-start | bytes 262144 | tf_op jit(solution)/shard_map/all_to_all | solution.py:282
  21.1 7.4 %collective-permute-start.1 = (bf16[2,128,128]{2,1,0:T(8,128)(2,1)S(1)}, bf16[2,128,128]{2,1,0:T(8,128)(2,1)S(1)}, u32[]{:S(2)}, u32[]{:S(2)}) collective-permute-start(bf16[2,128,128]{2,1,0:T(8,128)(2,1)S(1)} %collective-permute-done.one_ref), channel_id=1, source_target_pairs={{0,32},{8,40},{16,48},{24,56},{32,64},{40,72},{48,80},{56,88},{64,... | collective-permute-start | bytes 196616 | tf_op jit(solution)/shard_map/ppermute | solution.py:274
  29.6 13.2 %copy-start.2 = (bf16[128,1024]{1,0:T(8,128)(2,1)S(1)}, bf16[128,1024]{1,0:T(8,128)(2,1)}, u32[]{:S(2)}) copy-start(bf16[128,1024]{1,0:T(8,128)(2,1)} %q_ref.1) | copy-start | bytes 786436
  29.6 13.2 %copy-start.3 = (bf16[128,1024]{1,0:T(8,128)(2,1)S(1)}, bf16[128,1024]{1,0:T(8,128)(2,1)}, u32[]{:S(2)}) copy-start(bf16[128,1024]{1,0:T(8,128)(2,1)} %f_ref.1) | copy-start | bytes 786436
  29.6 13.2 %copy-start.4 = (bf16[1024,16]{0,1:T(8,128)(2,1)S(1)}, bf16[1024,16]{0,1:T(8,128)(2,1)}, u32[]{:S(2)}) copy-start(bf16[1024,16]{0,1:T(8,128)(2,1)} %param.28) | copy-start | bytes 98308
  29.6 19.1 %all-to-all-start.1 = ((bf16[4,4,2,128,128]{4,3,2,1,0:T(8,128)(2,1)}), bf16[4,4,2,128,128]{4,3,2,1,0:T(8,128)(2,1)S(1)}, u32[]{:S(2)}, u32[]{:S(2)}) async-start(bf16[4,4,2,128,128]{4,3,2,1,0:T(8,128)(2,1)} %get-tuple-element.51), calls=%async_computation.1 | async-start | bytes 2097152 | tf_op jit(solution)/shard_map/all_to_all | solution.py:278
  34.2 22.1 %collective-permute-start.4 = (bf16[672,128]{1,0:T(8,128)(2,1)}, bf16[672,128]{1,0:T(8,128)(2,1)S(1)}, u32[]{:S(2)}, u32[]{:S(2)}) collective-permute-start(bf16[672,128]{1,0:T(8,128)(2,1)} %get-tuple-element.57), channel_id=1, source_target_pairs={{0,64},{8,72},{16,80},{24,88},{32,96},{40,104},{48,112},{56,120},{... | collective-permute-start | bytes 516104 | tf_op jit(solution)/shard_map/ppermute | solution.py:274
  38.7 17.6 %collective-permute-start.3 = (bf16[672,128]{1,0:T(8,128)(2,1)}, bf16[672,128]{1,0:T(8,128)(2,1)S(1)}, u32[]{:S(2)}, u32[]{:S(2)}) collective-permute-start(bf16[672,128]{1,0:T(8,128)(2,1)} %get-tuple-element.57), channel_id=1, source_target_pairs={{0,32},{8,40},{16,48},{24,56},{32,64},{40,72},{48,80},{56,88},{64,... | collective-permute-start | bytes 516104 | tf_op jit(solution)/shard_map/ppermute | solution.py:274
  42.8 0.7 copy-start.12
  56.3 12.2 %copy-start.5 = (bf16[16,1024]{1,0:T(8,128)(2,1)S(1)}, bf16[16,1024]{1,0:T(8,128)(2,1)}, u32[]{:S(2)}) copy-start(bf16[16,1024]{1,0:T(8,128)(2,1)} %qu_ref.1) | copy-start | bytes 98308
  56.3 17.3 %all-to-all-start.2 = ((bf16[4,4,2,128,128]{4,3,2,1,0:T(8,128)(2,1)}), bf16[4,4,2,128,128]{4,3,2,1,0:T(8,128)(2,1)S(1)}, u32[]{:S(2)}, u32[]{:S(2)}) async-start(bf16[4,4,2,128,128]{4,3,2,1,0:T(8,128)(2,1)} %get-tuple-element.58), calls=%async_computation.2 | async-start | bytes 2097152 | tf_op jit(solution)/shard_map/all_to_all | solution.py:278
  60.0 14.7 %collective-permute-start.8 = (bf16[672,128]{1,0:T(8,128)(2,1)S(1)}, bf16[672,128]{1,0:T(8,128)(2,1)S(1)}, u32[]{:S(2)}, u32[]{:S(2)}) collective-permute-start(bf16[672,128]{1,0:T(8,128)(2,1)S(1)} %collective-permute-done.4.two_ref), channel_id=1, source_target_pairs={{0,64},{8,72},{16,80},{24,88},{32,96},{40,104},{48,112},{56,120},{... | collective-permute-start | bytes 516104 | tf_op jit(solution)/shard_map/ppermute | solution.py:274
  64.1 10.5 %collective-permute-start.9 = (bf16[672,128]{1,0:T(8,128)(2,1)S(1)}, bf16[672,128]{1,0:T(8,128)(2,1)S(1)}, u32[]{:S(2)}, u32[]{:S(2)}) collective-permute-start(bf16[672,128]{1,0:T(8,128)(2,1)S(1)} %collective-permute-done.4.two_ref), channel_id=1, source_target_pairs={{0,32},{8,40},{16,48},{24,56},{32,64},{40,72},{48,80},{56,88},{64,... | collective-permute-start | bytes 516104 | tf_op jit(solution)/shard_map/ppermute | solution.py:274
  68.5 5.0 %copy-start.10 = (bf16[16,128]{1,0:T(8,128)(2,1)S(1)}, bf16[16,128]{1,0:T(8,128)(2,1)}, u32[]{:S(2)}) copy-start(bf16[16,128]{1,0:T(8,128)(2,1)} %ku_ref.1) | copy-start | bytes 12292
  68.6 5.0 %copy-start.11 = (bf16[16,128]{1,0:T(8,128)(2,1)S(1)}, bf16[16,128]{1,0:T(8,128)(2,1)}, u32[]{:S(2)}) copy-start(bf16[16,128]{1,0:T(8,128)(2,1)} %vu_ref.1) | copy-start | bytes 12292
  74.6 12.5 %all-to-all-start.3 = ((bf16[8,192,128]{2,1,0:T(8,128)(2,1)}), bf16[8,192,128]{2,1,0:T(8,128)(2,1)S(1)}, u32[]{:S(2)}, u32[]{:S(2)}) async-start(bf16[8,192,128]{2,1,0:T(8,128)(2,1)} %get-tuple-element.67), calls=%async_computation.3 | async-start | bytes 786432 | tf_op jit(solution)/shard_map/all_to_all | solution.py:282
  79.4 7.7 %collective-permute-start.5 = (bf16[2,2,128,128]{3,2,1,0:T(8,128)(2,1)S(1)}, bf16[2,2,128,128]{3,2,1,0:T(8,128)(2,1)S(1)}, u32[]{:S(2)}, u32[]{:S(2)}) collective-permute-start(bf16[2,2,128,128]{3,2,1,0:T(8,128)(2,1)S(1)} %get-tuple-element.61), channel_id=1, source_target_pairs={{32,0},{40,8},{48,16},{56,24},{64,32},{72,40},{80,48},{88,56},{96,... | collective-permute-start | bytes 393224 | tf_op jit(solution)/shard_map/ppermute | solution.py:274
  100.2 26.2 %all-to-all-start.5 = ((bf16[8,5,16,128]{3,2,1,0:T(8,128)(2,1)}), bf16[8,5,16,128]{3,2,1,0:T(8,128)(2,1)S(1)}, u32[]{:S(2)}, u32[]{:S(2)}) async-start(bf16[8,5,16,128]{3,2,1,0:T(8,128)(2,1)} %shard_map.239), calls=%async_computation.5 | async-start | bytes 327680 | tf_op jit(solution)/shard_map/all_to_all | solution.py:278
  111.1 7.8 %collective-permute-start.6 = (bf16[2,128,128]{2,1,0:T(8,128)(2,1)S(1)}, bf16[2,128,128]{2,1,0:T(8,128)(2,1)S(1)}, u32[]{:S(2)}, u32[]{:S(2)}) collective-permute-start(bf16[2,128,128]{2,1,0:T(8,128)(2,1)S(1)} %get-tuple-element.62), channel_id=1, source_target_pairs={{32,0},{40,8},{48,16},{56,24},{64,32},{72,40},{80,48},{88,56},{96,... | collective-permute-start | bytes 196616 | tf_op jit(solution)/shard_map/ppermute | solution.py:274
  112.4 13.4 %collective-permute-start.7 = (bf16[2,128,128]{2,1,0:T(8,128)(2,1)S(1)}, bf16[2,128,128]{2,1,0:T(8,128)(2,1)S(1)}, u32[]{:S(2)}, u32[]{:S(2)}) collective-permute-start(bf16[2,128,128]{2,1,0:T(8,128)(2,1)S(1)} %get-tuple-element.63), channel_id=1, source_target_pairs={{96,0},{104,8},{112,16},{120,24},{128,32},{136,40},{144,48},{152,5... | collective-permute-start | bytes 196616 | tf_op jit(solution)/shard_map/ppermute | solution.py:274
  127.1 11.9 %all-to-all-start.6 = ((bf16[8,5,16,128]{3,2,1,0:T(8,128)(2,1)}), bf16[8,5,16,128]{3,2,1,0:T(8,128)(2,1)S(1)}, u32[]{:S(2)}, u32[]{:S(2)}) async-start(bf16[8,5,16,128]{3,2,1,0:T(8,128)(2,1)} %shard_map.240), calls=%async_computation.6 | async-start | bytes 327680 | tf_op jit(solution)/shard_map/all_to_all | solution.py:278

commit v5 on v4

--- a/solution.py
+++ b/solution.py
@@ -234,7 +234,7 @@
         out_ref[t // 5, t % 5] = tile
 
 
-def pass_kernel(part_ref, near_ref, one_ref, three_ref):
+def pass_kernel(part_ref, near_ref, three_ref, one_ref):
     one_ref[...] = (part_ref[1].astype(F32) + near_ref[0].astype(F32)).astype(BF16)
     three_ref[...] = (part_ref[3].astype(F32) + near_ref[1].astype(F32)).astype(BF16)
 
@@ -347,7 +347,7 @@
         down_kernel, packed, low_back, x, x_one, x_two, x_three, x_four, dout, parts, low, totals
     )
     sums = call(sum_spread_kernel, packed, exchange(sums, EIGHTS))
-    one_back, three_back = call(pass_kernel, (block, block), parts, near)
+    three_back, one_back = call(pass_kernel, (block, block), parts, near)
     three_back, one_back = shift(three_back, -12), shift(one_back, -4)
     sums = after(exchange(sums, STRIDED), three_back, one_back)
     sums = call(sum_spread_kernel, packed, sums)
@@ -355,7 +355,7 @@
     dk, dv = call(
         owner_kernel,
         (shaped((128, 128), BF16), shaped((128, 128), BF16)),
-        parts, one_back, three_back,
+        parts, three_back, one_back,
     )
     narrow, small = shaped((16, 640), F32), shaped((16, 128), F32)
     broad = shaped((16, 1024), F32)

time: 141 us -> 142 us (level)
    ppermute x10, waiting for transfers between devices: 22.3 us -> 19.9 us  [shift(): lax.ppermute(value, 'ctx', [(i, i + steps) for i in range(first, last)])]
    all_to_all x4, waiting for transfers between devices: 15.7 us -> 18.1 us  [exchange(): lax.all_to_all(value, 'ctx', 0, 0, tiled=True, axis_index_groups=groups)]
  transfers between devices with their start and end apart: 16 -> 16, of which waited for: 9 -> 8; matrix products, arithmetic and copies ran while one was open for 0% -> 0% of each run, Pallas kernels for 8% -> 8%
where the time goes in v5:
time: 142 us; the launch traced here: 141 us
  starting transfers between devices  73.3 us (52%)
  waiting for transfers between devices  38 us (27%)
  Pallas kernels  15.3 us (11%)
  blocking collectives  11.9 us (8%)
    ppermute x10, starting transfers between devices, shift(): lax.ppermute(value, 'ctx', [(i, i + steps) for i in range(first, last)])  38.3 us
    all_to_all x4, starting transfers between devices, exchange(): lax.all_to_all(value, 'ctx', 0, 0, tiled=True, axis_index_groups=groups)  25.4 us
    ppermute x10, waiting for transfers between devices, shift(): lax.ppermute(value, 'ctx', [(i, i + steps) for i in range(first, last)])  19.9 us
    all_to_all x4, waiting for transfers between devices, exchange(): lax.all_to_all(value, 'ctx', 0, 0, tiled=True, axis_index_groups=groups)  18.1 us
    pallas_call x12, Pallas kernels, call(): pl.pallas_call(body, out_shape=outs, scratch_shapes=list(scratch), compil...  15.3 us
    all_to_all x1, blocking collectives, exchange(): lax.all_to_all(value, 'ctx', 0, 0, tiled=True, axis_index_groups=groups)  11.9 us
    all_to_all x2, starting transfers between devices, exchange_head(): return lax.all_to_all(value, 'head', 0, 0, tiled=True)  9.64 us
  transfers between devices with their start and end apart: 16, of which 8 were waited for; matrix products, arithmetic and copies ran while one was open for 0% of the time, Pallas kernels for 8%

profile of v5, /device:TPU:2, one launch (start us, length us, event | category | flops | bytes accessed | tf_op | source)
XLA Modules:
  0.0 140.9 jit_solution(12412664001794401850)
XLA Ops:
  0.6 0.0 copy-start.1
  0.7 0.8 fusion
  1.5 0.0 copy-start
  1.5 4.0 %collective-permute-start = (bf16[2,128,128]{2,1,0:T(8,128)(2,1)S(1)}, bf16[2,128,128]{2,1,0:T(8,128)(2,1)S(1)}, u32[]{:S(2)}, u32[]{:S(2)}) collective-permute-start(bf16[2,128,128]{2,1,0:T(8,128)(2,1)S(1)} %get-tuple-element.80.pair_ref), channel_id=1, source_target_pairs={{0,32},{8,40},{16,48},{24,56},{32,64},{40,72},{48,80},{56,88},{64,... | collective-permute-start | bytes 196616 | tf_op jit(solution)/shard_map/ppermute | solution.py:274
  5.5 1.9 %collective-permute-done.one_ref = bf16[2,128,128]{2,1,0:T(8,128)(2,1)S(1)} collective-permute-done((bf16[2,128,128]{2,1,0:T(8,128)(2,1)S(1)}, bf16[2,128,128]{2,1,0:T(8,128)(2,1)S(1)}, u32[]{:S(2)}, u32[]{:S(2)}) %collective-permute-start) | collective-permute-done | bytes 65568 | tf_op jit(solution)/shard_map/ppermute | solution.py:274
  7.3 0.0 copy-start.6
  7.4 7.9 %collective-permute-start.2 = (bf16[2,2,128,128]{3,2,1,0:T(8,128)(2,1)S(1)}, bf16[2,2,128,128]{3,2,1,0:T(8,128)(2,1)S(1)}, u32[]{:S(2)}, u32[]{:S(2)}) collective-permute-start(bf16[2,2,128,128]{3,2,1,0:T(8,128)(2,1)S(1)} %pad_maximum_fusion), channel_id=1, source_target_pairs={{0,96},{8,104},{16,112},{24,120},{32,128},{40,136},{48,144},{56,15... | collective-permute-start | bytes 393224 | tf_op jit(solution)/shard_map/ppermute | solution.py:274
  15.3 0.0 copy-done.1
  15.3 0.0 copy-done
  15.3 0.0 copy-done.6
  15.3 0.0 copy-done.7
  15.3 0.0 copy-done.8
  15.3 0.0 copy-done.9
  15.3 1.0 shard_map.230
  16.3 4.8 %all-to-all-start = ((bf16[8,64,128]{2,1,0:T(8,128)(2,1)}), bf16[8,64,128]{2,1,0:T(8,128)(2,1)S(1)}, u32[]{:S(2)}, u32[]{:S(2)}) async-start(bf16[8,64,128]{2,1,0:T(8,128)(2,1)} %shard_map.230), calls=%async_computation | async-start | bytes 262144 | tf_op jit(solution)/shard_map/all_to_all | solution.py:282
  21.1 5.5 %collective-permute-start.1 = (bf16[2,128,128]{2,1,0:T(8,128)(2,1)S(1)}, bf16[2,128,128]{2,1,0:T(8,128)(2,1)S(1)}, u32[]{:S(2)}, u32[]{:S(2)}) collective-permute-start(bf16[2,128,128]{2,1,0:T(8,128)(2,1)S(1)} %collective-permute-done.one_ref), channel_id=1, source_target_pairs={{0,32},{8,40},{16,48},{24,56},{32,64},{40,72},{48,80},{56,88},{64,... | collective-permute-start | bytes 196616 | tf_op jit(solution)/shard_map/ppermute | solution.py:274
  26.6 1.9 %collective-permute-done.1.two_ref = bf16[2,128,128]{2,1,0:T(8,128)(2,1)S(1)} collective-permute-done((bf16[2,128,128]{2,1,0:T(8,128)(2,1)S(1)}, bf16[2,128,128]{2,1,0:T(8,128)(2,1)S(1)}, u32[]{:S(2)}, u32[]{:S(2)}) %collective-permute-start.1) | collective-permute-done | bytes 65568 | tf_op jit(solution)/shard_map/ppermute | solution.py:274
  28.5 0.0 all-to-all-done.low_ref
  28.5 0.0 collective-permute-done.2.back_ref
  28.5 1.1 shard_map.231
  29.6 4.6 %all-to-all-start.1 = ((bf16[4,4,2,128,128]{4,3,2,1,0:T(8,128)(2,1)}), bf16[4,4,2,128,128]{4,3,2,1,0:T(8,128)(2,1)S(1)}, u32[]{:S(2)}, u32[]{:S(2)}) async-start(bf16[4,4,2,128,128]{4,3,2,1,0:T(8,128)(2,1)} %get-tuple-element.51), calls=%async_computation.1 | async-start | bytes 2097152 | tf_op jit(solution)/shard_map/all_to_all | solution.py:278
  34.2 4.4 %collective-permute-start.4 = (bf16[672,128]{1,0:T(8,128)(2,1)}, bf16[672,128]{1,0:T(8,128)(2,1)S(1)}, u32[]{:S(2)}, u32[]{:S(2)}) collective-permute-start(bf16[672,128]{1,0:T(8,128)(2,1)} %get-tuple-element.57), channel_id=1, source_target_pairs={{0,64},{8,72},{16,80},{24,88},{32,96},{40,104},{48,112},{56,120},{... | collective-permute-start | bytes 516104 | tf_op jit(solution)/shard_map/ppermute | solution.py:274
  38.7 4.1 %collective-permute-start.3 = (bf16[672,128]{1,0:T(8,128)(2,1)}, bf16[672,128]{1,0:T(8,128)(2,1)S(1)}, u32[]{:S(2)}, u32[]{:S(2)}) collective-permute-start(bf16[672,128]{1,0:T(8,128)(2,1)} %get-tuple-element.57), channel_id=1, source_target_pairs={{0,32},{8,40},{16,48},{24,56},{32,64},{40,72},{48,80},{56,88},{64,... | collective-permute-start | bytes 516104 | tf_op jit(solution)/shard_map/ppermute | solution.py:274
  42.8 0.0 copy-start.12
  42.8 0.0 copy-done.2
  42.8 0.0 copy-done.3
  42.8 0.0 copy-done.4
  42.8 0.6 copy-done.12
  43.5 0.4 shard_map.232
  43.8 4.9 %all-to-all-done.1.kv_ref = bf16[4,4,2,128,128]{4,3,2,1,0:T(8,128)(2,1)S(1)} async-done(((bf16[4,4,2,128,128]{4,3,2,1,0:T(8,128)(2,1)}), bf16[4,4,2,128,128]{4,3,2,1,0:T(8,128)(2,1)S(1)}, u32[]{:S(2)}, u32[]{:S(2)}) %all-to-all-start.1) | async-done | bytes 1048608 | tf_op jit(solution)/shard_map/all_to_all | solution.py:278
  48.8 7.5 %shard_map.233 = (bf16[128,1024]{1,0:T(8,128)(2,1)S(1)}, bf16[128,1024]{1,0:T(8,128)(2,1)S(1)}, bf16[4,4,2,128,128]{4,3,2,1,0:T(8,128)(2,1)}) custom-call(bf16[1024,128]{1,0:T(8,128)(2,1)S(1)} %get-tuple-element.47.qs, bf16[128,1024]{1,0:T(8,128)(2,1)S(1)} %get-tuple-element.48.qt, bf16[1024,128]{1,0:T(8,128)(2,1)S(1)} %get-tuple-element.49.gs, ...), custom_call_target="tpu_custom_call" | custom-call | flops 3221225472 | bytes 1048576 | tf_op jit(solution)/shard_map/pallas_call | solution.py:40
  56.3 0.0 collective-permute-done.4.two_ref
  56.3 0.0 collective-permute-done.3.one_ref
  56.3 3.7 %all-to-all-start.2 = ((bf16[4,4,2,128,128]{4,3,2,1,0:T(8,128)(2,1)}), bf16[4,4,2,128,128]{4,3,2,1,0:T(8,128)(2,1)S(1)}, u32[]{:S(2)}, u32[]{:S(2)}) async-start(bf16[4,4,2,128,128]{4,3,2,1,0:T(8,128)(2,1)} %get-tuple-element.58), calls=%async_computation.2 | async-start | bytes 2097152 | tf_op jit(solution)/shard_map/all_to_all | solution.py:278
  60.0 4.1 %collective-permute-start.8 = (bf16[672,128]{1,0:T(8,128)(2,1)S(1)}, bf16[672,128]{1,0:T(8,128)(2,1)S(1)}, u32[]{:S(2)}, u32[]{:S(2)}) collective-permute-start(bf16[672,128]{1,0:T(8,128)(2,1)S(1)} %collective-permute-done.4.two_ref), channel_id=1, source_target_pairs={{0,64},{8,72},{16,80},{24,88},{32,96},{40,104},{48,112},{56,120},{... | collective-permute-start | bytes 516104 | tf_op jit(solution)/shard_map/ppermute | solution.py:274
  64.1 4.4 %collective-permute-start.9 = (bf16[672,128]{1,0:T(8,128)(2,1)S(1)}, bf16[672,128]{1,0:T(8,128)(2,1)S(1)}, u32[]{:S(2)}, u32[]{:S(2)}) collective-permute-start(bf16[672,128]{1,0:T(8,128)(2,1)S(1)} %collective-permute-done.4.two_ref), channel_id=1, source_target_pairs={{0,32},{8,40},{16,48},{24,56},{32,64},{40,72},{48,80},{56,88},{64,... | collective-permute-start | bytes 516104 | tf_op jit(solution)/shard_map/ppermute | solution.py:274
  68.5 0.0 copy-done.5
  68.5 0.0 copy-start.10
  68.6 0.0 copy-start.11
  68.6 1.0 shard_map.234
  69.6 4.0 %all-to-all-done.2.y_ref = bf16[4,4,2,128,128]{4,3,2,1,0:T(8,128)(2,1)S(1)} async-done(((bf16[4,4,2,128,128]{4,3,2,1,0:T(8,128)(2,1)}), bf16[4,4,2,128,128]{4,3,2,1,0:T(8,128)(2,1)S(1)}, u32[]{:S(2)}, u32[]{:S(2)}) %all-to-all-start.2) | async-done | bytes 1048608 | tf_op jit(solution)/shard_map/all_to_all | solution.py:278
  73.6 0.0 copy-done.10
  73.6 0.0 copy-done.11
  73.6 1.1 shard_map.235
  74.6 0.0 collective-permute-done.8.four_ref
  74.6 0.0 collective-permute-done.9.three_ref
  74.6 4.8 %all-to-all-start.3 = ((bf16[8,192,128]{2,1,0:T(8,128)(2,1)}), bf16[8,192,128]{2,1,0:T(8,128)(2,1)S(1)}, u32[]{:S(2)}, u32[]{:S(2)}) async-start(bf16[8,192,128]{2,1,0:T(8,128)(2,1)} %get-tuple-element.67), calls=%async_computation.3 | async-start | bytes 786432 | tf_op jit(solution)/shard_map/all_to_all | solution.py:282
  79.4 1.3 collective-permute-start.5
  80.7 6.4 %collective-permute-done.5.near_ref = bf16[2,2,128,128]{3,2,1,0:T(8,128)(2,1)S(1)} collective-permute-done((bf16[2,2,128,128]{3,2,1,0:T(8,128)(2,1)S(1)}, bf16[2,2,128,128]{3,2,1,0:T(8,128)(2,1)S(1)}, u32[]{:S(2)}, u32[]{:S(2)}) %collective-permute-start.5) | collective-permute-done | bytes 131104 | tf_op jit(solution)/shard_map/ppermute | solution.py:274
  87.2 0.0 all-to-all-done.3.low_ref
  87.2 0.4 shard_map.238
  87.6 11.9 %all_to_all.35.in_ref = bf16[8,5,16,128]{3,2,1,0:T(8,128)(2,1)S(1)} all-to-all(bf16[8,5,16,128]{3,2,1,0:T(8,128)(2,1)S(1)} %shard_map.238), channel_id=1, replica_groups={{0,8,16,24,32,40,48,56},{64,72,80,88,96,104,112,120},{128,136,144,152,1..., dimensions={0} | all-to-all | bytes 327680 | tf_op jit(solution)/shard_map/all_to_all | solution.py:278
  99.5 0.7 shard_map.239
  100.2 10.8 %all-to-all-start.5 = ((bf16[8,5,16,128]{3,2,1,0:T(8,128)(2,1)}), bf16[8,5,16,128]{3,2,1,0:T(8,128)(2,1)S(1)}, u32[]{:S(2)}, u32[]{:S(2)}) async-start(bf16[8,5,16,128]{3,2,1,0:T(8,128)(2,1)} %shard_map.239), calls=%async_computation.5 | async-start | bytes 327680 | tf_op jit(solution)/shard_map/all_to_all | solution.py:278
  111.1 1.3 collective-permute-start.6
  112.4 1.3 collective-permute-start.7
  113.7 9.7 %collective-permute-done.6.one_ref = bf16[2,128,128]{2,1,0:T(8,128)(2,1)S(1)} collective-permute-done((bf16[2,128,128]{2,1,0:T(8,128)(2,1)S(1)}, bf16[2,128,128]{2,1,0:T(8,128)(2,1)S(1)}, u32[]{:S(2)}, u32[]{:S(2)}) %collective-permute-start.6) | collective-permute-done | bytes 65568 | tf_op jit(solution)/shard_map/ppermute | solution.py:274
  123.3 0.0 collective-permute-done.7.three_ref
  123.3 3.0 %all-to-all-done.5.in_ref = bf16[8,5,16,128]{3,2,1,0:T(8,128)(2,1)S(1)} async-done(((bf16[8,5,16,128]{3,2,1,0:T(8,128)(2,1)}), bf16[8,5,16,128]{3,2,1,0:T(8,128)(2,1)S(1)}, u32[]{:S(2)}, u32[]{:S(2)}) %all-to-all-start.5) | async-done | bytes 163872 | tf_op jit(solution)/shard_map/all_to_all | solution.py:278
  126.4 0.7 shard_map.240
  127.1 6.3 %all-to-all-start.6 = ((bf16[8,5,16,128]{3,2,1,0:T(8,128)(2,1)}), bf16[8,5,16,128]{3,2,1,0:T(8,128)(2,1)S(1)}, u32[]{:S(2)}, u32[]{:S(2)}) async-start(bf16[8,5,16,128]{3,2,1,0:T(8,128)(2,1)} %shard_map.240), calls=%async_computation.6 | async-start | bytes 327680 | tf_op jit(solution)/shard_map/all_to_all | solution.py:278
  133.4 0.6 shard_map.237
  134.0 6.1 %all-to-all-done.6.in_ref = bf16[8,5,16,128]{3,2,1,0:T(8,128)(2,1)S(1)} async-done(((bf16[8,5,16,128]{3,2,1,0:T(8,128)(2,1)}), bf16[8,5,16,128]{3,2,1,0:T(8,128)(2,1)S(1)}, u32[]{:S(2)}, u32[]{:S(2)}) %all-to-all-start.6) | async-done | bytes 163872 | tf_op jit(solution)/shard_map/all_to_all | solution.py:278
  140.2 0.7 shard_map.241
  (9 shorter events, 0.1 us)
Async XLA Ops:
  0.6 14.6 %copy-start.1 = (bf16[128,640]{1,0:T(8,128)(2,1)S(1)}, bf16[128,640]{1,0:T(8,128)(2,1)}, u32[]{:S(2)}) copy-start(bf16[128,640]{1,0:T(8,128)(2,1)} %dout_ref.3) | copy-start | bytes 491524
  1.5 13.8 %copy-start = (bf16[128,640]{1,0:T(8,128)(2,1)S(1)}, bf16[128,640]{1,0:T(8,128)(2,1)}, u32[]{:S(2)}) copy-start(bf16[128,640]{1,0:T(8,128)(2,1)} %x_ref.5) | copy-start | bytes 491524
  1.5 5.8 %collective-permute-start = (bf16[2,128,128]{2,1,0:T(8,128)(2,1)S(1)}, bf16[2,128,128]{2,1,0:T(8,128)(2,1)S(1)}, u32[]{:S(2)}, u32[]{:S(2)}) collective-permute-start(bf16[2,128,128]{2,1,0:T(8,128)(2,1)S(1)} %get-tuple-element.80.pair_ref), channel_id=1, source_target_pairs={{0,32},{8,40},{16,48},{24,56},{32,64},{40,72},{48,80},{56,88},{64,... | collective-permute-start | bytes 196616 | tf_op jit(solution)/shard_map/ppermute | solution.py:274
  7.3 7.9 %copy-start.6 = (bf16[640,16]{0,1:T(8,128)(2,1)S(1)}, bf16[640,16]{0,1:T(8,128)(2,1)}, u32[]{:S(2)}) copy-start(bf16[640,16]{0,1:T(8,128)(2,1)} %param.22) | copy-start | bytes 61444
  7.3 7.9 %copy-start.7 = (bf16[640,16]{0,1:T(8,128)(2,1)S(1)}, bf16[640,16]{0,1:T(8,128)(2,1)}, u32[]{:S(2)}) copy-start(bf16[640,16]{0,1:T(8,128)(2,1)} %param.24) | copy-start | bytes 61444
  7.3 8.0 %copy-start.8 = (bf16[640,16]{0,1:T(8,128)(2,1)S(1)}, bf16[640,16]{0,1:T(8,128)(2,1)}, u32[]{:S(2)}) copy-start(bf16[640,16]{0,1:T(8,128)(2,1)} %param.26) | copy-start | bytes 61444
  7.3 8.0 %copy-start.9 = (bf16[16,640]{1,0:T(8,128)(2,1)S(1)}, bf16[16,640]{1,0:T(8,128)(2,1)}, u32[]{:S(2)}) copy-start(bf16[16,640]{1,0:T(8,128)(2,1)} %ou_ref.1) | copy-start | bytes 61444
  7.4 21.1 %collective-permute-start.2 = (bf16[2,2,128,128]{3,2,1,0:T(8,128)(2,1)S(1)}, bf16[2,2,128,128]{3,2,1,0:T(8,128)(2,1)S(1)}, u32[]{:S(2)}, u32[]{:S(2)}) collective-permute-start(bf16[2,2,128,128]{3,2,1,0:T(8,128)(2,1)S(1)} %pad_maximum_fusion), channel_id=1, source_target_pairs={{0,96},{8,104},{16,112},{24,120},{32,128},{40,136},{48,144},{56,15... | collective-permute-start | bytes 393224 | tf_op jit(solution)/shard_map/ppermute | solution.py:274
  16.3 12.2 %all-to-all-start = ((bf16[8,64,128]{2,1,0:T(8,128)(2,1)}), bf16[8,64,128]{2,1,0:T(8,128)(2,1)S(1)}, u32[]{:S(2)}, u32[]{:S(2)}) async-start(bf16[8,64,128]{2,1,0:T(8,128)(2,1)} %shard_map.230), calls=%async_computation | async-start | bytes 262144 | tf_op jit(solution)/shard_map/all_to_all | solution.py:282
  21.1 7.4 %collective-permute-start.1 = (bf16[2,128,128]{2,1,0:T(8,128)(2,1)S(1)}, bf16[2,128,128]{2,1,0:T(8,128)(2,1)S(1)}, u32[]{:S(2)}, u32[]{:S(2)}) collective-permute-start(bf16[2,128,128]{2,1,0:T(8,128)(2,1)S(1)} %collective-permute-done.one_ref), channel_id=1, source_target_pairs={{0,32},{8,40},{16,48},{24,56},{32,64},{40,72},{48,80},{56,88},{64,... | collective-permute-start | bytes 196616 | tf_op jit(solution)/shard_map/ppermute | solution.py:274
  29.6 13.2 %copy-start.2 = (bf16[128,1024]{1,0:T(8,128)(2,1)S(1)}, bf16[128,1024]{1,0:T(8,128)(2,1)}, u32[]{:S(2)}) copy-start(bf16[128,1024]{1,0:T(8,128)(2,1)} %q_ref.1) | copy-start | bytes 786436
  29.6 13.2 %copy-start.3 = (bf16[128,1024]{1,0:T(8,128)(2,1)S(1)}, bf16[128,1024]{1,0:T(8,128)(2,1)}, u32[]{:S(2)}) copy-start(bf16[128,1024]{1,0:T(8,128)(2,1)} %f_ref.1) | copy-start | bytes 786436
  29.6 13.2 %copy-start.4 = (bf16[1024,16]{0,1:T(8,128)(2,1)S(1)}, bf16[1024,16]{0,1:T(8,128)(2,1)}, u32[]{:S(2)}) copy-start(bf16[1024,16]{0,1:T(8,128)(2,1)} %param.28) | copy-start | bytes 98308
  29.6 19.1 %all-to-all-start.1 = ((bf16[4,4,2,128,128]{4,3,2,1,0:T(8,128)(2,1)}), bf16[4,4,2,128,128]{4,3,2,1,0:T(8,128)(2,1)S(1)}, u32[]{:S(2)}, u32[]{:S(2)}) async-start(bf16[4,4,2,128,128]{4,3,2,1,0:T(8,128)(2,1)} %get-tuple-element.51), calls=%async_computation.1 | async-start | bytes 2097152 | tf_op jit(solution)/shard_map/all_to_all | solution.py:278
  34.2 22.1 %collective-permute-start.4 = (bf16[672,128]{1,0:T(8,128)(2,1)}, bf16[672,128]{1,0:T(8,128)(2,1)S(1)}, u32[]{:S(2)}, u32[]{:S(2)}) collective-permute-start(bf16[672,128]{1,0:T(8,128)(2,1)} %get-tuple-element.57), channel_id=1, source_target_pairs={{0,64},{8,72},{16,80},{24,88},{32,96},{40,104},{48,112},{56,120},{... | collective-permute-start | bytes 516104 | tf_op jit(solution)/shard_map/ppermute | solution.py:274
  38.7 17.6 %collective-permute-start.3 = (bf16[672,128]{1,0:T(8,128)(2,1)}, bf16[672,128]{1,0:T(8,128)(2,1)S(1)}, u32[]{:S(2)}, u32[]{:S(2)}) collective-permute-start(bf16[672,128]{1,0:T(8,128)(2,1)} %get-tuple-element.57), channel_id=1, source_target_pairs={{0,32},{8,40},{16,48},{24,56},{32,64},{40,72},{48,80},{56,88},{64,... | collective-permute-start | bytes 516104 | tf_op jit(solution)/shard_map/ppermute | solution.py:274
  42.8 0.7 copy-start.12
  56.3 12.2 %copy-start.5 = (bf16[16,1024]{1,0:T(8,128)(2,1)S(1)}, bf16[16,1024]{1,0:T(8,128)(2,1)}, u32[]{:S(2)}) copy-start(bf16[16,1024]{1,0:T(8,128)(2,1)} %qu_ref.1) | copy-start | bytes 98308
  56.3 17.3 %all-to-all-start.2 = ((bf16[4,4,2,128,128]{4,3,2,1,0:T(8,128)(2,1)}), bf16[4,4,2,128,128]{4,3,2,1,0:T(8,128)(2,1)S(1)}, u32[]{:S(2)}, u32[]{:S(2)}) async-start(bf16[4,4,2,128,128]{4,3,2,1,0:T(8,128)(2,1)} %get-tuple-element.58), calls=%async_computation.2 | async-start | bytes 2097152 | tf_op jit(solution)/shard_map/all_to_all | solution.py:278
  60.0 14.7 %collective-permute-start.8 = (bf16[672,128]{1,0:T(8,128)(2,1)S(1)}, bf16[672,128]{1,0:T(8,128)(2,1)S(1)}, u32[]{:S(2)}, u32[]{:S(2)}) collective-permute-start(bf16[672,128]{1,0:T(8,128)(2,1)S(1)} %collective-permute-done.4.two_ref), channel_id=1, source_target_pairs={{0,64},{8,72},{16,80},{24,88},{32,96},{40,104},{48,112},{56,120},{... | collective-permute-start | bytes 516104 | tf_op jit(solution)/shard_map/ppermute | solution.py:274
  64.1 10.5 %collective-permute-start.9 = (bf16[672,128]{1,0:T(8,128)(2,1)S(1)}, bf16[672,128]{1,0:T(8,128)(2,1)S(1)}, u32[]{:S(2)}, u32[]{:S(2)}) collective-permute-start(bf16[672,128]{1,0:T(8,128)(2,1)S(1)} %collective-permute-done.4.two_ref), channel_id=1, source_target_pairs={{0,32},{8,40},{16,48},{24,56},{32,64},{40,72},{48,80},{56,88},{64,... | collective-permute-start | bytes 516104 | tf_op jit(solution)/shard_map/ppermute | solution.py:274
  68.5 5.0 %copy-start.10 = (bf16[16,128]{1,0:T(8,128)(2,1)S(1)}, bf16[16,128]{1,0:T(8,128)(2,1)}, u32[]{:S(2)}) copy-start(bf16[16,128]{1,0:T(8,128)(2,1)} %ku_ref.1) | copy-start | bytes 12292
  68.6 5.0 %copy-start.11 = (bf16[16,128]{1,0:T(8,128)(2,1)S(1)}, bf16[16,128]{1,0:T(8,128)(2,1)}, u32[]{:S(2)}) copy-start(bf16[16,128]{1,0:T(8,128)(2,1)} %vu_ref.1) | copy-start | bytes 12292
  74.6 12.5 %all-to-all-start.3 = ((bf16[8,192,128]{2,1,0:T(8,128)(2,1)}), bf16[8,192,128]{2,1,0:T(8,128)(2,1)S(1)}, u32[]{:S(2)}, u32[]{:S(2)}) async-start(bf16[8,192,128]{2,1,0:T(8,128)(2,1)} %get-tuple-element.67), calls=%async_computation.3 | async-start | bytes 786432 | tf_op jit(solution)/shard_map/all_to_all | solution.py:282
  79.4 7.7 %collective-permute-start.5 = (bf16[2,2,128,128]{3,2,1,0:T(8,128)(2,1)S(1)}, bf16[2,2,128,128]{3,2,1,0:T(8,128)(2,1)S(1)}, u32[]{:S(2)}, u32[]{:S(2)}) collective-permute-start(bf16[2,2,128,128]{3,2,1,0:T(8,128)(2,1)S(1)} %get-tuple-element.61), channel_id=1, source_target_pairs={{32,0},{40,8},{48,16},{56,24},{64,32},{72,40},{80,48},{88,56},{96,... | collective-permute-start | bytes 393224 | tf_op jit(solution)/shard_map/ppermute | solution.py:274
  100.2 26.2 %all-to-all-start.5 = ((bf16[8,5,16,128]{3,2,1,0:T(8,128)(2,1)}), bf16[8,5,16,128]{3,2,1,0:T(8,128)(2,1)S(1)}, u32[]{:S(2)}, u32[]{:S(2)}) async-start(bf16[8,5,16,128]{3,2,1,0:T(8,128)(2,1)} %shard_map.239), calls=%async_computation.5 | async-start | bytes 327680 | tf_op jit(solution)/shard_map/all_to_all | solution.py:278
  111.1 12.3 %collective-permute-start.6 = (bf16[2,128,128]{2,1,0:T(8,128)(2,1)S(1)}, bf16[2,128,128]{2,1,0:T(8,128)(2,1)S(1)}, u32[]{:S(2)}, u32[]{:S(2)}) collective-permute-start(bf16[2,128,128]{2,1,0:T(8,128)(2,1)S(1)} %get-tuple-element.62), channel_id=1, source_target_pairs={{96,0},{104,8},{112,16},{120,24},{128,32},{136,40},{144,48},{152,5... | collective-permute-start | bytes 196616 | tf_op jit(solution)/shard_map/ppermute | solution.py:274
  112.4 11.0 %collective-permute-start.7 = (bf16[2,128,128]{2,1,0:T(8,128)(2,1)S(1)}, bf16[2,128,128]{2,1,0:T(8,128)(2,1)S(1)}, u32[]{:S(2)}, u32[]{:S(2)}) collective-permute-start(bf16[2,128,128]{2,1,0:T(8,128)(2,1)S(1)} %get-tuple-element.63), channel_id=1, source_target_pairs={{32,0},{40,8},{48,16},{56,24},{64,32},{72,40},{80,48},{88,56},{96,... | collective-permute-start | bytes 196616 | tf_op jit(solution)/shard_map/ppermute | solution.py:274
  127.1 13.1 %all-to-all-start.6 = ((bf16[8,5,16,128]{3,2,1,0:T(8,128)(2,1)}), bf16[8,5,16,128]{3,2,1,0:T(8,128)(2,1)S(1)}, u32[]{:S(2)}, u32[]{:S(2)}) async-start(bf16[8,5,16,128]{3,2,1,0:T(8,128)(2,1)} %shard_map.240), calls=%async_computation.6 | async-start | bytes 327680 | tf_op jit(solution)/shard_map/all_to_all | solution.py:278
